TPU v7x, 128 devices: a whole 4x4x4 slice. The times are simulated.
128 devices in a mesh: leaf: 8 (over x, core), panel: 16 (over z, y).
Axes of the slice: x: 4, y: 4, z: 4, core: 2. Of those that a mesh axis runs over, the one named last changes fastest.
Arguments:
- potentials: float32 [131072, 384], P(('leaf', 'panel')), may hold values from -6 to 6
- leaf_to_panel: int32 [131072], P(('leaf', 'panel')), may hold values from 0 to 131071, as said below
- density: bfloat16 [131072, 384], P(('leaf', 'panel')), may hold values from -6 to 6
- corrections: bfloat16 [4096, 384, 384], P(('leaf', 'panel')), may hold values from -0.3125 to 0.3125
- correction_rows: int32 [4096], P(('leaf', 'panel')), may hold values from 0 to 131071, as said below
- correction_cols: int32 [4096], P(('leaf', 'panel')), may hold values from 0 to 131071, as said below
- block_count: int32 [128], P(('leaf', 'panel')), may hold values from 16 to 32, as said below
Outputs:
- velocity: float32 [131072, 384], P(('leaf', 'panel'))
Inputs may be any that keep to these rules, and one draw needn't show every extreme that they name: `leaf_to_panel`: device f holds leaf blocks f * 1024 to (f + 1) * 1024 - 1 and panel blocks likewise; the map is a bijection; at most 16 of one device's leaf blocks map to the panel blocks of any one device; exactly 16 map to its own, and exactly 16 to one other device. `correction_rows`: slot s of device f is entry f * 32 + s; its target lies among the panel blocks of devices f - 1, f and f + 1, cyclically. `correction_cols`: A slot's source block lies within 512 blocks of its target, cyclically, and among the panel blocks of devices f - 1, f and f + 1. `block_count`: some device has all 32 slots live.
All inputs are finite; a program needn't handle non-finite values.
Results may differ from a plain program's by a relative error of at most 0.0003.
Values may be sent and summed in bfloat16 or wider, within the bound.
No kernel may reach another device: no remote copies, remote signals or barrier semaphores. Data moves between devices by JAX's collectives and lax.ppermute only.
A program may use at most 64 MiB of HBM per device.

v0:
```python
import jax
import jax.numpy as jnp
from jax import lax
from jax.sharding import PartitionSpec as P


def extended_2(cells, sides, width):
    for axis, dim in sides:
        count = lax.axis_size(axis)
        head = lax.slice_in_dim(cells, 0, width, axis=dim)
        tail = lax.slice_in_dim(cells, cells.shape[dim] - width, cells.shape[dim], axis=dim)
        cells = jnp.concatenate(
            [
                lax.ppermute(tail, axis, [(i, (i + 1) % count) for i in range(count)]),
                cells,
                lax.ppermute(head, axis, [((i + 1) % count, i) for i in range(count)]),
            ],
            axis=dim,
        )
    return cells


def shifted(value, axis, steps):
    count = lax.axis_size(axis)
    pairs = [(source, (source + steps) % count) for source in range(count)]
    return lax.ppermute(value, axis, pairs)


def place_rows(values, labels, offset, blocks):
    index = labels - offset
    index = jnp.where((index >= 0) & (index < blocks), index, blocks)
    return jnp.zeros((blocks, values.shape[1]), jnp.float32).at[index].add(values, mode="drop")


def on_device(
    potentials, leaf_to_panel, density, corrections, correction_rows, correction_cols, block_count
):
    blocks, breadth = potentials.shape
    devices = lax.axis_size(("leaf", "panel"))
    own_index = lax.axis_index(("leaf", "panel"))
    capacity = max(2, 2 * blocks // devices)
    destination = leaf_to_panel // blocks
    target_slot = leaf_to_panel % blocks
    same_dest = destination[:, None] == destination[None, :]
    earlier = jnp.arange(blocks)[None, :] < jnp.arange(blocks)[:, None]
    rank_within = jnp.sum((same_dest & earlier).astype(jnp.int32), axis=1)
    position = destination * capacity + rank_within
    outgoing = jnp.zeros((devices * capacity, breadth), jnp.float32).at[position].set(potentials)
    labels = (
        jnp.zeros((devices * capacity,), jnp.float32)
        .at[position]
        .set((target_slot + 1).astype(jnp.float32))
    )
    arrived, arrived_labels = (
        lax.all_to_all(
            outgoing.reshape(devices, capacity, breadth),
            ("leaf", "panel"),
            split_axis=0,
            concat_axis=0,
            tiled=True,
        ),
        lax.all_to_all(
            labels.reshape(devices, capacity),
            ("leaf", "panel"),
            split_axis=0,
            concat_axis=0,
            tiled=True,
        ),
    )
    arrived = arrived.reshape(devices * capacity, breadth)
    slot_index = arrived_labels.reshape(devices * capacity).astype(jnp.int32) - 1
    far_field = place_rows(arrived, slot_index, 0, blocks)
    extended = extended_2(density, ((("leaf", "panel"), 0),), blocks)
    total = devices * blocks
    first_block = own_index * blocks - blocks
    col_local = (correction_cols - first_block) % total
    row_local = (correction_rows - first_block) % total
    slot_total = corrections.shape[0]
    fetched = jnp.take(extended, col_local, axis=0)
    live = jnp.arange(slot_total) < block_count[0]
    terms = jnp.einsum("kij,kj->ki", corrections, fetched, preferred_element_type=jnp.float32)
    terms = jnp.where(live[:, None], terms, jnp.zeros_like(terms))
    accum = jnp.zeros((3 * blocks, breadth), jnp.float32).at[row_local].add(terms)
    from_previous = shifted(accum[2 * blocks :], ("leaf", "panel"), 1)
    from_following = shifted(accum[:blocks], ("leaf", "panel"), -1)
    near_field = accum[blocks : 2 * blocks] + from_previous + from_following
    return far_field + near_field


def solution(mesh):
    in_specs = (
        P(("leaf", "panel"), None),
        P(("leaf", "panel")),
        P(("leaf", "panel"), None),
        P(("leaf", "panel"), None, None),
        P(("leaf", "panel")),
        P(("leaf", "panel")),
        P(("leaf", "panel")),
    )
    out_specs = P(("leaf", "panel"), None)
    return jax.shard_map(
        on_device, mesh=mesh, in_specs=in_specs, out_specs=out_specs, check_vma=False
    )
```

profile of v0, /device:TPU:1, one launch (start us, length us, event | category | flops | bytes accessed | tf_op | source)
XLA Modules:
  0.0 131.8 jit_solution(94487415600687752)
XLA Ops:
  0.0 2.1 %collective-permute-start = (bf16[1024,384]{1,0:T(8,128)(2,1)}, bf16[1024,384]{1,0:T(8,128)(2,1)}, u32[]{:S(2)}, u32[]{:S(2)}) collective-permute-start(bf16[1024,384]{1,0:T(8,128)(2,1)} %param.9), channel_id=1, source_target_pairs={{0,1},{1,2},{2,3},{3,4},{4,5},{5,6},{6,7},{7,8},{8,9},{9,10},{10,1... | collective-permute-start | bytes 2359304 | tf_op jit(solution)/shard_map/ppermute | solution.py:14
  2.1 5.5 %collective-permute-start.1 = (bf16[1024,384]{1,0:T(8,128)(2,1)}, bf16[1024,384]{1,0:T(8,128)(2,1)}, u32[]{:S(2)}, u32[]{:S(2)}) collective-permute-start(bf16[1024,384]{1,0:T(8,128)(2,1)} %param.9), channel_id=1, source_target_pairs={{1,0},{2,1},{3,2},{4,3},{5,4},{6,5},{7,6},{8,7},{9,8},{10,9},{11,1... | collective-permute-start | bytes 2359304 | tf_op jit(solution)/shard_map/ppermute | solution.py:16
  7.6 0.7 add_select_fusion.1
  8.3 0.5 convert_reduce_fusion
  8.8 0.7 fusion.12
  9.5 4.3 %scatter_custom_fusion.1 = f32[2048]{0:T(1024)S(1)} fusion(s32[1024]{0:T(1024)S(1)} %get-tuple-element.10, f32[1024]{0:T(1024)S(1)} %get-tuple-element.9, f32[]{:T(128)} %constant.75.clone.1), kind=kCustom, calls=%fused_computation.35 | custom fusion | bytes 8196 | tf_op jit(solution)/shard_map/scatter | solution.py:52
  13.8 0.7 all_to_all.9
  14.6 5.9 %all-to-all-start = ((f32[128,1,16]{2,1,0:T(1,128)}), f32[128,1,16]{2,1,0:T(1,128)S(1)}, u32[]{:S(2)}, u32[]{:S(2)}) async-start(f32[128,1,16]{2,1,0:T(1,128)} %bitcast.3), calls=%async_computation | async-start | bytes 131072 | tf_op jit(solution)/shard_map/all_to_all | solution.py:62
  21.1 0.7 compare_and_fusion
  21.8 0.7 compare_select_fusion.3
  22.5 7.2 %scatter_custom_fusion.2 = f32[2048,384]{1,0:T(8,128)} fusion(s32[1024]{0:T(1024)S(1)} %get-tuple-element.10, f32[1024,384]{1,0:T(8,128)} %param.7, f32[]{:T(128)} %constant.75.clone.1), kind=kCustom, calls=%fused_computation.13 | custom fusion | bytes 3146240 | tf_op jit(solution)/shard_map/scatter | solution.py:48
  29.7 0.5 all-to-all-done
  30.2 9.3 %all-to-all-start.1 = ((f32[128,16,384]{2,1,0:T(8,128)}), f32[128,16,384]{2,1,0:T(8,128)S(1)}, u32[]{:S(2)}, u32[]{:S(2)}) async-start(f32[128,16,384]{2,1,0:T(8,128)} %bitcast.13), calls=%async_computation.1 | async-start | bytes 6291456 | tf_op jit(solution)/shard_map/all_to_all | solution.py:55
  39.5 3.3 %pad_maximum_fusion = bf16[3072,384]{1,0:T(8,128)(2,1)} fusion(bf16[1024,384]{1,0:T(8,128)(2,1)} %collective-permute-done.1, bf16[1024,384]{1,0:T(8,128)(2,1)} %param.9, bf16[1024,384]{1,0:T(8,128)(2,1)} %collective-permute-done), kind=kLoop, calls=%fused_computation.8 | loop fusion | flops 7077888 | bytes 4718592 | tf_op jit(solution)/shard_map/concatenate | solution.py:12
  42.7 2.6 %gather_fusion = bf16[32,384]{1,0:T(8,128)(2,1)S(1)} fusion(bf16[3072,384]{1,0:T(8,128)(2,1)} %pad_maximum_fusion, s32[1024]{0:T(1024)S(1)} %pad_clamp_fusion), kind=kCustom, calls=%fused_computation | custom fusion | bytes 49280 | tf_op jit(solution)/shard_map/jit(_take)/gather | solution.py:79
  45.4 6.5 %fusion.7 = f32[32,1,384]{2,1,0:T(1,128)S(1)} fusion(bf16[32,384,384]{2,1,0:T(8,128)(2,1)} %param.10, bf16[32,384,1]{1,0,2:T(8,128)(2,1)S(1)} %select_bitcast_fusion), kind=kOutput, calls=%fused_computation.18 | convolution fusion | flops 9437184 | bytes 9510912 | tf_op jit(solution)/shard_map/kij,kj->ki/dot_general | solution.py:81
  51.9 3.2 %scatter_custom_fusion = f32[3072,384]{1,0:T(8,128)} fusion(s32[32]{0:T(128)S(1)} %compare_select_fusion.3, f32[]{:T(128)} %constant.75.clone.1, f32[32,1,384]{2,1,0:T(1,128)S(1)} %fusion.7, pred[32]{0:T(512)(128)(4,1)S(1)} %iota_compare_fusion.1), kind=kCustom, calls=%fused_computation.9 | custom fusion | flops 24576 | bytes 4769280 | tf_op jit(solution)/shard_map/scatter-add | solution.py:83
  55.1 3.7 %fusion.19 = (f32[1024,384]{1,0:T(8,128)}, f32[1024,384]{1,0:T(8,128)}) fusion(f32[3072,384]{1,0:T(8,128)} %scatter_custom_fusion), kind=kLoop, calls=%fused_computation.51 | loop fusion | bytes 6291456 | tf_op jit(solution)/shard_map/slice | solution.py:84
  58.9 1.4 %collective-permute-start.2 = (f32[1024,384]{1,0:T(8,128)}, f32[1024,384]{1,0:T(8,128)}, u32[]{:S(2)}, u32[]{:S(2)}) collective-permute-start(f32[1024,384]{1,0:T(8,128)} %get-tuple-element.7), channel_id=1, source_target_pairs={{0,1},{1,2},{2,3},{3,4},{4,5},{5,6},{6,7},{7,8},{8,9},{9,10},{10,1... | collective-permute-start | bytes 4718600 | tf_op jit(solution)/shard_map/ppermute | solution.py:26
  60.3 4.4 %collective-permute-start.3 = (f32[1024,384]{1,0:T(8,128)}, f32[1024,384]{1,0:T(8,128)}, u32[]{:S(2)}, u32[]{:S(2)}) collective-permute-start(f32[1024,384]{1,0:T(8,128)} %get-tuple-element.8), channel_id=1, source_target_pairs={{0,127},{1,0},{2,1},{3,2},{4,3},{5,4},{6,5},{7,6},{8,7},{9,8},{10,... | collective-permute-start | bytes 4718600 | tf_op jit(solution)/shard_map/ppermute | solution.py:26
  64.7 0.2 add_reduce_fusion
  65.0 47.9 %collective-permute-done.2 = f32[1024,384]{1,0:T(8,128)} collective-permute-done((f32[1024,384]{1,0:T(8,128)}, f32[1024,384]{1,0:T(8,128)}, u32[]{:S(2)}, u32[]{:S(2)}) %collective-permute-start.2) | collective-permute-done | bytes 1572896 | tf_op jit(solution)/shard_map/ppermute | solution.py:26
  112.9 3.7 %fusion.3 = f32[1024,384]{1,0:T(8,128)} fusion(f32[1024,384]{1,0:T(8,128)} %collective-permute-done.3, f32[1024,384]{1,0:T(8,128)} %collective-permute-done.2, f32[3072,384]{1,0:T(8,128)} %scatter_custom_fusion), kind=kLoop, calls=%fused_computation.12 | loop fusion | flops 786432 | bytes 6291456 | tf_op jit(solution)/shard_map/add | solution.py:86
  116.6 15.2 %scatter_fusion = f32[1024,384]{1,0:T(8,128)} fusion(f32[1024,384]{1,0:T(8,128)} %fusion.3, s32[2048]{0:T(1024)S(1)} %bitcast.14, f32[2048,384]{1,0:T(8,128)S(1)} %bitcast.12), kind=kCustom, calls=%fused_computation.4 | custom fusion | flops 786432 | bytes 9445376 | tf_op jit(solution)/shard_map/scatter-add | solution.py:32
  (9 shorter events, 0.2 us)
Async XLA Ops:
  0.0 39.5 %collective-permute-start = (bf16[1024,384]{1,0:T(8,128)(2,1)}, bf16[1024,384]{1,0:T(8,128)(2,1)}, u32[]{:S(2)}, u32[]{:S(2)}) collective-permute-start(bf16[1024,384]{1,0:T(8,128)(2,1)} %param.9), channel_id=1, source_target_pairs={{0,1},{1,2},{2,3},{3,4},{4,5},{5,6},{6,7},{7,8},{8,9},{9,10},{10,1... | collective-permute-start | bytes 2359304 | tf_op jit(solution)/shard_map/ppermute | solution.py:14
  2.1 37.4 %collective-permute-start.1 = (bf16[1024,384]{1,0:T(8,128)(2,1)}, bf16[1024,384]{1,0:T(8,128)(2,1)}, u32[]{:S(2)}, u32[]{:S(2)}) collective-permute-start(bf16[1024,384]{1,0:T(8,128)(2,1)} %param.9), channel_id=1, source_target_pairs={{1,0},{2,1},{3,2},{4,3},{5,4},{6,5},{7,6},{8,7},{9,8},{10,9},{11,1... | collective-permute-start | bytes 2359304 | tf_op jit(solution)/shard_map/ppermute | solution.py:16
  14.6 15.6 %all-to-all-start = ((f32[128,1,16]{2,1,0:T(1,128)}), f32[128,1,16]{2,1,0:T(1,128)S(1)}, u32[]{:S(2)}, u32[]{:S(2)}) async-start(f32[128,1,16]{2,1,0:T(1,128)} %bitcast.3), calls=%async_computation | async-start | bytes 131072 | tf_op jit(solution)/shard_map/all_to_all | solution.py:62
  30.2 86.4 %all-to-all-start.1 = ((f32[128,16,384]{2,1,0:T(8,128)}), f32[128,16,384]{2,1,0:T(8,128)S(1)}, u32[]{:S(2)}, u32[]{:S(2)}) async-start(f32[128,16,384]{2,1,0:T(8,128)} %bitcast.13), calls=%async_computation.1 | async-start | bytes 6291456 | tf_op jit(solution)/shard_map/all_to_all | solution.py:55
  58.9 54.0 %collective-permute-start.2 = (f32[1024,384]{1,0:T(8,128)}, f32[1024,384]{1,0:T(8,128)}, u32[]{:S(2)}, u32[]{:S(2)}) collective-permute-start(f32[1024,384]{1,0:T(8,128)} %get-tuple-element.7), channel_id=1, source_target_pairs={{0,1},{1,2},{2,3},{3,4},{4,5},{5,6},{6,7},{7,8},{8,9},{9,10},{10,1... | collective-permute-start | bytes 4718600 | tf_op jit(solution)/shard_map/ppermute | solution.py:26
  60.3 52.7 %collective-permute-start.3 = (f32[1024,384]{1,0:T(8,128)}, f32[1024,384]{1,0:T(8,128)}, u32[]{:S(2)}, u32[]{:S(2)}) collective-permute-start(f32[1024,384]{1,0:T(8,128)} %get-tuple-element.8), channel_id=1, source_target_pairs={{0,127},{1,0},{2,1},{3,2},{4,3},{5,4},{6,5},{7,6},{8,7},{9,8},{10,... | collective-permute-start | bytes 4718600 | tf_op jit(solution)/shard_map/ppermute | solution.py:26
where the time goes:
time: 132 us
  waiting for transfers between devices  48.4 us (37%)
  other arithmetic  29 us (22%)
  starting transfers between devices  28.6 us (22%)
  local copies, waits for them, and re-layouts  18.6 us (14%)
  matrix products  6.47 us (5%)
    ppermute x2, waiting for transfers between devices, shifted(): return lax.ppermute(value, axis, pairs)  47.9 us
    scatter-add x1, other arithmetic, place_rows(): jnp.zeros((blocks, values.shape[1]), jnp.float32).at[index]  15.2 us
    all_to_all x1, starting transfers between devices, on_device(): lax.all_to_all(outgoing.reshape(devices, capacity, breadth), ('leaf', 'pa...  9.27 us
    scatter x1, local copies, waits for them, and re-layouts, on_device(): jnp.zeros((devices * capacity, breadth), jnp.float32).at[position]  7.19 us
    dot_general x1, matrix products, on_device(): jnp.einsum('kij,kj->ki', corrections, fetched, preferred_element_type=jnp...  6.47 us
    all_to_all x1, starting transfers between devices, on_device(): lax.all_to_all(labels.reshape(devices, capacity), ('leaf', 'panel'), spli...  5.92 us
    ppermute x2, starting transfers between devices, shifted(): return lax.ppermute(value, axis, pairs)  5.82 us
    ppermute x1, starting transfers between devices, extended_2(): lax.ppermute(head, axis, [((i + 1) % count, i) for i in range(count)])  5.47 us
  transfers between devices with their start and end apart: 6, of which 2 were waited for; matrix products, arithmetic and copies ran while one was open for 29% of the time, Pallas kernels for 0%

commit v1 on v0

v1 whole, which is shorter than its diff:
```python
import functools

import jax
import jax.numpy as jnp
from jax import lax
from jax.experimental import pallas as pl
from jax.experimental.pallas import tpu as pltpu
from jax.sharding import PartitionSpec as P

AXES = ("leaf", "panel")
DEV = 128
CAP = 16
ROWS = 1024
BW = 384
TILES = BW // 128
LINES = CAP // 2 * TILES + 1
SLOTS = 32
TOTAL = DEV * ROWS
F32, BF16, I32 = jnp.float32, jnp.bfloat16, jnp.int32
NT = (((1,), (1,)), ((), ()))
VMEM = pl.BlockSpec(memory_space=pltpu.VMEM)
SMEM = pl.BlockSpec(memory_space=pltpu.SMEM)


def iota(shape, dim):
    return lax.broadcasted_iota(I32, shape, dim)


def one_hot(mask):
    return jnp.where(mask, 1.0, 0.0).astype(BF16)


def row16(row):
    return jnp.broadcast_to(row, (16, 128)).astype(BF16)[None]


def times_row(block, row):
    return (block.reshape(8, 16, 128) * row16(row)).reshape(128, 128)


def mm(a, b):
    return jnp.dot(a, b, preferred_element_type=F32)


def pack_kernel(map_ref, pot_ref, out_ref, sel, dig, head):
    for g in range(8):
        rows = pl.ds(g * 128, 128)
        x = pot_ref[rows, :]
        top = jnp.max(jnp.abs(x), axis=1, keepdims=True)
        step = jnp.maximum(top * (1.0 / 32766.0), 2.0**-100)
        expo = jnp.floor(jnp.log2(step) + 1e-3)
        power = jnp.exp2(expo).astype(BF16).astype(F32)
        mant = jnp.maximum(jnp.ceil((step / power - 1.0) * 64.0), 0.0)
        scale = power * (1.0 + mant * (1.0 / 64.0))
        q = jnp.clip(jnp.round(x * (1.0 / scale)), -32767.0, 32767.0)
        hi = jnp.floor(q * (1.0 / 256.0))
        lo = q - hi * 256.0
        for n in range(TILES):
            dig[rows, pl.ds(n * 256, 128)] = hi[:, n * 128 : n * 128 + 128].astype(BF16)
            dig[rows, pl.ds(n * 256 + 128, 128)] = lo[:, n * 128 : n * 128 + 128].astype(BF16)
        lane = iota((128, 128), 1)
        head[rows, :] = jnp.where(lane == 0, expo + 128.0, jnp.where(lane == 1, mant, 0.0)).astype(BF16)
    eye = one_hot(iota((16, 128), 0) == iota((16, 128), 1))
    codes = lax.dot_general(eye, head[...], NT, preferred_element_type=F32)

    place = map_ref[...]
    dest, label = place >> 10, (place & (ROWS - 1)) + 1
    sub = iota((128, 128), 0)
    before = jnp.concatenate([one_hot(sub < iota((128, 128), 1)), one_hot(sub >= 0)], axis=1)
    hits = [dest[b : b + 1, :] == sub for b in range(8)]
    hot = [one_hot(h) for h in hits]
    counts = mm(jnp.concatenate(hot, axis=0), before)
    carry = jnp.zeros((128, 128), F32)
    ranks = []
    for b in range(8):
        part = counts[b * 128 : b * 128 + 128]
        ranks.append(jnp.sum(jnp.where(hits[b], part[:, :128] + carry, 0.0), axis=0, keepdims=True))
        carry = carry + part[:, 128:]

    low = iota((128, 128), 0) & (CAP - 1)
    digits = [[], [], [], []]
    ranked = []
    for b in range(8):
        lanes = pl.ds(b * 128, 128)
        for c in range(CAP):
            at = (c % 8) * 256 + (c // 8) * 128
            sel[pl.ds(at, 128), lanes] = times_row(hot[b], jnp.where(ranks[b] == c, 1.0, 0.0))
        lab = label[b : b + 1, :]
        cols = slice(b * 128, b * 128 + 128)
        for k, row in enumerate(
            ((lab >> 7).astype(F32), (lab & 127).astype(F32), codes[0:1, cols], codes[1:2, cols])
        ):
            digits[k].append(times_row(hot[b], row))
        ranked.append(one_hot(ranks[b].astype(I32) == low))
    left = jnp.concatenate([jnp.concatenate(d, axis=1) for d in digits], axis=0)
    meta = lax.dot_general(left, jnp.concatenate(ranked, axis=1), NT, preferred_element_type=F32).astype(I32)
    words = jnp.where(
        iota((128, 128), 1) < CAP, meta[0:128] * 128 + meta[128:256], meta[256:384] * 128 + meta[384:512]
    )
    out_ref[pl.ds(LINES - 1, DEV, stride=LINES), :] = words

    for n in range(TILES):
        for r in range(8):
            both = mm(sel[pl.ds(r * 256, 256), :], dig[:, pl.ds(n * 256, 256)])
            q = (both[:, :128] * 256.0 + both[:, 128:]).astype(I32)
            out_ref[pl.ds(n * 8 + r, DEV, stride=LINES), :] = (q[128:] << 16) | (q[:128] & 0xFFFF)


def pack(leaf_to_panel, potentials):
    return pl.pallas_call(
        pack_kernel,
        out_shape=jax.ShapeDtypeStruct((DEV * LINES, 128), I32),
        in_specs=[VMEM, VMEM],
        out_specs=VMEM,
        scratch_shapes=[
            pltpu.VMEM((DEV * CAP, ROWS), BF16),
            pltpu.VMEM((ROWS, 2 * BW), BF16),
            pltpu.VMEM((ROWS, 128), BF16),
        ],
        compiler_params=pltpu.CompilerParams(vmem_limit_bytes=40 * 2**20),
        cost_estimate=pl.CostEstimate(flops=2 * DEV * CAP * ROWS * 2 * BW, bytes_accessed=4 * 2**20, transcendentals=0),
        name="pack_rows",
    )(leaf_to_panel.reshape(8, 128), potentials)


def place_kernel(me_ref, msg_ref, own_ref, prev_ref, next_ref, asks_ref, ask_prev_ref, ask_next_ref, out_ref, sel, dig):
    heads = jnp.transpose(msg_ref[pl.ds(LINES - 1, DEV, stride=LINES), :].astype(F32)).astype(I32)
    target = heads[0:CAP] - 1
    code = heads[CAP : 2 * CAP]
    high, low = target >> 7, target & 127
    scale = jnp.exp2((code >> 7).astype(F32) - 128.0).astype(BF16).astype(F32)
    scale = scale * (1.0 + (code & 127).astype(F32) * (1.0 / 64.0))
    sub = iota((128, 128), 0)
    for c in range(CAP):
        hot = one_hot(low[c : c + 1] == sub)
        for g in range(8):
            row = jnp.where(high[c : c + 1] == g, scale[c : c + 1], 0.0)
            sel[pl.ds(g * 128, 128), pl.ds(c * 128, 128)] = times_row(hot, row)
    lane = iota((1, 128), 1)
    base = me_ref[0] * ROWS
    rows = jnp.where(
        lane < SLOTS,
        asks_ref[SLOTS : SLOTS + 1, :],
        jnp.where(lane < 2 * SLOTS, ask_prev_ref[SLOTS : SLOTS + 1, :], ask_next_ref[SLOTS : SLOTS + 1, :]),
    )
    target = jnp.where((rows < 0) | (lane >= 3 * SLOTS), -1, (rows - base) & (TOTAL - 1))
    for g in range(8):
        hot = one_hot(target - g * 128 == sub)
        sel[pl.ds(g * 128, 128), pl.ds(CAP * 128, 128)] = hot
        sel[pl.ds(g * 128, 128), pl.ds(CAP * 128 + 128, 128)] = hot
    near = jnp.concatenate([own_ref[...], prev_ref[...], next_ref[...], jnp.zeros((SLOTS, BW), F32)], axis=0)
    first = near.astype(BF16)
    second = (near - first.astype(F32)).astype(BF16)
    blank = jnp.zeros((256, 128), BF16)
    for n in range(TILES):
        for r in range(8):
            w = msg_ref[pl.ds(n * 8 + r, DEV, stride=LINES), :]
            for c, hi, lo in ((r, (w << 16) >> 24, w & 255), (r + 8, w >> 24, (w >> 16) & 255)):
                dig[pl.ds(c * 128, 128), pl.ds(n * 256, 128)] = hi.astype(F32).astype(BF16)
                dig[pl.ds(c * 128, 128), pl.ds(n * 256 + 128, 128)] = lo.astype(F32).astype(BF16)
        dig[pl.ds(CAP * 128, 256), pl.ds(n * 256, 128)] = blank
        dig[pl.ds(CAP * 128, 128), pl.ds(n * 256 + 128, 128)] = first[:, n * 128 : n * 128 + 128]
        dig[pl.ds(CAP * 128 + 128, 128), pl.ds(n * 256 + 128, 128)] = second[:, n * 128 : n * 128 + 128]
        for g in range(4):
            both = mm(sel[pl.ds(g * 256, 256), :], dig[:, pl.ds(n * 256, 256)])
            out_ref[pl.ds(g * 256, 256), pl.ds(n * 128, 128)] = both[:, :128] * 256.0 + both[:, 128:]


def place(me, arrived, terms, asks):
    return pl.pallas_call(
        place_kernel,
        out_shape=jax.ShapeDtypeStruct((ROWS, BW), F32),
        in_specs=[SMEM] + [VMEM] * 7,
        out_specs=VMEM,
        scratch_shapes=[
            pltpu.VMEM((ROWS, CAP * 128 + 256), BF16),
            pltpu.VMEM((CAP * 128 + 256, 2 * BW), BF16),
        ],
        compiler_params=pltpu.CompilerParams(vmem_limit_bytes=40 * 2**20),
        cost_estimate=pl.CostEstimate(flops=2 * DEV * CAP * ROWS * 2 * BW, bytes_accessed=4 * 2**20, transcendentals=0),
        name="place_rows",
    )(me, arrived, *terms, *asks)


def fetch_kernel(me_ref, asks_ref, ask_prev_ref, ask_next_ref, density_ref, own_ref, prev_ref, next_ref):
    base = me_ref[0] * ROWS
    asked = jnp.concatenate([asks_ref[0:SLOTS, :], ask_prev_ref[0:SLOTS, :], ask_next_ref[0:SLOTS, :]], axis=0)
    at = (asked - base) & (TOTAL - 1)
    lane = iota((3 * SLOTS, 128), 1)
    hot = jnp.concatenate([one_hot(at - b * 128 == lane) for b in range(8)], axis=1)
    got = mm(hot, density_ref[...]).astype(BF16)
    own_ref[...] = got[0:SLOTS]
    prev_ref[...] = got[SLOTS : 2 * SLOTS]
    next_ref[...] = got[2 * SLOTS :]


def fetch(me, asks, density):
    rows = jax.ShapeDtypeStruct((SLOTS, BW), BF16)
    return pl.pallas_call(
        fetch_kernel,
        out_shape=(rows, rows, rows),
        in_specs=[SMEM] + [VMEM] * 4,
        out_specs=(VMEM, VMEM, VMEM),
        cost_estimate=pl.CostEstimate(flops=10**8, bytes_accessed=2**20, transcendentals=0),
        name="fetch_density",
    )(me, *asks, density)


STEP = 4


def term_kernel(count_ref, mats_ref, own_ref, prev_ref, next_ref, out_ref, acc):
    step = pl.program_id(0)

    @pl.when(step == 0)
    def _():
        acc[...] = jnp.zeros_like(acc)

    rows = (own_ref[...].astype(F32) + prev_ref[...].astype(F32) + next_ref[...].astype(F32)).astype(BF16)
    vecs = jnp.concatenate([rows, jnp.zeros((128 - SLOTS, BW), BF16)], axis=0)
    lane = iota((BW, 128), 1)
    total = acc[...]
    for k in range(STEP):
        prod = lax.dot_general(mats_ref[k], vecs, NT, preferred_element_type=F32)
        total = jnp.where(lane == step * STEP + k, prod, total)
    acc[...] = total

    @pl.when(step == SLOTS // STEP - 1)
    def _():
        live = iota((SLOTS, BW), 0) < count_ref[0]
        out_ref[...] = jnp.where(live, jnp.transpose(acc[...])[0:SLOTS], 0.0)


def make_terms(count, mats, rows):
    whole = pl.BlockSpec((SLOTS, BW), lambda i: (0, 0))
    return pl.pallas_call(
        term_kernel,
        grid=(SLOTS // STEP,),
        out_shape=jax.ShapeDtypeStruct((SLOTS, BW), F32),
        in_specs=[SMEM, pl.BlockSpec((STEP, BW, BW), lambda i: (i, 0, 0)), whole, whole, whole],
        out_specs=whole,
        scratch_shapes=[pltpu.VMEM((BW, 128), F32)],
        compiler_params=pltpu.CompilerParams(vmem_limit_bytes=20 * 2**20),
        cost_estimate=pl.CostEstimate(flops=2 * SLOTS * BW * BW * 128, bytes_accessed=SLOTS * BW * BW * 2, transcendentals=0),
        name="near_terms",
    )(count, mats, *rows)


def shift(value, steps):
    return lax.ppermute(value, AXES, [(i, (i + steps) % DEV) for i in range(DEV)])


def on_device(potentials, leaf_to_panel, density, corrections, correction_rows, correction_cols, block_count):
    me = lax.axis_index(AXES).astype(I32).reshape(1)
    live = jnp.arange(SLOTS) < block_count[0]
    ask = jnp.concatenate(
        [
            jnp.broadcast_to(correction_cols[:, None], (SLOTS, 128)),
            jnp.broadcast_to(jnp.tile(jnp.where(live, correction_rows, -1), 4)[None], (8, 128)),
        ],
        axis=0,
    )
    asks = (ask, shift(ask, 1), shift(ask, -1))
    message = pack(leaf_to_panel, potentials)
    arrived = lax.all_to_all(
        message.reshape(DEV, LINES, 1, 128), AXES, split_axis=0, concat_axis=0, tiled=True
    ).reshape(DEV * LINES, 128)
    own, for_prev, for_next = fetch(me, asks, density)
    rows = (own, shift(for_next, 1), shift(for_prev, -1))
    term = make_terms(block_count, corrections, rows)
    terms = (term, shift(term, 1), shift(term, -1))
    return place(me, arrived, terms, asks)


def solution(mesh):
    rows = P(AXES, None)
    flat = P(AXES)
    return jax.shard_map(
        on_device,
        mesh=mesh,
        in_specs=(rows, flat, rows, P(AXES, None, None), flat, flat, flat),
        out_specs=rows,
        check_vma=False,
    )
```

time: 132 us -> 79.5 us (0.60)
  the two profiles are of different devices: /device:TPU:1 before, /device:TPU:0 now
where the time goes in v1:
time: 79.5 us; the launch traced here: 79.1 us
  starting transfers between devices  33 us (42%)
  waiting for transfers between devices  20.7 us (26%)
  Pallas kernels  17.3 us (22%)
  local copies, waits for them, and re-layouts  7.23 us (9%)
    ppermute x6, starting transfers between devices, shift(): lax.ppermute(value, AXES, [(i, (i + steps) % DEV) for i in range(DEV)])  21.9 us
    ppermute x6, waiting for transfers between devices, shift(): lax.ppermute(value, AXES, [(i, (i + steps) % DEV) for i in range(DEV)])  20.7 us
    all_to_all x1, starting transfers between devices, on_device(): lax.all_to_all(message.reshape(DEV, LINES, 1, 128), AXES, split_axis=0, c...  11.1 us
    unnamed x24, local copies, waits for them, and re-layouts  7.14 us
    pallas_call x1, Pallas kernels, pack(): pl.pallas_call(pack_kernel, out_shape=jax.ShapeDtypeStruct((DEV * LINES,...  6.08 us
    pallas_call x1, Pallas kernels, place(): pl.pallas_call(place_kernel, out_shape=jax.ShapeDtypeStruct((ROWS, BW), F...  5.36 us
    pallas_call x1, Pallas kernels, make_terms(): pl.pallas_call(term_kernel, grid=(SLOTS // STEP,), out_shape=jax.ShapeDty...  3.81 us
    pallas_call x1, Pallas kernels, fetch(): pl.pallas_call(fetch_kernel, out_shape=(rows, rows, rows), in_specs=[SMEM...  2.08 us
  transfers between devices with their start and end apart: 7, of which 4 were waited for; matrix products, arithmetic and copies ran while one was open for 0% of the time, Pallas kernels for 7%

profile of v1, /device:TPU:0, one launch (start us, length us, event | category | flops | bytes accessed | tf_op | source)
XLA Modules:
  0.0 79.1 jit_solution(2494613348937374298)
XLA Ops:
  0.0 1.4 %copy-done.8 = f32[1024,384]{1,0:T(8,128)S(1)} copy-done((f32[1024,384]{1,0:T(8,128)S(1)}, f32[1024,384]{1,0:T(8,128)}, u32[]{:S(2)}) %copy-start.8) | copy-done | bytes 1572888
  1.4 0.7 copy-done.9
  2.1 6.1 %pack_rows.1 = s32[3200,128]{1,0:T(8,128)} custom-call(s32[8,128]{1,0:T(8,128)S(1)} %bitcast.7, f32[1024,384]{1,0:T(8,128)S(1)} %copy-done.8), custom_call_target="tpu_custom_call" | custom-call | flops 3221225472 | bytes 4194304 | tf_op jit(solution)/shard_map/pack_rows/pallas_call | solution.py:110
  8.2 11.1 %all-to-all-start = ((s32[128,25,1,128]{3,2,1,0:T(1,128)}), s32[128,25,1,128]{3,2,1,0:T(1,128)S(1)}, u32[]{:S(2)}, u32[]{:S(2)}) async-start(s32[128,25,1,128]{3,2,1,0:T(1,128)} %bitcast.2), calls=%async_computation | async-start | bytes 3276800 | tf_op jit(solution)/shard_map/all_to_all | solution.py:265
  20.0 0.1 broadcast_in_dim.19
  20.1 0.1 pad_add_fusion.asks_ref
  20.2 1.0 %collective-permute-start = (s32[40,128]{1,0:T(8,128)S(1)}, s32[40,128]{1,0:T(8,128)S(1)}, u32[]{:S(2)}, u32[]{:S(2)}) collective-permute-start(s32[40,128]{1,0:T(8,128)S(1)} %pad_add_fusion.asks_ref), channel_id=1, source_target_pairs={{0,1},{1,2},{2,3},{3,4},{4,5},{5,6},{6,7},{7,8},{8,9},{9,10},{10,1... | collective-permute-start | bytes 61448 | tf_op jit(solution)/shard_map/ppermute | solution.py:250
  21.2 6.2 %collective-permute-start.1 = (s32[40,128]{1,0:T(8,128)S(1)}, s32[40,128]{1,0:T(8,128)S(1)}, u32[]{:S(2)}, u32[]{:S(2)}) collective-permute-start(s32[40,128]{1,0:T(8,128)S(1)} %pad_add_fusion.asks_ref), channel_id=1, source_target_pairs={{0,127},{1,0},{2,1},{3,2},{4,3},{5,4},{6,5},{7,6},{8,7},{9,8},{10,... | collective-permute-start | bytes 61448 | tf_op jit(solution)/shard_map/ppermute | solution.py:250
  27.4 17.2 %collective-permute-done.ask_prev_ref = s32[40,128]{1,0:T(8,128)S(1)} collective-permute-done((s32[40,128]{1,0:T(8,128)S(1)}, s32[40,128]{1,0:T(8,128)S(1)}, u32[]{:S(2)}, u32[]{:S(2)}) %collective-permute-start) | collective-permute-done | bytes 20512 | tf_op jit(solution)/shard_map/ppermute | solution.py:250
  44.6 0.0 collective-permute-done.1.ask_next_ref
  44.6 0.6 copy-done.4
  45.2 0.0 copy-done.6
  45.2 2.1 %fetch_density.1 = (bf16[32,384]{1,0:T(8,128)(2,1)}, bf16[32,384]{1,0:T(8,128)(2,1)}, bf16[32,384]{1,0:T(8,128)(2,1)}) custom-call(s32[1]{0:T(128)} %bitcast.me_ref, s32[40,128]{1,0:T(8,128)} %copy-done.1, s32[40,128]{1,0:T(8,128)} %copy-done.4, s32[40,128]{1,0:T(8,128)} %copy-done.6, bf16[1024,384]{1,0:T(8,128)(2,1)} %density_ref.1), custom_call_target="tpu_custom_call" | custom-call | flops 100000000 | bytes 1048576 | tf_op jit(solution)/shard_map/fetch_density/pallas_call | solution.py:199
  47.3 7.2 %collective-permute-start.3 = (bf16[32,384]{1,0:T(8,128)(2,1)}, bf16[32,384]{1,0:T(8,128)(2,1)S(1)}, u32[]{:S(2)}, u32[]{:S(2)}) collective-permute-start(bf16[32,384]{1,0:T(8,128)(2,1)} %get-tuple-element.10), channel_id=1, source_target_pairs={{0,127},{1,0},{2,1},{3,2},{4,3},{5,4},{6,5},{7,6},{8,7},{9,8},{10,... | collective-permute-start | bytes 73736 | tf_op jit(solution)/shard_map/ppermute | solution.py:250
  54.5 1.7 %collective-permute-done.2.prev_ref = bf16[32,384]{1,0:T(8,128)(2,1)S(1)} collective-permute-done((bf16[32,384]{1,0:T(8,128)(2,1)}, bf16[32,384]{1,0:T(8,128)(2,1)S(1)}, u32[]{:S(2)}, u32[]{:S(2)}) %collective-permute-start.2) | collective-permute-done | bytes 24608 | tf_op jit(solution)/shard_map/ppermute | solution.py:250
  56.2 0.0 collective-permute-done.3.next_ref
  56.2 3.7 %copy-done = bf16[32,384,384]{2,1,0:T(8,128)(2,1)S(1)} copy-done((bf16[32,384,384]{2,1,0:T(8,128)(2,1)S(1)}, bf16[32,384,384]{2,1,0:T(8,128)(2,1)}, u32[]{:S(2)}) %copy-start) | copy-done | bytes 9437208
  59.9 0.7 copy-done.3
  60.7 3.8 %near_terms.1.own_ref = f32[32,384]{1,0:T(8,128)S(1)} custom-call(s32[1]{0:T(128)} %copy.9.count_ref, bf16[32,384,384]{2,1,0:T(8,128)(2,1)S(1)} %copy-done, bf16[32,384]{1,0:T(8,128)(2,1)S(1)} %copy-done.3, bf16[32,384]{1,0:T(8,128)(2,1)S(1)} %collective-permute-done.2.prev_ref, bf16[32,384]{1,0:T(8,128)(2,1)S(1)} %collective-permute-done.3.next_ref), custom_call_target="tpu_custom_call" | custom-call | flops 1207959552 | bytes 9437184 | tf_op jit(solution)/shard_map/near_terms/pallas_call | solution.py:236
  64.5 0.1 collective-permute-start.4
  64.6 7.4 %collective-permute-start.5 = (f32[32,384]{1,0:T(8,128)S(1)}, f32[32,384]{1,0:T(8,128)S(1)}, u32[]{:S(2)}, u32[]{:S(2)}) collective-permute-start(f32[32,384]{1,0:T(8,128)S(1)} %near_terms.1.own_ref), channel_id=1, source_target_pairs={{0,127},{1,0},{2,1},{3,2},{4,3},{5,4},{6,5},{7,6},{8,7},{9,8},{10,... | collective-permute-start | bytes 147464 | tf_op jit(solution)/shard_map/ppermute | solution.py:250
  72.0 1.5 %collective-permute-done.4.prev_ref = f32[32,384]{1,0:T(8,128)S(1)} collective-permute-done((f32[32,384]{1,0:T(8,128)S(1)}, f32[32,384]{1,0:T(8,128)S(1)}, u32[]{:S(2)}, u32[]{:S(2)}) %collective-permute-start.4) | collective-permute-done | bytes 49184 | tf_op jit(solution)/shard_map/ppermute | solution.py:250
  73.5 0.2 collective-permute-done.5.next_ref
  73.7 5.4 %place_rows.1 = f32[1024,384]{1,0:T(8,128)} custom-call(s32[1]{0:T(128)} %bitcast.me_ref, s32[3200,128]{1,0:T(8,128)S(1)} %bitcast.6, f32[32,384]{1,0:T(8,128)S(1)} %near_terms.1.own_ref, f32[32,384]{1,0:T(8,128)S(1)} %collective-permute-done.4.prev_ref, f32[32,384]{1,0:T(8,128)S(1)} %collective-permute-done.5.next_ref, s32[40,128]{1,0:T(8,128)S(1)} %copy-done.2, ...), custom_call_target="tpu_custom_call" | custom-call | flops 3221225472 | bytes 4194304 | tf_op jit(solution)/shard_map/place_rows/pallas_call | solution.py:170
  (24 shorter events, 0.0 us)
Async XLA Ops:
  0.0 1.4 %copy-start.8 = (f32[1024,384]{1,0:T(8,128)S(1)}, f32[1024,384]{1,0:T(8,128)}, u32[]{:S(2)}) copy-start(f32[1024,384]{1,0:T(8,128)} %pot_ref.1) | copy-start | bytes 4718596
  1.4 0.7 copy-start.9
  8.2 11.8 %copy-start.10 = (s32[32]{0:T(128)S(1)}, s32[32]{0:T(128)}, u32[]{:S(2)}) copy-start(s32[32]{0:T(128)} %param.11) | copy-start | bytes 388
  8.2 11.9 %copy-start.11 = (s32[32]{0:T(128)S(1)}, s32[32]{0:T(128)}, u32[]{:S(2)}) copy-start(s32[32]{0:T(128)} %param.12) | copy-start | bytes 388
  8.2 65.5 %all-to-all-start = ((s32[128,25,1,128]{3,2,1,0:T(1,128)}), s32[128,25,1,128]{3,2,1,0:T(1,128)S(1)}, u32[]{:S(2)}, u32[]{:S(2)}) async-start(s32[128,25,1,128]{3,2,1,0:T(1,128)} %bitcast.2), calls=%async_computation | async-start | bytes 3276800 | tf_op jit(solution)/shard_map/all_to_all | solution.py:265
  20.2 24.5 %copy-start.1 = (s32[40,128]{1,0:T(8,128)}, s32[40,128]{1,0:T(8,128)S(1)}, u32[]{:S(2)}) copy-start(s32[40,128]{1,0:T(8,128)S(1)} %pad_add_fusion.asks_ref) | copy-start | bytes 61444
  20.2 24.4 %collective-permute-start = (s32[40,128]{1,0:T(8,128)S(1)}, s32[40,128]{1,0:T(8,128)S(1)}, u32[]{:S(2)}, u32[]{:S(2)}) collective-permute-start(s32[40,128]{1,0:T(8,128)S(1)} %pad_add_fusion.asks_ref), channel_id=1, source_target_pairs={{0,1},{1,2},{2,3},{3,4},{4,5},{5,6},{6,7},{7,8},{8,9},{9,10},{10,1... | collective-permute-start | bytes 61448 | tf_op jit(solution)/shard_map/ppermute | solution.py:250
  21.2 23.5 %collective-permute-start.1 = (s32[40,128]{1,0:T(8,128)S(1)}, s32[40,128]{1,0:T(8,128)S(1)}, u32[]{:S(2)}, u32[]{:S(2)}) collective-permute-start(s32[40,128]{1,0:T(8,128)S(1)} %pad_add_fusion.asks_ref), channel_id=1, source_target_pairs={{0,127},{1,0},{2,1},{3,2},{4,3},{5,4},{6,5},{7,6},{8,7},{9,8},{10,... | collective-permute-start | bytes 61448 | tf_op jit(solution)/shard_map/ppermute | solution.py:250
  44.6 0.6 copy-start.4
  44.6 0.6 copy-start.6
  47.3 8.9 %collective-permute-start.2 = (bf16[32,384]{1,0:T(8,128)(2,1)}, bf16[32,384]{1,0:T(8,128)(2,1)S(1)}, u32[]{:S(2)}, u32[]{:S(2)}) collective-permute-start(bf16[32,384]{1,0:T(8,128)(2,1)} %get-tuple-element.9), channel_id=1, source_target_pairs={{0,1},{1,2},{2,3},{3,4},{4,5},{5,6},{6,7},{7,8},{8,9},{9,10},{10,1... | collective-permute-start | bytes 73736 | tf_op jit(solution)/shard_map/ppermute | solution.py:250
  47.3 8.9 %collective-permute-start.3 = (bf16[32,384]{1,0:T(8,128)(2,1)}, bf16[32,384]{1,0:T(8,128)(2,1)S(1)}, u32[]{:S(2)}, u32[]{:S(2)}) collective-permute-start(bf16[32,384]{1,0:T(8,128)(2,1)} %get-tuple-element.10), channel_id=1, source_target_pairs={{0,127},{1,0},{2,1},{3,2},{4,3},{5,4},{6,5},{7,6},{8,7},{9,8},{10,... | collective-permute-start | bytes 73736 | tf_op jit(solution)/shard_map/ppermute | solution.py:250
  56.2 3.7 %copy-start = (bf16[32,384,384]{2,1,0:T(8,128)(2,1)S(1)}, bf16[32,384,384]{2,1,0:T(8,128)(2,1)}, u32[]{:S(2)}) copy-start(bf16[32,384,384]{2,1,0:T(8,128)(2,1)} %mats_ref.1) | copy-start | bytes 28311556
  59.9 0.7 copy-start.3
  60.7 13.1 %copy-start.2 = (s32[40,128]{1,0:T(8,128)S(1)}, s32[40,128]{1,0:T(8,128)}, u32[]{:S(2)}) copy-start(s32[40,128]{1,0:T(8,128)} %copy-done.1) | copy-start | bytes 61444
  60.7 13.1 %copy-start.5 = (s32[40,128]{1,0:T(8,128)S(1)}, s32[40,128]{1,0:T(8,128)}, u32[]{:S(2)}) copy-start(s32[40,128]{1,0:T(8,128)} %copy-done.4) | copy-start | bytes 61444
  60.7 13.1 %copy-start.7 = (s32[40,128]{1,0:T(8,128)S(1)}, s32[40,128]{1,0:T(8,128)}, u32[]{:S(2)}) copy-start(s32[40,128]{1,0:T(8,128)} %copy-done.6) | copy-start | bytes 61444
  64.5 9.0 %collective-permute-start.4 = (f32[32,384]{1,0:T(8,128)S(1)}, f32[32,384]{1,0:T(8,128)S(1)}, u32[]{:S(2)}, u32[]{:S(2)}) collective-permute-start(f32[32,384]{1,0:T(8,128)S(1)} %near_terms.1.own_ref), channel_id=1, source_target_pairs={{0,1},{1,2},{2,3},{3,4},{4,5},{5,6},{6,7},{7,8},{8,9},{9,10},{10,1... | collective-permute-start | bytes 147464 | tf_op jit(solution)/shard_map/ppermute | solution.py:250
  64.6 9.2 %collective-permute-start.5 = (f32[32,384]{1,0:T(8,128)S(1)}, f32[32,384]{1,0:T(8,128)S(1)}, u32[]{:S(2)}, u32[]{:S(2)}) collective-permute-start(f32[32,384]{1,0:T(8,128)S(1)} %near_terms.1.own_ref), channel_id=1, source_target_pairs={{0,127},{1,0},{2,1},{3,2},{4,3},{5,4},{6,5},{7,6},{8,7},{9,8},{10,... | collective-permute-start | bytes 147464 | tf_op jit(solution)/shard_map/ppermute | solution.py:250

commit v2 on v1

--- a/solution.py
+++ b/solution.py
@@ -20,6 +20,7 @@
 NT = (((1,), (1,)), ((), ()))
 VMEM = pl.BlockSpec(memory_space=pltpu.VMEM)
 SMEM = pl.BlockSpec(memory_space=pltpu.SMEM)
+HBM = pl.BlockSpec(memory_space=pltpu.HBM)
 
 
 def iota(shape, dim):
@@ -42,10 +43,43 @@
     return jnp.dot(a, b, preferred_element_type=F32)
 
 
-def pack_kernel(map_ref, pot_ref, out_ref, sel, dig, head):
+def pack_kernel(map_hbm, pot_hbm, out_hbm, place, pot, msg, sel, dig, head, sems):
+    get_map = pltpu.make_async_copy(map_hbm, place, sems.at[0])
+    get_map.start()
+    get_pot = []
+    for g in range(4):
+        rows = pl.ds(g * 256, 256)
+        get_pot.append(pltpu.make_async_copy(pot_hbm.at[rows], pot.at[rows], sems.at[1 + g]))
+        get_pot[g].start()
+    get_map.wait()
+
+    dest, label = place[...] >> 10, (place[...] & (ROWS - 1)) + 1
+    sub = iota((128, 128), 0)
+    before = jnp.concatenate([one_hot(sub < iota((128, 128), 1)), one_hot(sub >= 0)], axis=1)
+    hits = [dest[b : b + 1, :] == sub for b in range(8)]
+    hot = [one_hot(h) for h in hits]
+    counts = mm(jnp.concatenate(hot, axis=0), before)
+    carry = jnp.zeros((128, 128), F32)
+    ranks = []
+    for b in range(8):
+        part = counts[b * 128 : b * 128 + 128]
+        ranks.append(jnp.sum(jnp.where(hits[b], part[:, :128] + carry, 0.0), axis=0, keepdims=True))
+        carry = carry + part[:, 128:]
+    low = sub & (CAP - 1)
+    ranked = []
+    for b in range(8):
+        lanes = pl.ds(b * 128, 128)
+        for c in range(CAP):
+            block = times_row(hot[b], jnp.where(ranks[b] == c, 1.0, 0.0))
+            for g in range(8):
+                sel[pl.ds(g * 256 + c * 16, 16), lanes] = block[g * 16 : g * 16 + 16]
+        ranked.append(one_hot(ranks[b].astype(I32) == low))
+
     for g in range(8):
+        if g % 2 == 0:
+            get_pot[g // 2].wait()
         rows = pl.ds(g * 128, 128)
-        x = pot_ref[rows, :]
+        x = pot[rows, :]
         top = jnp.max(jnp.abs(x), axis=1, keepdims=True)
         step = jnp.maximum(top * (1.0 / 32766.0), 2.0**-100)
         expo = jnp.floor(jnp.log2(step) + 1e-3)
@@ -63,64 +97,60 @@
     eye = one_hot(iota((16, 128), 0) == iota((16, 128), 1))
     codes = lax.dot_general(eye, head[...], NT, preferred_element_type=F32)
 
-    place = map_ref[...]
-    dest, label = place >> 10, (place & (ROWS - 1)) + 1
-    sub = iota((128, 128), 0)
-    before = jnp.concatenate([one_hot(sub < iota((128, 128), 1)), one_hot(sub >= 0)], axis=1)
-    hits = [dest[b : b + 1, :] == sub for b in range(8)]
-    hot = [one_hot(h) for h in hits]
-    counts = mm(jnp.concatenate(hot, axis=0), before)
-    carry = jnp.zeros((128, 128), F32)
-    ranks = []
+    digits = [[], [], [], []]
     for b in range(8):
-        part = counts[b * 128 : b * 128 + 128]
-        ranks.append(jnp.sum(jnp.where(hits[b], part[:, :128] + carry, 0.0), axis=0, keepdims=True))
-        carry = carry + part[:, 128:]
-
-    low = iota((128, 128), 0) & (CAP - 1)
-    digits = [[], [], [], []]
-    ranked = []
-    for b in range(8):
-        lanes = pl.ds(b * 128, 128)
-        for c in range(CAP):
-            at = (c % 8) * 256 + (c // 8) * 128
-            sel[pl.ds(at, 128), lanes] = times_row(hot[b], jnp.where(ranks[b] == c, 1.0, 0.0))
         lab = label[b : b + 1, :]
         cols = slice(b * 128, b * 128 + 128)
         for k, row in enumerate(
             ((lab >> 7).astype(F32), (lab & 127).astype(F32), codes[0:1, cols], codes[1:2, cols])
         ):
             digits[k].append(times_row(hot[b], row))
-        ranked.append(one_hot(ranks[b].astype(I32) == low))
     left = jnp.concatenate([jnp.concatenate(d, axis=1) for d in digits], axis=0)
     meta = lax.dot_general(left, jnp.concatenate(ranked, axis=1), NT, preferred_element_type=F32).astype(I32)
     words = jnp.where(
         iota((128, 128), 1) < CAP, meta[0:128] * 128 + meta[128:256], meta[256:384] * 128 + meta[384:512]
     )
-    out_ref[pl.ds(LINES - 1, DEV, stride=LINES), :] = words
-
-    for n in range(TILES):
-        for r in range(8):
-            both = mm(sel[pl.ds(r * 256, 256), :], dig[:, pl.ds(n * 256, 256)])
+    msg[pl.ds(LINES - 1, DEV, stride=LINES), :] = words
+
+    put = []
+    for g in range(8):
+        for n in range(TILES):
+            both = mm(sel[pl.ds(g * 256, 256), :], dig[:, pl.ds(n * 256, 256)])
             q = (both[:, :128] * 256.0 + both[:, 128:]).astype(I32)
-            out_ref[pl.ds(n * 8 + r, DEV, stride=LINES), :] = (q[128:] << 16) | (q[:128] & 0xFFFF)
+            w = (q[128:] << 16) | (q[:128] & 0xFFFF)
+            for r in range(8):
+                msg[pl.ds(g * 16 * LINES + n * 8 + r, 16, stride=LINES), :] = w[r * 16 : r * 16 + 16]
+        lines = pl.ds(g * 16 * LINES, 16 * LINES)
+        put.append(pltpu.make_async_copy(msg.at[lines], out_hbm.at[lines], sems.at[5 + g]))
+        put[g].start()
+    for copy in put:
+        copy.wait()
 
 
 def pack(leaf_to_panel, potentials):
     return pl.pallas_call(
         pack_kernel,
         out_shape=jax.ShapeDtypeStruct((DEV * LINES, 128), I32),
-        in_specs=[VMEM, VMEM],
-        out_specs=VMEM,
+        in_specs=[HBM, HBM],
+        out_specs=HBM,
         scratch_shapes=[
+            pltpu.VMEM((8, 128), I32),
+            pltpu.VMEM((ROWS, BW), F32),
+            pltpu.VMEM((DEV * LINES, 128), I32),
             pltpu.VMEM((DEV * CAP, ROWS), BF16),
             pltpu.VMEM((ROWS, 2 * BW), BF16),
             pltpu.VMEM((ROWS, 128), BF16),
+            pltpu.SemaphoreType.DMA((13,)),
         ],
-        compiler_params=pltpu.CompilerParams(vmem_limit_bytes=40 * 2**20),
+        compiler_params=pltpu.CompilerParams(vmem_limit_bytes=60 * 2**20),
         cost_estimate=pl.CostEstimate(flops=2 * DEV * CAP * ROWS * 2 * BW, bytes_accessed=4 * 2**20, transcendentals=0),
         name="pack_rows",
     )(leaf_to_panel.reshape(8, 128), potentials)
+
+
+def by_slot(lane, own_ref, prev_ref, next_ref, line):
+    own, prev, following = (ref[line : line + 1, :] for ref in (own_ref, prev_ref, next_ref))
+    return jnp.where(lane < SLOTS, own, jnp.where(lane < 2 * SLOTS, prev, following))
 
 
 def place_kernel(me_ref, msg_ref, own_ref, prev_ref, next_ref, asks_ref, ask_prev_ref, ask_next_ref, out_ref, sel, dig):
@@ -138,11 +168,7 @@
             sel[pl.ds(g * 128, 128), pl.ds(c * 128, 128)] = times_row(hot, row)
     lane = iota((1, 128), 1)
     base = me_ref[0] * ROWS
-    rows = jnp.where(
-        lane < SLOTS,
-        asks_ref[SLOTS : SLOTS + 1, :],
-        jnp.where(lane < 2 * SLOTS, ask_prev_ref[SLOTS : SLOTS + 1, :], ask_next_ref[SLOTS : SLOTS + 1, :]),
-    )
+    rows = by_slot(lane, asks_ref, ask_prev_ref, ask_next_ref, 1)
     target = jnp.where((rows < 0) | (lane >= 3 * SLOTS), -1, (rows - base) & (TOTAL - 1))
     for g in range(8):
         hot = one_hot(target - g * 128 == sub)
@@ -182,10 +208,11 @@
     )(me, arrived, *terms, *asks)
 
 
-def fetch_kernel(me_ref, asks_ref, ask_prev_ref, ask_next_ref, density_ref, own_ref, prev_ref, next_ref):
+def fetch_kernel(me_ref, asks_ref, ask_prev_ref, ask_next_ref, density_ref, msg_ref, own_ref, prev_ref, next_ref, out_ref):
     base = me_ref[0] * ROWS
-    asked = jnp.concatenate([asks_ref[0:SLOTS, :], ask_prev_ref[0:SLOTS, :], ask_next_ref[0:SLOTS, :]], axis=0)
-    at = (asked - base) & (TOTAL - 1)
+    cols = by_slot(iota((1, 128), 1), asks_ref, ask_prev_ref, ask_next_ref, 0)
+    at = ((cols - base) & (TOTAL - 1)).astype(F32)
+    at = jnp.transpose(jnp.broadcast_to(at, (128, 128)))[0 : 3 * SLOTS].astype(I32)
     lane = iota((3 * SLOTS, 128), 1)
     hot = jnp.concatenate([one_hot(at - b * 128 == lane) for b in range(8)], axis=1)
     got = mm(hot, density_ref[...]).astype(BF16)
@@ -194,16 +221,18 @@
     next_ref[...] = got[2 * SLOTS :]
 
 
-def fetch(me, asks, density):
+def fetch(me, asks, density, message):
     rows = jax.ShapeDtypeStruct((SLOTS, BW), BF16)
     return pl.pallas_call(
         fetch_kernel,
-        out_shape=(rows, rows, rows),
-        in_specs=[SMEM] + [VMEM] * 4,
-        out_specs=(VMEM, VMEM, VMEM),
+        out_shape=(rows, rows, rows, jax.ShapeDtypeStruct(message.shape, message.dtype)),
+        in_specs=[SMEM] + [VMEM] * 4 + [HBM],
+        out_specs=(VMEM, VMEM, VMEM, HBM),
+        input_output_aliases={5: 3},
+        compiler_params=pltpu.CompilerParams(vmem_limit_bytes=105 * 2**19),
         cost_estimate=pl.CostEstimate(flops=10**8, bytes_accessed=2**20, transcendentals=0),
         name="fetch_density",
-    )(me, *asks, density)
+    )(me, *asks, density, message)
 
 
 STEP = 4
@@ -241,7 +270,7 @@
         out_specs=whole,
         scratch_shapes=[pltpu.VMEM((BW, 128), F32)],
         compiler_params=pltpu.CompilerParams(vmem_limit_bytes=20 * 2**20),
-        cost_estimate=pl.CostEstimate(flops=2 * SLOTS * BW * BW * 128, bytes_accessed=SLOTS * BW * BW * 2, transcendentals=0),
+        cost_estimate=pl.CostEstimate(flops=6 * 10**10, bytes_accessed=SLOTS * BW * BW * 2, transcendentals=0),
         name="near_terms",
     )(count, mats, *rows)
 
@@ -253,20 +282,14 @@
 def on_device(potentials, leaf_to_panel, density, corrections, correction_rows, correction_cols, block_count):
     me = lax.axis_index(AXES).astype(I32).reshape(1)
     live = jnp.arange(SLOTS) < block_count[0]
-    ask = jnp.concatenate(
-        [
-            jnp.broadcast_to(correction_cols[:, None], (SLOTS, 128)),
-            jnp.broadcast_to(jnp.tile(jnp.where(live, correction_rows, -1), 4)[None], (8, 128)),
-        ],
-        axis=0,
-    )
+    ask = jnp.stack([jnp.tile(correction_cols, 4), jnp.tile(jnp.where(live, correction_rows, -1), 4)])
     asks = (ask, shift(ask, 1), shift(ask, -1))
     message = pack(leaf_to_panel, potentials)
+    own, for_prev, for_next, message = fetch(me, asks, density, message)
+    rows = (own, shift(for_next, 1), shift(for_prev, -1))
     arrived = lax.all_to_all(
         message.reshape(DEV, LINES, 1, 128), AXES, split_axis=0, concat_axis=0, tiled=True
     ).reshape(DEV * LINES, 128)
-    own, for_prev, for_next = fetch(me, asks, density)
-    rows = (own, shift(for_next, 1), shift(for_prev, -1))
     term = make_terms(block_count, corrections, rows)
     terms = (term, shift(term, 1), shift(term, -1))
     return place(me, arrived, terms, asks)

time: 79.5 us -> 62.4 us (0.78)
  the two profiles are of different devices: /device:TPU:0 before, /device:TPU:1 now
where the time goes in v2:
time: 62.4 us; the launch traced here: 61.5 us
  starting transfers between devices  26.9 us (43%)
  Pallas kernels  17.4 us (28%)
  waiting for transfers between devices  11.3 us (18%)
  local copies, waits for them, and re-layouts  4.51 us (7%)
  between operations  0.75 us (1%)
  other arithmetic  0.67 us (1%)
    ppermute x6, starting transfers between devices, shift(): lax.ppermute(value, AXES, [(i, (i + steps) % DEV) for i in range(DEV)])  18.9 us
    ppermute x6, waiting for transfers between devices, shift(): lax.ppermute(value, AXES, [(i, (i + steps) % DEV) for i in range(DEV)])  9.5 us
    all_to_all x1, starting transfers between devices, on_device(): lax.all_to_all(message.reshape(DEV, LINES, 1, 128), AXES, split_axis=0, c...  7.96 us
    pallas_call x1, Pallas kernels, pack(): pl.pallas_call(pack_kernel, out_shape=jax.ShapeDtypeStruct((DEV * LINES,...  7.91 us
    pallas_call x1, Pallas kernels, place(): pl.pallas_call(place_kernel, out_shape=jax.ShapeDtypeStruct((ROWS, BW), F...  5.36 us
    pallas_call x1, Pallas kernels, make_terms(): pl.pallas_call(term_kernel, grid=(SLOTS // STEP,), out_shape=jax.ShapeDty...  3.81 us
    unnamed x4, local copies, waits for them, and re-layouts  3.68 us
    all_to_all x1, waiting for transfers between devices, on_device(): lax.all_to_all(message.reshape(DEV, LINES, 1, 128), AXES, split_axis=0, c...  1.82 us
  transfers between devices with their start and end apart: 7, of which 3 were waited for; matrix products, arithmetic and copies ran while one was open for 0% of the time, Pallas kernels for 19%

profile of v2, /device:TPU:1, one launch (start us, length us, event | category | flops | bytes accessed | tf_op | source)
XLA Modules:
  0.0 61.5 jit_solution(17362993445965285094)
XLA Ops:
  0.7 0.7 %compare_select_fusion = s32[32]{0:T(128)S(1)} fusion(s32[32]{0:T(128)} %param.11, s32[]{:T(128)} %bitcast.5), kind=kLoop, calls=%fused_computation | loop fusion | flops 64 | bytes 260 | tf_op jit(solution)/shard_map/jit(_where)/select_n | solution.py:285
  1.3 0.1 stack_tile.7
  1.4 0.7 %tile.4 = s32[4,32]{1,0:T(4,128)S(1)} broadcast(s32[32]{0:T(128)} %param.12), dimensions={1} | broadcast | bytes 640 | tf_op jit(solution)/shard_map/tile | solution.py:285
  2.1 0.1 stack_tile.6
  2.2 7.7 %collective-permute-start.1 = (s32[2,128]{1,0:T(2,128)S(1)}, s32[2,128]{1,0:T(2,128)S(1)}, u32[]{:S(2)}, u32[]{:S(2)}) collective-permute-start(s32[2,128]{1,0:T(2,128)S(1)} %pad_add_fusion.asks_ref), channel_id=1, source_target_pairs={{0,127},{1,0},{2,1},{3,2},{4,3},{5,4},{6,5},{7,6},{8,7},{9,8},{10,... | collective-permute-start | bytes 3080 | tf_op jit(solution)/shard_map/ppermute | solution.py:279
  9.8 0.0 collective-permute-start
  9.8 7.9 %pack_rows.1.msg_ref = s32[3200,128]{1,0:T(8,128)} custom-call(s32[8,128]{1,0:T(8,128)} %bitcast.8, f32[1024,384]{1,0:T(8,128)} %pot_hbm.1), custom_call_target="tpu_custom_call" | custom-call | flops 3221225472 | bytes 4194304 | tf_op jit(solution)/shard_map/pack_rows/pallas_call | solution.py:131
  17.8 0.0 collective-permute-done.1.ask_next_ref
  17.8 0.0 collective-permute-done.ask_prev_ref
  17.8 0.3 fetch_density.1
  18.1 0.1 collective-permute-start.2
  18.2 5.1 %collective-permute-start.3 = (bf16[32,384]{1,0:T(8,128)(2,1)S(1)}, bf16[32,384]{1,0:T(8,128)(2,1)S(1)}, u32[]{:S(2)}, u32[]{:S(2)}) collective-permute-start(bf16[32,384]{1,0:T(8,128)(2,1)S(1)} %get-tuple-element.12), channel_id=1, source_target_pairs={{0,127},{1,0},{2,1},{3,2},{4,3},{5,4},{6,5},{7,6},{8,7},{9,8},{10,... | collective-permute-start | bytes 73736 | tf_op jit(solution)/shard_map/ppermute | solution.py:279
  23.4 8.0 %all-to-all-start = ((s32[128,25,1,128]{3,2,1,0:T(1,128)}), s32[128,25,1,128]{3,2,1,0:T(1,128)S(1)}, u32[]{:S(2)}, u32[]{:S(2)}) async-start(s32[128,25,1,128]{3,2,1,0:T(1,128)} %bitcast.7), calls=%async_computation | async-start | bytes 3276800 | tf_op jit(solution)/shard_map/all_to_all | solution.py:290
  31.3 0.0 collective-permute-done.2.prev_ref
  31.3 0.0 collective-permute-done.3.next_ref
  31.3 0.0 copy-start.1
  31.4 3.7 %copy-done.1 = bf16[32,384,384]{2,1,0:T(8,128)(2,1)S(1)} copy-done((bf16[32,384,384]{2,1,0:T(8,128)(2,1)S(1)}, bf16[32,384,384]{2,1,0:T(8,128)(2,1)}, u32[]{:S(2)}) %copy-start.1) | copy-done | bytes 9437208
  35.0 3.8 %near_terms.1.own_ref = f32[32,384]{1,0:T(8,128)S(1)} custom-call(s32[1]{0:T(128)} %copy.11.count_ref, bf16[32,384,384]{2,1,0:T(8,128)(2,1)S(1)} %copy-done.1, bf16[32,384]{1,0:T(8,128)(2,1)S(1)} %get-tuple-element.10.own_ref, bf16[32,384]{1,0:T(8,128)(2,1)S(1)} %collective-permute-done.2.prev_ref, bf16[32,384]{1,0:T(8,128)(2,1)S(1)} %collective-permute-done.3.next_ref), custom_call_target="tpu_custom_call" | custom-call | flops 60000002048 | bytes 9437184 | tf_op jit(solution)/shard_map/near_terms/pallas_call | solution.py:265
  38.8 6.0 %collective-permute-start.5 = (f32[32,384]{1,0:T(8,128)S(1)}, f32[32,384]{1,0:T(8,128)S(1)}, u32[]{:S(2)}, u32[]{:S(2)}) collective-permute-start(f32[32,384]{1,0:T(8,128)S(1)} %near_terms.1.own_ref), channel_id=1, source_target_pairs={{0,127},{1,0},{2,1},{3,2},{4,3},{5,4},{6,5},{7,6},{8,7},{9,8},{10,... | collective-permute-start | bytes 147464 | tf_op jit(solution)/shard_map/ppermute | solution.py:279
  44.9 0.0 collective-permute-start.4
  44.9 4.3 %collective-permute-done.5.next_ref = f32[32,384]{1,0:T(8,128)S(1)} collective-permute-done((f32[32,384]{1,0:T(8,128)S(1)}, f32[32,384]{1,0:T(8,128)S(1)}, u32[]{:S(2)}, u32[]{:S(2)}) %collective-permute-start.5) | collective-permute-done | bytes 49184 | tf_op jit(solution)/shard_map/ppermute | solution.py:279
  49.2 5.2 %collective-permute-done.4.prev_ref = f32[32,384]{1,0:T(8,128)S(1)} collective-permute-done((f32[32,384]{1,0:T(8,128)S(1)}, f32[32,384]{1,0:T(8,128)S(1)}, u32[]{:S(2)}, u32[]{:S(2)}) %collective-permute-start.4) | collective-permute-done | bytes 49184 | tf_op jit(solution)/shard_map/ppermute | solution.py:279
  54.4 1.8 %all-to-all-done = s32[128,25,1,128]{3,2,1,0:T(1,128)S(1)} async-done(((s32[128,25,1,128]{3,2,1,0:T(1,128)}), s32[128,25,1,128]{3,2,1,0:T(1,128)S(1)}, u32[]{:S(2)}, u32[]{:S(2)}) %all-to-all-start) | async-done | bytes 1638432 | tf_op jit(solution)/shard_map/all_to_all | solution.py:290
  56.2 5.4 %place_rows.1 = f32[1024,384]{1,0:T(8,128)} custom-call(s32[1]{0:T(128)} %bitcast.me_ref, s32[3200,128]{1,0:T(8,128)S(1)} %bitcast.6, f32[32,384]{1,0:T(8,128)S(1)} %near_terms.1.own_ref, f32[32,384]{1,0:T(8,128)S(1)} %collective-permute-done.4.prev_ref, f32[32,384]{1,0:T(8,128)S(1)} %collective-permute-done.5.next_ref, s32[2,128]{1,0:T(2,128)S(1)} %pad_add_fusion.asks_ref, ...), custom_call_target="tpu_custom_call" | custom-call | flops 3221225472 | bytes 4194304 | tf_op jit(solution)/shard_map/place_rows/pallas_call | solution.py:196
  (4 shorter events, 0.0 us)
Async XLA Ops:
  2.2 15.6 %collective-permute-start.1 = (s32[2,128]{1,0:T(2,128)S(1)}, s32[2,128]{1,0:T(2,128)S(1)}, u32[]{:S(2)}, u32[]{:S(2)}) collective-permute-start(s32[2,128]{1,0:T(2,128)S(1)} %pad_add_fusion.asks_ref), channel_id=1, source_target_pairs={{0,127},{1,0},{2,1},{3,2},{4,3},{5,4},{6,5},{7,6},{8,7},{9,8},{10,... | collective-permute-start | bytes 3080 | tf_op jit(solution)/shard_map/ppermute | solution.py:279
  9.8 7.9 %collective-permute-start = (s32[2,128]{1,0:T(2,128)S(1)}, s32[2,128]{1,0:T(2,128)S(1)}, u32[]{:S(2)}, u32[]{:S(2)}) collective-permute-start(s32[2,128]{1,0:T(2,128)S(1)} %pad_add_fusion.asks_ref), channel_id=1, source_target_pairs={{0,1},{1,2},{2,3},{3,4},{4,5},{5,6},{6,7},{7,8},{8,9},{9,10},{10,1... | collective-permute-start | bytes 3080 | tf_op jit(solution)/shard_map/ppermute | solution.py:279
  9.8 8.0 %copy-start = (bf16[1024,384]{1,0:T(8,128)(2,1)S(1)}, bf16[1024,384]{1,0:T(8,128)(2,1)}, u32[]{:S(2)}) copy-start(bf16[1024,384]{1,0:T(8,128)(2,1)} %density_ref.1) | copy-start | bytes 2359300
  18.1 13.2 %collective-permute-start.2 = (bf16[32,384]{1,0:T(8,128)(2,1)S(1)}, bf16[32,384]{1,0:T(8,128)(2,1)S(1)}, u32[]{:S(2)}, u32[]{:S(2)}) collective-permute-start(bf16[32,384]{1,0:T(8,128)(2,1)S(1)} %get-tuple-element.11), channel_id=1, source_target_pairs={{0,1},{1,2},{2,3},{3,4},{4,5},{5,6},{6,7},{7,8},{8,9},{9,10},{10,1... | collective-permute-start | bytes 73736 | tf_op jit(solution)/shard_map/ppermute | solution.py:279
  18.2 13.1 %collective-permute-start.3 = (bf16[32,384]{1,0:T(8,128)(2,1)S(1)}, bf16[32,384]{1,0:T(8,128)(2,1)S(1)}, u32[]{:S(2)}, u32[]{:S(2)}) collective-permute-start(bf16[32,384]{1,0:T(8,128)(2,1)S(1)} %get-tuple-element.12), channel_id=1, source_target_pairs={{0,127},{1,0},{2,1},{3,2},{4,3},{5,4},{6,5},{7,6},{8,7},{9,8},{10,... | collective-permute-start | bytes 73736 | tf_op jit(solution)/shard_map/ppermute | solution.py:279
  23.4 32.8 %all-to-all-start = ((s32[128,25,1,128]{3,2,1,0:T(1,128)}), s32[128,25,1,128]{3,2,1,0:T(1,128)S(1)}, u32[]{:S(2)}, u32[]{:S(2)}) async-start(s32[128,25,1,128]{3,2,1,0:T(1,128)} %bitcast.7), calls=%async_computation | async-start | bytes 3276800 | tf_op jit(solution)/shard_map/all_to_all | solution.py:290
  31.3 3.7 %copy-start.1 = (bf16[32,384,384]{2,1,0:T(8,128)(2,1)S(1)}, bf16[32,384,384]{2,1,0:T(8,128)(2,1)}, u32[]{:S(2)}) copy-start(bf16[32,384,384]{2,1,0:T(8,128)(2,1)} %mats_ref.1) | copy-start | bytes 28311556
  38.8 10.3 %collective-permute-start.5 = (f32[32,384]{1,0:T(8,128)S(1)}, f32[32,384]{1,0:T(8,128)S(1)}, u32[]{:S(2)}, u32[]{:S(2)}) collective-permute-start(f32[32,384]{1,0:T(8,128)S(1)} %near_terms.1.own_ref), channel_id=1, source_target_pairs={{0,127},{1,0},{2,1},{3,2},{4,3},{5,4},{6,5},{7,6},{8,7},{9,8},{10,... | collective-permute-start | bytes 147464 | tf_op jit(solution)/shard_map/ppermute | solution.py:279
  44.9 9.5 %collective-permute-start.4 = (f32[32,384]{1,0:T(8,128)S(1)}, f32[32,384]{1,0:T(8,128)S(1)}, u32[]{:S(2)}, u32[]{:S(2)}) collective-permute-start(f32[32,384]{1,0:T(8,128)S(1)} %near_terms.1.own_ref), channel_id=1, source_target_pairs={{0,1},{1,2},{2,3},{3,4},{4,5},{5,6},{6,7},{7,8},{8,9},{9,10},{10,1... | collective-permute-start | bytes 147464 | tf_op jit(solution)/shard_map/ppermute | solution.py:279

commit v3 on v2

--- a/solution.py
+++ b/solution.py
@@ -148,12 +148,7 @@
     )(leaf_to_panel.reshape(8, 128), potentials)
 
 
-def by_slot(lane, own_ref, prev_ref, next_ref, line):
-    own, prev, following = (ref[line : line + 1, :] for ref in (own_ref, prev_ref, next_ref))
-    return jnp.where(lane < SLOTS, own, jnp.where(lane < 2 * SLOTS, prev, following))
-
-
-def place_kernel(me_ref, msg_ref, own_ref, prev_ref, next_ref, asks_ref, ask_prev_ref, ask_next_ref, out_ref, sel, dig):
+def place_kernel(me_ref, msg_ref, own_ref, prev_ref, next_ref, out_ref, sel, dig):
     heads = jnp.transpose(msg_ref[pl.ds(LINES - 1, DEV, stride=LINES), :].astype(F32)).astype(I32)
     target = heads[0:CAP] - 1
     code = heads[CAP : 2 * CAP]
@@ -168,13 +163,14 @@
             sel[pl.ds(g * 128, 128), pl.ds(c * 128, 128)] = times_row(hot, row)
     lane = iota((1, 128), 1)
     base = me_ref[0] * ROWS
-    rows = by_slot(lane, asks_ref, ask_prev_ref, ask_next_ref, 1)
+    own, prev, following = (ref[SLOTS : SLOTS + 1, 0:128] for ref in (own_ref, prev_ref, next_ref))
+    rows = jnp.where(lane < SLOTS, own, jnp.where(lane < 2 * SLOTS, prev, following)).astype(I32)
     target = jnp.where((rows < 0) | (lane >= 3 * SLOTS), -1, (rows - base) & (TOTAL - 1))
     for g in range(8):
         hot = one_hot(target - g * 128 == sub)
         sel[pl.ds(g * 128, 128), pl.ds(CAP * 128, 128)] = hot
         sel[pl.ds(g * 128, 128), pl.ds(CAP * 128 + 128, 128)] = hot
-    near = jnp.concatenate([own_ref[...], prev_ref[...], next_ref[...], jnp.zeros((SLOTS, BW), F32)], axis=0)
+    near = jnp.concatenate([own_ref[0:SLOTS], prev_ref[0:SLOTS], next_ref[0:SLOTS], jnp.zeros((SLOTS, BW), F32)], axis=0)
     first = near.astype(BF16)
     second = (near - first.astype(F32)).astype(BF16)
     blank = jnp.zeros((256, 128), BF16)
@@ -192,11 +188,11 @@
             out_ref[pl.ds(g * 256, 256), pl.ds(n * 128, 128)] = both[:, :128] * 256.0 + both[:, 128:]
 
 
-def place(me, arrived, terms, asks):
+def place(me, arrived, terms):
     return pl.pallas_call(
         place_kernel,
         out_shape=jax.ShapeDtypeStruct((ROWS, BW), F32),
-        in_specs=[SMEM] + [VMEM] * 7,
+        in_specs=[SMEM] + [VMEM] * 4,
         out_specs=VMEM,
         scratch_shapes=[
             pltpu.VMEM((ROWS, CAP * 128 + 256), BF16),
@@ -205,74 +201,61 @@
         compiler_params=pltpu.CompilerParams(vmem_limit_bytes=40 * 2**20),
         cost_estimate=pl.CostEstimate(flops=2 * DEV * CAP * ROWS * 2 * BW, bytes_accessed=4 * 2**20, transcendentals=0),
         name="place_rows",
-    )(me, arrived, *terms, *asks)
-
-
-def fetch_kernel(me_ref, asks_ref, ask_prev_ref, ask_next_ref, density_ref, msg_ref, own_ref, prev_ref, next_ref, out_ref):
-    base = me_ref[0] * ROWS
-    cols = by_slot(iota((1, 128), 1), asks_ref, ask_prev_ref, ask_next_ref, 0)
-    at = ((cols - base) & (TOTAL - 1)).astype(F32)
-    at = jnp.transpose(jnp.broadcast_to(at, (128, 128)))[0 : 3 * SLOTS].astype(I32)
-    lane = iota((3 * SLOTS, 128), 1)
-    hot = jnp.concatenate([one_hot(at - b * 128 == lane) for b in range(8)], axis=1)
-    got = mm(hot, density_ref[...]).astype(BF16)
-    own_ref[...] = got[0:SLOTS]
-    prev_ref[...] = got[SLOTS : 2 * SLOTS]
-    next_ref[...] = got[2 * SLOTS :]
-
-
-def fetch(me, asks, density, message):
-    rows = jax.ShapeDtypeStruct((SLOTS, BW), BF16)
-    return pl.pallas_call(
-        fetch_kernel,
-        out_shape=(rows, rows, rows, jax.ShapeDtypeStruct(message.shape, message.dtype)),
-        in_specs=[SMEM] + [VMEM] * 4 + [HBM],
-        out_specs=(VMEM, VMEM, VMEM, HBM),
-        input_output_aliases={5: 3},
-        compiler_params=pltpu.CompilerParams(vmem_limit_bytes=105 * 2**19),
-        cost_estimate=pl.CostEstimate(flops=10**8, bytes_accessed=2**20, transcendentals=0),
-        name="fetch_density",
-    )(me, *asks, density, message)
+    )(me, arrived, *terms)
 
 
 STEP = 4
 
 
-def term_kernel(count_ref, mats_ref, own_ref, prev_ref, next_ref, out_ref, acc):
+def term_kernel(me_ref, count_ref, mats_ref, cols_ref, rows_ref, own_ref, prev_ref, next_ref, out_ref, acc, vecs):
     step = pl.program_id(0)
 
     @pl.when(step == 0)
     def _():
         acc[...] = jnp.zeros_like(acc)
-
-    rows = (own_ref[...].astype(F32) + prev_ref[...].astype(F32) + next_ref[...].astype(F32)).astype(BF16)
-    vecs = jnp.concatenate([rows, jnp.zeros((128 - SLOTS, BW), BF16)], axis=0)
+        at = ((cols_ref[...] - (me_ref[0] - 1) * ROWS) & (TOTAL - 1)).astype(F32)
+        at = jnp.transpose(jnp.broadcast_to(at, (128, 128)))[0:SLOTS].astype(I32)
+        lane = iota((SLOTS, 128), 1)
+        got = jnp.zeros((SLOTS, BW), F32)
+        for k, ref in enumerate((prev_ref, own_ref, next_ref)):
+            hot = [one_hot(at - (k * ROWS + b * 128) == lane) for b in range(8)]
+            got = got + mm(jnp.concatenate(hot, axis=1), ref[...])
+        vecs[...] = jnp.concatenate([got, jnp.zeros((128 - SLOTS, BW), F32)], axis=0).astype(BF16)
+
     lane = iota((BW, 128), 1)
     total = acc[...]
     for k in range(STEP):
-        prod = lax.dot_general(mats_ref[k], vecs, NT, preferred_element_type=F32)
+        prod = lax.dot_general(mats_ref[k], vecs[...], NT, preferred_element_type=F32)
         total = jnp.where(lane == step * STEP + k, prod, total)
     acc[...] = total
 
     @pl.when(step == SLOTS // STEP - 1)
     def _():
         live = iota((SLOTS, BW), 0) < count_ref[0]
-        out_ref[...] = jnp.where(live, jnp.transpose(acc[...])[0:SLOTS], 0.0)
-
-
-def make_terms(count, mats, rows):
-    whole = pl.BlockSpec((SLOTS, BW), lambda i: (0, 0))
+        out_ref[0:SLOTS, :] = jnp.where(live, jnp.transpose(acc[...])[0:SLOTS], 0.0)
+        slot = iota((1, 128), 1) & (SLOTS - 1)
+        rows = jnp.where(slot < count_ref[0], rows_ref[...], -1).astype(F32)
+        for n in range(TILES):
+            out_ref[SLOTS : SLOTS + 8, n * 128 : n * 128 + 128] = jnp.broadcast_to(rows, (8, 128))
+
+
+def make_terms(me, count, mats, cols, rows, blocks):
+    def whole(rows, width):
+        return pl.BlockSpec((rows, width), lambda i: (0, 0))
+
     return pl.pallas_call(
         term_kernel,
         grid=(SLOTS // STEP,),
-        out_shape=jax.ShapeDtypeStruct((SLOTS, BW), F32),
-        in_specs=[SMEM, pl.BlockSpec((STEP, BW, BW), lambda i: (i, 0, 0)), whole, whole, whole],
-        out_specs=whole,
-        scratch_shapes=[pltpu.VMEM((BW, 128), F32)],
-        compiler_params=pltpu.CompilerParams(vmem_limit_bytes=20 * 2**20),
-        cost_estimate=pl.CostEstimate(flops=6 * 10**10, bytes_accessed=SLOTS * BW * BW * 2, transcendentals=0),
+        out_shape=jax.ShapeDtypeStruct((SLOTS + 8, BW), F32),
+        in_specs=[SMEM, SMEM, pl.BlockSpec((STEP, BW, BW), lambda i: (i, 0, 0))]
+        + [whole(1, 128)] * 2
+        + [whole(ROWS, BW)] * 3,
+        out_specs=whole(SLOTS + 8, BW),
+        scratch_shapes=[pltpu.VMEM((BW, 128), F32), pltpu.VMEM((128, BW), BF16)],
+        compiler_params=pltpu.CompilerParams(vmem_limit_bytes=30 * 2**20),
+        cost_estimate=pl.CostEstimate(flops=10**10, bytes_accessed=SLOTS * BW * BW * 2, transcendentals=0),
         name="near_terms",
-    )(count, mats, *rows)
+    )(me, count, mats, cols, rows, *blocks)
 
 
 def shift(value, steps):
@@ -281,18 +264,15 @@
 
 def on_device(potentials, leaf_to_panel, density, corrections, correction_rows, correction_cols, block_count):
     me = lax.axis_index(AXES).astype(I32).reshape(1)
-    live = jnp.arange(SLOTS) < block_count[0]
-    ask = jnp.stack([jnp.tile(correction_cols, 4), jnp.tile(jnp.where(live, correction_rows, -1), 4)])
-    asks = (ask, shift(ask, 1), shift(ask, -1))
+    blocks = (density, shift(density, 1), shift(density, -1))
     message = pack(leaf_to_panel, potentials)
-    own, for_prev, for_next, message = fetch(me, asks, density, message)
-    rows = (own, shift(for_next, 1), shift(for_prev, -1))
     arrived = lax.all_to_all(
         message.reshape(DEV, LINES, 1, 128), AXES, split_axis=0, concat_axis=0, tiled=True
     ).reshape(DEV * LINES, 128)
-    term = make_terms(block_count, corrections, rows)
+    cols, rows = (jnp.tile(x, 128 // SLOTS).reshape(1, 128) for x in (correction_cols, correction_rows))
+    term = make_terms(me, block_count, corrections, cols, rows, blocks)
     terms = (term, shift(term, 1), shift(term, -1))
-    return place(me, arrived, terms, asks)
+    return place(me, arrived, terms)
 
 
 def solution(mesh):

time: 62.4 us -> 65.9 us (1.056)
  waiting for transfers between devices: 11.3 us -> 21.8 us
  starting transfers between devices: 26.9 us -> 20.5 us
  Pallas kernels: 17.4 us -> 18.8 us
  other arithmetic: 0.67 us -> 0 us
    ppermute x6 -> x4, waiting for transfers between devices: 9.5 us -> 21.8 us  [shift(): lax.ppermute(value, AXES, [(i, (i + steps) % DEV) for i in range(DEV)])]
    ppermute x6 -> x4, starting transfers between devices: 18.9 us -> 14.5 us  [shift(): lax.ppermute(value, AXES, [(i, (i + steps) % DEV) for i in range(DEV)])]
    all_to_all x1, starting transfers between devices: 7.96 us -> 5.93 us  [on_device(): lax.all_to_all(message.reshape(DEV, LINES, 1, 128), AXES, split_axis=0, c...]
    all_to_all x1, waiting for transfers between devices: 1.82 us -> 0.01 us  [on_device(): lax.all_to_all(message.reshape(DEV, LINES, 1, 128), AXES, split_axis=0, c...]
    pallas_call x1, Pallas kernels: 3.81 us -> 5.58 us  [make_terms(): pl.pallas_call(term_kernel, grid=(SLOTS // STEP,), out_shape=jax.ShapeDty...]
    select_n x1 -> x0, other arithmetic: 0.66 us -> none  [on_device(): jnp.where(live, correction_rows, -1)]
    another operation x4, local copies, waits for them, and re-layouts: 0.83 us -> 0.17 us  [on_device(): jnp.tile(x, 128 // SLOTS).reshape(1, 128)]
    unnamed x4 -> x8, local copies, waits for them, and re-layouts: 3.68 us -> 3.7 us
  transfers between devices with their start and end apart: 7 -> 5, of which waited for: 3 -> 3; matrix products, arithmetic and copies ran while one was open for 0% -> 0% of each run, Pallas kernels for 19% -> 20%
where the time goes in v3:
time: 65.9 us; the launch traced here: 65.6 us
  waiting for transfers between devices  21.8 us (33%)
  starting transfers between devices  20.5 us (31%)
  Pallas kernels  18.8 us (29%)
  local copies, waits for them, and re-layouts  3.87 us (6%)
  between operations  0.73 us (1%)
    ppermute x4, waiting for transfers between devices, shift(): lax.ppermute(value, AXES, [(i, (i + steps) % DEV) for i in range(DEV)])  21.8 us
    ppermute x4, starting transfers between devices, shift(): lax.ppermute(value, AXES, [(i, (i + steps) % DEV) for i in range(DEV)])  14.5 us
    pallas_call x1, Pallas kernels, pack(): pl.pallas_call(pack_kernel, out_shape=jax.ShapeDtypeStruct((DEV * LINES,...  7.83 us
    all_to_all x1, starting transfers between devices, on_device(): lax.all_to_all(message.reshape(DEV, LINES, 1, 128), AXES, split_axis=0, c...  5.93 us
    pallas_call x1, Pallas kernels, make_terms(): pl.pallas_call(term_kernel, grid=(SLOTS // STEP,), out_shape=jax.ShapeDty...  5.58 us
    pallas_call x1, Pallas kernels, place(): pl.pallas_call(place_kernel, out_shape=jax.ShapeDtypeStruct((ROWS, BW), F...  5.35 us
    unnamed x8, local copies, waits for them, and re-layouts  3.7 us
  transfers between devices with their start and end apart: 5, of which 3 were waited for; matrix products, arithmetic and copies ran while one was open for 0% of the time, Pallas kernels for 20%

profile of v3, /device:TPU:1, one launch (start us, length us, event | category | flops | bytes accessed | tf_op | source)
XLA Modules:
  0.0 65.6 jit_solution(6779771836416473150)
XLA Ops:
  0.0 2.1 %collective-permute-start = (bf16[1024,384]{1,0:T(8,128)(2,1)}, bf16[1024,384]{1,0:T(8,128)(2,1)S(1)}, u32[]{:S(2)}, u32[]{:S(2)}) collective-permute-start(bf16[1024,384]{1,0:T(8,128)(2,1)} %own_ref.1), channel_id=1, source_target_pairs={{0,1},{1,2},{2,3},{3,4},{4,5},{5,6},{6,7},{7,8},{8,9},{9,10},{10,1... | collective-permute-start | bytes 2359304 | tf_op jit(solution)/shard_map/ppermute | solution.py:262
  2.1 5.5 %collective-permute-start.1 = (bf16[1024,384]{1,0:T(8,128)(2,1)}, bf16[1024,384]{1,0:T(8,128)(2,1)}, u32[]{:S(2)}, u32[]{:S(2)}) collective-permute-start(bf16[1024,384]{1,0:T(8,128)(2,1)} %own_ref.1), channel_id=1, source_target_pairs={{0,127},{1,0},{2,1},{3,2},{4,3},{5,4},{6,5},{7,6},{8,7},{9,8},{10,... | collective-permute-start | bytes 2359304 | tf_op jit(solution)/shard_map/ppermute | solution.py:262
  7.6 7.8 %pack_rows.1 = s32[3200,128]{1,0:T(8,128)} custom-call(s32[8,128]{1,0:T(8,128)} %bitcast.6, f32[1024,384]{1,0:T(8,128)} %pot_hbm.1), custom_call_target="tpu_custom_call" | custom-call | flops 3221225472 | bytes 4194304 | tf_op jit(solution)/shard_map/pack_rows/pallas_call | solution.py:131
  15.4 0.0 copy-start.2
  15.4 0.0 copy-start.3
  15.5 0.0 copy-start.1
  15.5 5.9 %all-to-all-start = ((s32[128,25,1,128]{3,2,1,0:T(1,128)}), s32[128,25,1,128]{3,2,1,0:T(1,128)S(1)}, u32[]{:S(2)}, u32[]{:S(2)}) async-start(s32[128,25,1,128]{3,2,1,0:T(1,128)} %bitcast.5), calls=%async_computation | async-start | bytes 3276800 | tf_op jit(solution)/shard_map/all_to_all | solution.py:269
  22.1 0.0 copy-done.2
  22.1 0.1 reshape_tile.6.cols_ref
  22.2 0.0 copy-done.3
  22.2 0.1 reshape_tile.7.rows_ref
  22.3 3.8 %collective-permute-done.prev_ref = bf16[1024,384]{1,0:T(8,128)(2,1)S(1)} collective-permute-done((bf16[1024,384]{1,0:T(8,128)(2,1)}, bf16[1024,384]{1,0:T(8,128)(2,1)S(1)}, u32[]{:S(2)}, u32[]{:S(2)}) %collective-permute-start) | collective-permute-done | bytes 786464 | tf_op jit(solution)/shard_map/ppermute | solution.py:262
  26.1 16.4 %collective-permute-done.1.next_ref = bf16[1024,384]{1,0:T(8,128)(2,1)} collective-permute-done((bf16[1024,384]{1,0:T(8,128)(2,1)}, bf16[1024,384]{1,0:T(8,128)(2,1)}, u32[]{:S(2)}, u32[]{:S(2)}) %collective-permute-start.1) | collective-permute-done | bytes 786464 | tf_op jit(solution)/shard_map/ppermute | solution.py:262
  42.4 0.0 copy-done.1
  42.4 0.0 copy-start
  42.4 3.7 %copy-done = bf16[32,384,384]{2,1,0:T(8,128)(2,1)S(1)} copy-done((bf16[32,384,384]{2,1,0:T(8,128)(2,1)S(1)}, bf16[32,384,384]{2,1,0:T(8,128)(2,1)}, u32[]{:S(2)}) %copy-start) | copy-done | bytes 9437208
  46.1 5.6 %near_terms.1.own_ref = f32[40,384]{1,0:T(8,128)S(1)} custom-call(s32[1]{0:T(128)} %bitcast.me_ref, s32[1]{0:T(128)S(6)} %copy.9.count_ref, bf16[32,384,384]{2,1,0:T(8,128)(2,1)S(1)} %copy-done, s32[1,128]{1,0:T(1,128)S(1)} %reshape_tile.6.cols_ref, s32[1,128]{1,0:T(1,128)S(1)} %reshape_tile.7.rows_ref, bf16[1024,384]{1,0:T(8,128)(2,1)S(1)} %copy-done.1, ...), custom_call_target="tpu_custom_call" | custom-call | flops 10000000000 | bytes 9437184 | tf_op jit(solution)/shard_map/near_terms/pallas_call | solution.py:246
  51.7 0.1 collective-permute-start.2
  51.8 6.9 %collective-permute-start.3 = (f32[40,384]{1,0:T(8,128)S(1)}, f32[40,384]{1,0:T(8,128)S(1)}, u32[]{:S(2)}, u32[]{:S(2)}) collective-permute-start(f32[40,384]{1,0:T(8,128)S(1)} %near_terms.1.own_ref), channel_id=1, source_target_pairs={{0,127},{1,0},{2,1},{3,2},{4,3},{5,4},{6,5},{7,6},{8,7},{9,8},{10,... | collective-permute-start | bytes 184328 | tf_op jit(solution)/shard_map/ppermute | solution.py:262
  58.6 1.6 %collective-permute-done.2.prev_ref = f32[40,384]{1,0:T(8,128)S(1)} collective-permute-done((f32[40,384]{1,0:T(8,128)S(1)}, f32[40,384]{1,0:T(8,128)S(1)}, u32[]{:S(2)}, u32[]{:S(2)}) %collective-permute-start.2) | collective-permute-done | bytes 61472 | tf_op jit(solution)/shard_map/ppermute | solution.py:262
  60.3 0.0 collective-permute-done.3.next_ref
  60.3 0.0 all-to-all-done
  60.3 5.3 %place_rows.1 = f32[1024,384]{1,0:T(8,128)} custom-call(s32[1]{0:T(128)} %bitcast.me_ref, s32[3200,128]{1,0:T(8,128)S(1)} %bitcast.4, f32[40,384]{1,0:T(8,128)S(1)} %near_terms.1.own_ref, f32[40,384]{1,0:T(8,128)S(1)} %collective-permute-done.2.prev_ref, f32[40,384]{1,0:T(8,128)S(1)} %collective-permute-done.3.next_ref), custom_call_target="tpu_custom_call" | custom-call | flops 3221225472 | bytes 4194304 | tf_op jit(solution)/shard_map/place_rows/pallas_call | solution.py:192
  (2 shorter events, 0.0 us)
Async XLA Ops:
  0.0 26.1 %collective-permute-start = (bf16[1024,384]{1,0:T(8,128)(2,1)}, bf16[1024,384]{1,0:T(8,128)(2,1)S(1)}, u32[]{:S(2)}, u32[]{:S(2)}) collective-permute-start(bf16[1024,384]{1,0:T(8,128)(2,1)} %own_ref.1), channel_id=1, source_target_pairs={{0,1},{1,2},{2,3},{3,4},{4,5},{5,6},{6,7},{7,8},{8,9},{9,10},{10,1... | collective-permute-start | bytes 2359304 | tf_op jit(solution)/shard_map/ppermute | solution.py:262
  2.1 40.3 %collective-permute-start.1 = (bf16[1024,384]{1,0:T(8,128)(2,1)}, bf16[1024,384]{1,0:T(8,128)(2,1)}, u32[]{:S(2)}, u32[]{:S(2)}) collective-permute-start(bf16[1024,384]{1,0:T(8,128)(2,1)} %own_ref.1), channel_id=1, source_target_pairs={{0,127},{1,0},{2,1},{3,2},{4,3},{5,4},{6,5},{7,6},{8,7},{9,8},{10,... | collective-permute-start | bytes 2359304 | tf_op jit(solution)/shard_map/ppermute | solution.py:262
  15.4 6.6 %copy-start.2 = (s32[32]{0:T(128)S(1)}, s32[32]{0:T(128)}, u32[]{:S(2)}) copy-start(s32[32]{0:T(128)} %param.12) | copy-start | bytes 388
  15.4 6.7 %copy-start.3 = (s32[32]{0:T(128)S(1)}, s32[32]{0:T(128)}, u32[]{:S(2)}) copy-start(s32[32]{0:T(128)} %param.11) | copy-start | bytes 388
  15.5 27.0 %copy-start.1 = (bf16[1024,384]{1,0:T(8,128)(2,1)S(1)}, bf16[1024,384]{1,0:T(8,128)(2,1)}, u32[]{:S(2)}) copy-start(bf16[1024,384]{1,0:T(8,128)(2,1)} %own_ref.1) | copy-start | bytes 2359300
  15.5 44.8 %all-to-all-start = ((s32[128,25,1,128]{3,2,1,0:T(1,128)}), s32[128,25,1,128]{3,2,1,0:T(1,128)S(1)}, u32[]{:S(2)}, u32[]{:S(2)}) async-start(s32[128,25,1,128]{3,2,1,0:T(1,128)} %bitcast.5), calls=%async_computation | async-start | bytes 3276800 | tf_op jit(solution)/shard_map/all_to_all | solution.py:269
  42.4 3.7 %copy-start = (bf16[32,384,384]{2,1,0:T(8,128)(2,1)S(1)}, bf16[32,384,384]{2,1,0:T(8,128)(2,1)}, u32[]{:S(2)}) copy-start(bf16[32,384,384]{2,1,0:T(8,128)(2,1)} %mats_ref.1) | copy-start | bytes 28311556
  51.7 8.6 %collective-permute-start.2 = (f32[40,384]{1,0:T(8,128)S(1)}, f32[40,384]{1,0:T(8,128)S(1)}, u32[]{:S(2)}, u32[]{:S(2)}) collective-permute-start(f32[40,384]{1,0:T(8,128)S(1)} %near_terms.1.own_ref), channel_id=1, source_target_pairs={{0,1},{1,2},{2,3},{3,4},{4,5},{5,6},{6,7},{7,8},{8,9},{9,10},{10,1... | collective-permute-start | bytes 184328 | tf_op jit(solution)/shard_map/ppermute | solution.py:262
  51.8 8.5 %collective-permute-start.3 = (f32[40,384]{1,0:T(8,128)S(1)}, f32[40,384]{1,0:T(8,128)S(1)}, u32[]{:S(2)}, u32[]{:S(2)}) collective-permute-start(f32[40,384]{1,0:T(8,128)S(1)} %near_terms.1.own_ref), channel_id=1, source_target_pairs={{0,127},{1,0},{2,1},{3,2},{4,3},{5,4},{6,5},{7,6},{8,7},{9,8},{10,... | collective-permute-start | bytes 184328 | tf_op jit(solution)/shard_map/ppermute | solution.py:262

commit v4 on v3

--- a/solution.py
+++ b/solution.py
@@ -148,7 +148,7 @@
     )(leaf_to_panel.reshape(8, 128), potentials)
 
 
-def place_kernel(me_ref, msg_ref, own_ref, prev_ref, next_ref, out_ref, sel, dig):
+def place_kernel(me_ref, msg_ref, own_ref, near_ref, far_ref, out_ref, sel, dig):
     heads = jnp.transpose(msg_ref[pl.ds(LINES - 1, DEV, stride=LINES), :].astype(F32)).astype(I32)
     target = heads[0:CAP] - 1
     code = heads[CAP : 2 * CAP]
@@ -163,14 +163,14 @@
             sel[pl.ds(g * 128, 128), pl.ds(c * 128, 128)] = times_row(hot, row)
     lane = iota((1, 128), 1)
     base = me_ref[0] * ROWS
-    own, prev, following = (ref[SLOTS : SLOTS + 1, 0:128] for ref in (own_ref, prev_ref, next_ref))
-    rows = jnp.where(lane < SLOTS, own, jnp.where(lane < 2 * SLOTS, prev, following)).astype(I32)
+    own, adjacent, other = (ref[SLOTS : SLOTS + 1, 0:128] for ref in (own_ref, near_ref, far_ref))
+    rows = jnp.where(lane < SLOTS, own, jnp.where(lane < 2 * SLOTS, adjacent, other)).astype(I32)
     target = jnp.where((rows < 0) | (lane >= 3 * SLOTS), -1, (rows - base) & (TOTAL - 1))
     for g in range(8):
         hot = one_hot(target - g * 128 == sub)
         sel[pl.ds(g * 128, 128), pl.ds(CAP * 128, 128)] = hot
         sel[pl.ds(g * 128, 128), pl.ds(CAP * 128 + 128, 128)] = hot
-    near = jnp.concatenate([own_ref[0:SLOTS], prev_ref[0:SLOTS], next_ref[0:SLOTS], jnp.zeros((SLOTS, BW), F32)], axis=0)
+    near = jnp.concatenate([own_ref[0:SLOTS], near_ref[0:SLOTS], far_ref[0:SLOTS], jnp.zeros((SLOTS, BW), F32)], axis=0)
     first = near.astype(BF16)
     second = (near - first.astype(F32)).astype(BF16)
     blank = jnp.zeros((256, 128), BF16)
@@ -204,22 +204,43 @@
     )(me, arrived, *terms)
 
 
+def fetch_kernel(me_ref, own_cols, near_cols, far_cols, density_ref, msg_ref, own_ref, near_ref, far_ref, out_ref):
+    base = me_ref[0] * ROWS
+    cols = jnp.concatenate([own_cols[...], near_cols[...], far_cols[...], own_cols[...]], axis=1)
+    at = ((cols - base) & (TOTAL - 1)).astype(F32)
+    at = jnp.transpose(jnp.broadcast_to(at, (128, 128)))[0 : 3 * SLOTS].astype(I32)
+    lane = iota((3 * SLOTS, 128), 1)
+    hot = jnp.concatenate([one_hot(at - b * 128 == lane) for b in range(8)], axis=1)
+    got = mm(hot, density_ref[...]).astype(BF16)
+    own_ref[...] = got[0:SLOTS]
+    near_ref[...] = got[SLOTS : 2 * SLOTS]
+    far_ref[...] = got[2 * SLOTS :]
+
+
+def fetch(me, cols, density, message):
+    rows = jax.ShapeDtypeStruct((SLOTS, BW), BF16)
+    return pl.pallas_call(
+        fetch_kernel,
+        out_shape=(rows, rows, rows, jax.ShapeDtypeStruct(message.shape, message.dtype)),
+        in_specs=[SMEM] + [VMEM] * 4 + [HBM],
+        out_specs=(VMEM, VMEM, VMEM, HBM),
+        input_output_aliases={5: 3},
+        compiler_params=pltpu.CompilerParams(vmem_limit_bytes=105 * 2**19),
+        cost_estimate=pl.CostEstimate(flops=10**8, bytes_accessed=2**20, transcendentals=0),
+        name="fetch_density",
+    )(me, *(x.reshape(1, SLOTS) for x in cols), density, message)
+
+
 STEP = 4
 
 
-def term_kernel(me_ref, count_ref, mats_ref, cols_ref, rows_ref, own_ref, prev_ref, next_ref, out_ref, acc, vecs):
+def term_kernel(count_ref, mats_ref, targets_ref, own_ref, near_ref, far_ref, out_ref, acc, vecs):
     step = pl.program_id(0)
 
     @pl.when(step == 0)
     def _():
         acc[...] = jnp.zeros_like(acc)
-        at = ((cols_ref[...] - (me_ref[0] - 1) * ROWS) & (TOTAL - 1)).astype(F32)
-        at = jnp.transpose(jnp.broadcast_to(at, (128, 128)))[0:SLOTS].astype(I32)
-        lane = iota((SLOTS, 128), 1)
-        got = jnp.zeros((SLOTS, BW), F32)
-        for k, ref in enumerate((prev_ref, own_ref, next_ref)):
-            hot = [one_hot(at - (k * ROWS + b * 128) == lane) for b in range(8)]
-            got = got + mm(jnp.concatenate(hot, axis=1), ref[...])
+        got = own_ref[...].astype(F32) + near_ref[...].astype(F32) + far_ref[...].astype(F32)
         vecs[...] = jnp.concatenate([got, jnp.zeros((128 - SLOTS, BW), F32)], axis=0).astype(BF16)
 
     lane = iota((BW, 128), 1)
@@ -234,12 +255,12 @@
         live = iota((SLOTS, BW), 0) < count_ref[0]
         out_ref[0:SLOTS, :] = jnp.where(live, jnp.transpose(acc[...])[0:SLOTS], 0.0)
         slot = iota((1, 128), 1) & (SLOTS - 1)
-        rows = jnp.where(slot < count_ref[0], rows_ref[...], -1).astype(F32)
+        rows = jnp.where(slot < count_ref[0], targets_ref[...], -1).astype(F32)
         for n in range(TILES):
             out_ref[SLOTS : SLOTS + 8, n * 128 : n * 128 + 128] = jnp.broadcast_to(rows, (8, 128))
 
 
-def make_terms(me, count, mats, cols, rows, blocks):
+def make_terms(count, mats, targets, rows):
     def whole(rows, width):
         return pl.BlockSpec((rows, width), lambda i: (0, 0))
 
@@ -247,31 +268,35 @@
         term_kernel,
         grid=(SLOTS // STEP,),
         out_shape=jax.ShapeDtypeStruct((SLOTS + 8, BW), F32),
-        in_specs=[SMEM, SMEM, pl.BlockSpec((STEP, BW, BW), lambda i: (i, 0, 0))]
-        + [whole(1, 128)] * 2
-        + [whole(ROWS, BW)] * 3,
+        in_specs=[SMEM, pl.BlockSpec((STEP, BW, BW), lambda i: (i, 0, 0)), whole(1, 128)] + [whole(SLOTS, BW)] * 3,
         out_specs=whole(SLOTS + 8, BW),
         scratch_shapes=[pltpu.VMEM((BW, 128), F32), pltpu.VMEM((128, BW), BF16)],
-        compiler_params=pltpu.CompilerParams(vmem_limit_bytes=30 * 2**20),
-        cost_estimate=pl.CostEstimate(flops=10**10, bytes_accessed=SLOTS * BW * BW * 2, transcendentals=0),
+        compiler_params=pltpu.CompilerParams(vmem_limit_bytes=20 * 2**20),
+        cost_estimate=pl.CostEstimate(flops=6 * 10**10, bytes_accessed=SLOTS * BW * BW * 2, transcendentals=0),
         name="near_terms",
-    )(me, count, mats, cols, rows, *blocks)
-
-
-def shift(value, steps):
-    return lax.ppermute(value, AXES, [(i, (i + steps) % DEV) for i in range(DEV)])
+    )(count, mats, targets, *rows)
+
+
+def swap_near(value):
+    return lax.ppermute(value, AXES, [(i, i ^ 1) for i in range(DEV)])
+
+
+def swap_far(value):
+    return lax.ppermute(value, AXES, [(i, (i - 1 + 2 * (i % 2)) % DEV) for i in range(DEV)])
 
 
 def on_device(potentials, leaf_to_panel, density, corrections, correction_rows, correction_cols, block_count):
     me = lax.axis_index(AXES).astype(I32).reshape(1)
-    blocks = (density, shift(density, 1), shift(density, -1))
+    cols = (correction_cols, swap_near(correction_cols), swap_far(correction_cols))
     message = pack(leaf_to_panel, potentials)
+    own, for_near, for_far, message = fetch(me, cols, density, message)
+    rows = (own, swap_near(for_near), swap_far(for_far))
     arrived = lax.all_to_all(
         message.reshape(DEV, LINES, 1, 128), AXES, split_axis=0, concat_axis=0, tiled=True
     ).reshape(DEV * LINES, 128)
-    cols, rows = (jnp.tile(x, 128 // SLOTS).reshape(1, 128) for x in (correction_cols, correction_rows))
-    term = make_terms(me, block_count, corrections, cols, rows, blocks)
-    terms = (term, shift(term, 1), shift(term, -1))
+    targets = jnp.tile(correction_rows, 128 // SLOTS).reshape(1, 128)
+    term = make_terms(block_count, corrections, targets, rows)
+    terms = (term, swap_near(term), swap_far(term))
     return place(me, arrived, terms)
 
 

time: 65.9 us -> 60 us (0.910); the launches traced: 65.6 us -> 59 us
  waiting for transfers between devices: 21.8 us -> 11.1 us
  starting transfers between devices: 20.5 us -> 25.7 us
  Pallas kernels: 18.8 us -> 17.6 us
    ppermute x4 -> x6, waiting for transfers between devices: 21.8 us -> 9.09 us  [the longest x3 9.08 us: swap_far(): lax.ppermute(value, AXES, [(i, (i - 1 + 2 * (i % 2)) % DEV) for i in rang...]
    all_to_all x1, starting transfers between devices: 5.93 us -> 10.1 us  [on_device(): lax.all_to_all(message.reshape(DEV, LINES, 1, 128), AXES, split_axis=0, c...]
    all_to_all x1, waiting for transfers between devices: 0.01 us -> 2.06 us  [on_device(): lax.all_to_all(message.reshape(DEV, LINES, 1, 128), AXES, split_axis=0, c...]
    pallas_call x1, Pallas kernels: 5.58 us -> 3.97 us  [make_terms(): pl.pallas_call(term_kernel, grid=(SLOTS // STEP,), out_shape=jax.ShapeDty...]
    ppermute x4 -> x6, starting transfers between devices: 14.5 us -> 15.6 us  [the longest x3 14.1 us: swap_far(): lax.ppermute(value, AXES, [(i, (i - 1 + 2 * (i % 2)) % DEV) for i in rang...]
  transfers between devices with their start and end apart: 5 -> 7, of which waited for: 3 -> 2; matrix products, arithmetic and copies ran while one was open for 0% -> 0% of each run, Pallas kernels for 20% -> 20%
where the time goes in v4:
time: 60 us; the launch traced here: 59 us
  starting transfers between devices  25.7 us (43%)
  Pallas kernels  17.6 us (29%)
  waiting for transfers between devices  11.1 us (18%)
  local copies, waits for them, and re-layouts  3.77 us (6%)
  between operations  0.77 us (1%)
    ppermute x3, starting transfers between devices, swap_far(): lax.ppermute(value, AXES, [(i, (i - 1 + 2 * (i % 2)) % DEV) for i in rang...  14.1 us
    all_to_all x1, starting transfers between devices, on_device(): lax.all_to_all(message.reshape(DEV, LINES, 1, 128), AXES, split_axis=0, c...  10.1 us
    ppermute x3, waiting for transfers between devices, swap_far(): lax.ppermute(value, AXES, [(i, (i - 1 + 2 * (i % 2)) % DEV) for i in rang...  9.08 us
    pallas_call x1, Pallas kernels, pack(): pl.pallas_call(pack_kernel, out_shape=jax.ShapeDtypeStruct((DEV * LINES,...  7.91 us
    pallas_call x1, Pallas kernels, place(): pl.pallas_call(place_kernel, out_shape=jax.ShapeDtypeStruct((ROWS, BW), F...  5.35 us
    pallas_call x1, Pallas kernels, make_terms(): pl.pallas_call(term_kernel, grid=(SLOTS // STEP,), out_shape=jax.ShapeDty...  3.97 us
    unnamed x8, local copies, waits for them, and re-layouts  3.69 us
    all_to_all x1, waiting for transfers between devices, on_device(): lax.all_to_all(message.reshape(DEV, LINES, 1, 128), AXES, split_axis=0, c...  2.06 us
  transfers between devices with their start and end apart: 7, of which 2 were waited for; matrix products, arithmetic and copies ran while one was open for 0% of the time, Pallas kernels for 20%

profile of v4, /device:TPU:1, one launch (start us, length us, event | category | flops | bytes accessed | tf_op | source)
XLA Modules:
  0.0 59.0 jit_solution(8436673174175125409)
XLA Ops:
  0.0 7.6 %collective-permute-start.1 = (s32[32]{0:T(128)}, s32[32]{0:T(128)S(1)}, u32[]{:S(2)}, u32[]{:S(2)}) collective-permute-start(s32[32]{0:T(128)} %param.12), channel_id=1, source_target_pairs={{0,127},{1,2},{2,1},{3,4},{4,3},{5,6},{6,5},{7,8},{8,7},{9,10},{10... | collective-permute-start | bytes 392 | tf_op jit(solution)/shard_map/ppermute | solution.py:285
  7.6 0.0 collective-permute-start
  7.6 7.9 %pack_rows.1.msg_ref = s32[3200,128]{1,0:T(8,128)} custom-call(s32[8,128]{1,0:T(8,128)} %bitcast.12, f32[1024,384]{1,0:T(8,128)} %pot_hbm.1), custom_call_target="tpu_custom_call" | custom-call | flops 3221225472 | bytes 4194304 | tf_op jit(solution)/shard_map/pack_rows/pallas_call | solution.py:131
  15.5 0.0 copy-start.3
  15.5 0.0 collective-permute-done.1
  15.6 0.0 collective-permute-done
  15.6 0.0 copy-done
  15.6 0.0 copy-done.1
  15.6 0.4 fetch_density.1
  16.0 1.5 %collective-permute-start.2 = (bf16[32,384]{1,0:T(8,128)(2,1)S(1)}, bf16[32,384]{1,0:T(8,128)(2,1)S(1)}, u32[]{:S(2)}, u32[]{:S(2)}) collective-permute-start(bf16[32,384]{1,0:T(8,128)(2,1)S(1)} %get-tuple-element.11), channel_id=1, source_target_pairs={{0,1},{1,0},{2,3},{3,2},{4,5},{5,4},{6,7},{7,6},{8,9},{9,8},{10,11... | collective-permute-start | bytes 73736 | tf_op jit(solution)/shard_map/ppermute | solution.py:281
  17.5 0.6 collective-permute-start.3
  18.8 0.1 reshape_tile.3.targets_ref
  18.9 10.1 %all-to-all-start = ((s32[128,25,1,128]{3,2,1,0:T(1,128)}), s32[128,25,1,128]{3,2,1,0:T(1,128)S(1)}, u32[]{:S(2)}, u32[]{:S(2)}) async-start(s32[128,25,1,128]{3,2,1,0:T(1,128)} %bitcast.11), calls=%async_computation | async-start | bytes 3276800 | tf_op jit(solution)/shard_map/all_to_all | solution.py:294
  28.9 0.0 collective-permute-done.2.near_ref
  28.9 0.0 collective-permute-done.3.far_ref
  29.0 0.0 copy-start.2
  29.0 3.7 %copy-done.2 = bf16[32,384,384]{2,1,0:T(8,128)(2,1)S(1)} copy-done((bf16[32,384,384]{2,1,0:T(8,128)(2,1)S(1)}, bf16[32,384,384]{2,1,0:T(8,128)(2,1)}, u32[]{:S(2)}) %copy-start.2) | copy-done | bytes 9437208
  32.6 4.0 %near_terms.1.own_ref = f32[40,384]{1,0:T(8,128)S(1)} custom-call(s32[1]{0:T(128)S(6)} %copy.11.count_ref, bf16[32,384,384]{2,1,0:T(8,128)(2,1)S(1)} %copy-done.2, s32[1,128]{1,0:T(1,128)S(1)} %reshape_tile.3.targets_ref, bf16[32,384]{1,0:T(8,128)(2,1)S(1)} %get-tuple-element.10.own_ref, bf16[32,384]{1,0:T(8,128)(2,1)S(1)} %collective-permute-done.2.near_ref, ...), custom_call_target="tpu_custom_call" | custom-call | flops 60000002048 | bytes 9437184 | tf_op jit(solution)/shard_map/near_terms/pallas_call | solution.py:267
  36.6 5.9 %collective-permute-start.5 = (f32[40,384]{1,0:T(8,128)S(1)}, f32[40,384]{1,0:T(8,128)S(1)}, u32[]{:S(2)}, u32[]{:S(2)}) collective-permute-start(f32[40,384]{1,0:T(8,128)S(1)} %near_terms.1.own_ref), channel_id=1, source_target_pairs={{0,127},{1,2},{2,1},{3,4},{4,3},{5,6},{6,5},{7,8},{8,7},{9,10},{10... | collective-permute-start | bytes 184328 | tf_op jit(solution)/shard_map/ppermute | solution.py:285
  42.5 0.0 collective-permute-start.4
  42.5 9.1 %collective-permute-done.5.far_ref = f32[40,384]{1,0:T(8,128)S(1)} collective-permute-done((f32[40,384]{1,0:T(8,128)S(1)}, f32[40,384]{1,0:T(8,128)S(1)}, u32[]{:S(2)}, u32[]{:S(2)}) %collective-permute-start.5) | collective-permute-done | bytes 61472 | tf_op jit(solution)/shard_map/ppermute | solution.py:285
  51.6 0.0 collective-permute-done.4.near_ref
  51.6 2.1 %all-to-all-done = s32[128,25,1,128]{3,2,1,0:T(1,128)S(1)} async-done(((s32[128,25,1,128]{3,2,1,0:T(1,128)}), s32[128,25,1,128]{3,2,1,0:T(1,128)S(1)}, u32[]{:S(2)}, u32[]{:S(2)}) %all-to-all-start) | async-done | bytes 1638432 | tf_op jit(solution)/shard_map/all_to_all | solution.py:294
  53.6 5.4 %place_rows.1 = f32[1024,384]{1,0:T(8,128)} custom-call(s32[1]{0:T(128)} %bitcast.me_ref, s32[3200,128]{1,0:T(8,128)S(1)} %bitcast.7, f32[40,384]{1,0:T(8,128)S(1)} %near_terms.1.own_ref, f32[40,384]{1,0:T(8,128)S(1)} %collective-permute-done.4.near_ref, f32[40,384]{1,0:T(8,128)S(1)} %collective-permute-done.5.far_ref), custom_call_target="tpu_custom_call" | custom-call | flops 3221225472 | bytes 4194304 | tf_op jit(solution)/shard_map/place_rows/pallas_call | solution.py:192
  (4 shorter events, 0.0 us)
Async XLA Ops:
  0.0 15.5 %collective-permute-start.1 = (s32[32]{0:T(128)}, s32[32]{0:T(128)S(1)}, u32[]{:S(2)}, u32[]{:S(2)}) collective-permute-start(s32[32]{0:T(128)} %param.12), channel_id=1, source_target_pairs={{0,127},{1,2},{2,1},{3,4},{4,3},{5,6},{6,5},{7,8},{8,7},{9,10},{10... | collective-permute-start | bytes 392 | tf_op jit(solution)/shard_map/ppermute | solution.py:285
  7.6 8.0 %collective-permute-start = (s32[32]{0:T(128)}, s32[32]{0:T(128)S(1)}, u32[]{:S(2)}, u32[]{:S(2)}) collective-permute-start(s32[32]{0:T(128)} %param.12), channel_id=1, source_target_pairs={{0,1},{1,0},{2,3},{3,2},{4,5},{5,4},{6,7},{7,6},{8,9},{9,8},{10,11... | collective-permute-start | bytes 392 | tf_op jit(solution)/shard_map/ppermute | solution.py:281
  7.6 8.0 %copy-start = (bf16[1024,384]{1,0:T(8,128)(2,1)S(1)}, bf16[1024,384]{1,0:T(8,128)(2,1)}, u32[]{:S(2)}) copy-start(bf16[1024,384]{1,0:T(8,128)(2,1)} %density_ref.1) | copy-start | bytes 2359300
  7.6 8.0 %copy-start.1 = (s32[32]{0:T(128)S(1)}, s32[32]{0:T(128)}, u32[]{:S(2)}) copy-start(s32[32]{0:T(128)} %param.12) | copy-start | bytes 388
  15.5 3.2 %copy-start.3 = (s32[32]{0:T(128)S(1)}, s32[32]{0:T(128)}, u32[]{:S(2)}) copy-start(s32[32]{0:T(128)} %param.11) | copy-start | bytes 388
  16.0 12.9 %collective-permute-start.2 = (bf16[32,384]{1,0:T(8,128)(2,1)S(1)}, bf16[32,384]{1,0:T(8,128)(2,1)S(1)}, u32[]{:S(2)}, u32[]{:S(2)}) collective-permute-start(bf16[32,384]{1,0:T(8,128)(2,1)S(1)} %get-tuple-element.11), channel_id=1, source_target_pairs={{0,1},{1,0},{2,3},{3,2},{4,5},{5,4},{6,7},{7,6},{8,9},{9,8},{10,11... | collective-permute-start | bytes 73736 | tf_op jit(solution)/shard_map/ppermute | solution.py:281
  17.5 11.4 %collective-permute-start.3 = (bf16[32,384]{1,0:T(8,128)(2,1)S(1)}, bf16[32,384]{1,0:T(8,128)(2,1)S(1)}, u32[]{:S(2)}, u32[]{:S(2)}) collective-permute-start(bf16[32,384]{1,0:T(8,128)(2,1)S(1)} %get-tuple-element.12), channel_id=1, source_target_pairs={{0,127},{1,2},{2,1},{3,4},{4,3},{5,6},{6,5},{7,8},{8,7},{9,10},{10... | collective-permute-start | bytes 73736 | tf_op jit(solution)/shard_map/ppermute | solution.py:285
  18.9 34.8 %all-to-all-start = ((s32[128,25,1,128]{3,2,1,0:T(1,128)}), s32[128,25,1,128]{3,2,1,0:T(1,128)S(1)}, u32[]{:S(2)}, u32[]{:S(2)}) async-start(s32[128,25,1,128]{3,2,1,0:T(1,128)} %bitcast.11), calls=%async_computation | async-start | bytes 3276800 | tf_op jit(solution)/shard_map/all_to_all | solution.py:294
  29.0 3.7 %copy-start.2 = (bf16[32,384,384]{2,1,0:T(8,128)(2,1)S(1)}, bf16[32,384,384]{2,1,0:T(8,128)(2,1)}, u32[]{:S(2)}) copy-start(bf16[32,384,384]{2,1,0:T(8,128)(2,1)} %mats_ref.1) | copy-start | bytes 28311556
  36.6 15.0 %collective-permute-start.5 = (f32[40,384]{1,0:T(8,128)S(1)}, f32[40,384]{1,0:T(8,128)S(1)}, u32[]{:S(2)}, u32[]{:S(2)}) collective-permute-start(f32[40,384]{1,0:T(8,128)S(1)} %near_terms.1.own_ref), channel_id=1, source_target_pairs={{0,127},{1,2},{2,1},{3,4},{4,3},{5,6},{6,5},{7,8},{8,7},{9,10},{10... | collective-permute-start | bytes 184328 | tf_op jit(solution)/shard_map/ppermute | solution.py:285
  42.5 9.1 %collective-permute-start.4 = (f32[40,384]{1,0:T(8,128)S(1)}, f32[40,384]{1,0:T(8,128)S(1)}, u32[]{:S(2)}, u32[]{:S(2)}) collective-permute-start(f32[40,384]{1,0:T(8,128)S(1)} %near_terms.1.own_ref), channel_id=1, source_target_pairs={{0,1},{1,0},{2,3},{3,2},{4,5},{5,4},{6,7},{7,6},{8,9},{9,8},{10,11... | collective-permute-start | bytes 184328 | tf_op jit(solution)/shard_map/ppermute | solution.py:281

commit v5 on v4

--- a/solution.py
+++ b/solution.py
@@ -10,10 +10,11 @@
 AXES = ("leaf", "panel")
 DEV = 128
 CAP = 16
+HALF = CAP // 2
 ROWS = 1024
 BW = 384
 TILES = BW // 128
-LINES = CAP // 2 * TILES + 1
+LINES = HALF * TILES + 1
 SLOTS = 32
 TOTAL = DEV * ROWS
 F32, BF16, I32 = jnp.float32, jnp.bfloat16, jnp.int32
@@ -69,10 +70,11 @@
     ranked = []
     for b in range(8):
         lanes = pl.ds(b * 128, 128)
-        for c in range(CAP):
-            block = times_row(hot[b], jnp.where(ranks[b] == c, 1.0, 0.0))
-            for g in range(8):
-                sel[pl.ds(g * 256 + c * 16, 16), lanes] = block[g * 16 : g * 16 + 16]
+        for r in range(HALF):
+            weight = jnp.where(ranks[b] == r, 1.0, jnp.where(ranks[b] == r + HALF, 256.0, 0.0))
+            block = times_row(hot[b], weight)
+            for g in range(4):
+                sel[pl.ds(g * 256 + r * 32, 32), lanes] = block[g * 32 : g * 32 + 32]
         ranked.append(one_hot(ranks[b].astype(I32) == low))
 
     for g in range(8):
@@ -89,6 +91,7 @@
         q = jnp.clip(jnp.round(x * (1.0 / scale)), -32767.0, 32767.0)
         hi = jnp.floor(q * (1.0 / 256.0))
         lo = q - hi * 256.0
+        hi = hi + 128.0
         for n in range(TILES):
             dig[rows, pl.ds(n * 256, 128)] = hi[:, n * 128 : n * 128 + 128].astype(BF16)
             dig[rows, pl.ds(n * 256 + 128, 128)] = lo[:, n * 128 : n * 128 + 128].astype(BF16)
@@ -113,14 +116,13 @@
     msg[pl.ds(LINES - 1, DEV, stride=LINES), :] = words
 
     put = []
-    for g in range(8):
+    for g in range(4):
         for n in range(TILES):
-            both = mm(sel[pl.ds(g * 256, 256), :], dig[:, pl.ds(n * 256, 256)])
-            q = (both[:, :128] * 256.0 + both[:, 128:]).astype(I32)
-            w = (q[128:] << 16) | (q[:128] & 0xFFFF)
-            for r in range(8):
-                msg[pl.ds(g * 16 * LINES + n * 8 + r, 16, stride=LINES), :] = w[r * 16 : r * 16 + 16]
-        lines = pl.ds(g * 16 * LINES, 16 * LINES)
+            both = mm(sel[pl.ds(g * 256, 256), :], dig[:, pl.ds(n * 256, 256)]).astype(I32)
+            w = (both[:, :128] << 16) | both[:, 128:]
+            for r in range(HALF):
+                msg[pl.ds(g * 32 * LINES + n * HALF + r, 32, stride=LINES), :] = w[r * 32 : r * 32 + 32]
+        lines = pl.ds(g * 32 * LINES, 32 * LINES)
         put.append(pltpu.make_async_copy(msg.at[lines], out_hbm.at[lines], sems.at[5 + g]))
         put[g].start()
     for copy in put:
@@ -137,10 +139,10 @@
             pltpu.VMEM((8, 128), I32),
             pltpu.VMEM((ROWS, BW), F32),
             pltpu.VMEM((DEV * LINES, 128), I32),
-            pltpu.VMEM((DEV * CAP, ROWS), BF16),
+            pltpu.VMEM((DEV * HALF, ROWS), BF16),
             pltpu.VMEM((ROWS, 2 * BW), BF16),
             pltpu.VMEM((ROWS, 128), BF16),
-            pltpu.SemaphoreType.DMA((13,)),
+            pltpu.SemaphoreType.DMA((9,)),
         ],
         compiler_params=pltpu.CompilerParams(vmem_limit_bytes=60 * 2**20),
         cost_estimate=pl.CostEstimate(flops=2 * DEV * CAP * ROWS * 2 * BW, bytes_accessed=4 * 2**20, transcendentals=0),
@@ -148,44 +150,60 @@
     )(leaf_to_panel.reshape(8, 128), potentials)
 
 
-def place_kernel(me_ref, msg_ref, own_ref, near_ref, far_ref, out_ref, sel, dig):
-    heads = jnp.transpose(msg_ref[pl.ds(LINES - 1, DEV, stride=LINES), :].astype(F32)).astype(I32)
-    target = heads[0:CAP] - 1
-    code = heads[CAP : 2 * CAP]
+def place_kernel(me_ref, msg_ref, own_ref, near_ref, far_ref, out_hbm, out, sel, dig, hot_near, sems):
+    heads = msg_ref[pl.ds(LINES - 1, DEV, stride=LINES), :]
+    turned = jnp.transpose(heads.astype(F32)).astype(I32)
+    target = turned[0:CAP] - 1
     high, low = target >> 7, target & 127
-    scale = jnp.exp2((code >> 7).astype(F32) - 128.0).astype(BF16).astype(F32)
-    scale = scale * (1.0 + (code & 127).astype(F32) * (1.0 / 64.0))
     sub = iota((128, 128), 0)
+    lane = iota((128, 128), 1)
     for c in range(CAP):
         hot = one_hot(low[c : c + 1] == sub)
-        for g in range(8):
-            row = jnp.where(high[c : c + 1] == g, scale[c : c + 1], 0.0)
+        for g in range(4):
+            row = jnp.where(high[c : c + 1] == g, 1.0, jnp.where(high[c : c + 1] == g + 4, 256.0, 0.0))
             sel[pl.ds(g * 128, 128), pl.ds(c * 128, 128)] = times_row(hot, row)
+        code = heads[:, CAP + c : CAP + c + 1]
+        code = jnp.where(lane == 0, code >> 7, jnp.where(lane == 1, code & 127, 0))
+        dig[pl.ds(c * 128, 128), pl.ds(2 * BW, 128)] = code.astype(F32).astype(BF16)
+    for n in range(TILES):
+        for r in range(HALF):
+            w = msg_ref[pl.ds(n * HALF + r, DEV, stride=LINES), :]
+            for c, hi, lo in ((r, (w >> 16) & 255, w & 255), (r + HALF, (w >> 24) & 255, (w >> 8) & 255)):
+                dig[pl.ds(c * 128, 128), pl.ds(n * 256, 128)] = hi.astype(F32).astype(BF16)
+                dig[pl.ds(c * 128, 128), pl.ds(n * 256 + 128, 128)] = lo.astype(F32).astype(BF16)
     lane = iota((1, 128), 1)
-    base = me_ref[0] * ROWS
     own, adjacent, other = (ref[SLOTS : SLOTS + 1, 0:128] for ref in (own_ref, near_ref, far_ref))
     rows = jnp.where(lane < SLOTS, own, jnp.where(lane < 2 * SLOTS, adjacent, other)).astype(I32)
-    target = jnp.where((rows < 0) | (lane >= 3 * SLOTS), -1, (rows - base) & (TOTAL - 1))
+    target = jnp.where((rows < 0) | (lane >= 3 * SLOTS), -1, (rows - me_ref[0] * ROWS) & (TOTAL - 1))
     for g in range(8):
         hot = one_hot(target - g * 128 == sub)
-        sel[pl.ds(g * 128, 128), pl.ds(CAP * 128, 128)] = hot
-        sel[pl.ds(g * 128, 128), pl.ds(CAP * 128 + 128, 128)] = hot
+        hot_near[pl.ds(g * 128, 128), 0:128] = hot
+        hot_near[pl.ds(g * 128, 128), 128:256] = hot
     near = jnp.concatenate([own_ref[0:SLOTS], near_ref[0:SLOTS], far_ref[0:SLOTS], jnp.zeros((SLOTS, BW), F32)], axis=0)
     first = near.astype(BF16)
-    second = (near - first.astype(F32)).astype(BF16)
-    blank = jnp.zeros((256, 128), BF16)
-    for n in range(TILES):
-        for r in range(8):
-            w = msg_ref[pl.ds(n * 8 + r, DEV, stride=LINES), :]
-            for c, hi, lo in ((r, (w << 16) >> 24, w & 255), (r + 8, w >> 24, (w >> 16) & 255)):
-                dig[pl.ds(c * 128, 128), pl.ds(n * 256, 128)] = hi.astype(F32).astype(BF16)
-                dig[pl.ds(c * 128, 128), pl.ds(n * 256 + 128, 128)] = lo.astype(F32).astype(BF16)
-        dig[pl.ds(CAP * 128, 256), pl.ds(n * 256, 128)] = blank
-        dig[pl.ds(CAP * 128, 128), pl.ds(n * 256 + 128, 128)] = first[:, n * 128 : n * 128 + 128]
-        dig[pl.ds(CAP * 128 + 128, 128), pl.ds(n * 256 + 128, 128)] = second[:, n * 128 : n * 128 + 128]
-        for g in range(4):
-            both = mm(sel[pl.ds(g * 256, 256), :], dig[:, pl.ds(n * 256, 256)])
-            out_ref[pl.ds(g * 256, 256), pl.ds(n * 128, 128)] = both[:, :128] * 256.0 + both[:, 128:]
+    near = jnp.concatenate([first, (near - first.astype(F32)).astype(BF16)], axis=0)
+    put = []
+    for g in range(2):
+        part = sel[pl.ds(g * 256, 256), :]
+        codes = mm(part, dig[:, pl.ds(2 * BW, 128)])[:, 0:2].astype(I32)
+        scales = []
+        for code in (codes & 255, codes >> 8):
+            power = jnp.exp2(code[:, 0:1].astype(F32) - 128.0).astype(BF16).astype(F32)
+            scales.append(power * (1.0 + code[:, 1:2].astype(F32) * (1.0 / 64.0)))
+        spots = [pl.ds(h * 512 + g * 256, 256) for h in range(2)]
+        for n in range(TILES):
+            cols = pl.ds(n * 128, 128)
+            both = mm(part, dig[:, pl.ds(n * 256, 256)]).astype(I32)
+            hi, lo = both[:, :128], both[:, 128:]
+            values = (((hi & 255) << 8) | (lo & 255), (hi & 0xFF00) | (lo >> 8))
+            for h in range(2):
+                added = mm(hot_near[spots[h], :], near[:, n * 128 : n * 128 + 128])
+                out[spots[h], cols] = (values[h] - 32768).astype(F32) * scales[h] + added
+        for h in range(2):
+            put.append(pltpu.make_async_copy(out.at[spots[h]], out_hbm.at[spots[h]], sems.at[g * 2 + h]))
+            put[-1].start()
+    for copy in put:
+        copy.wait()
 
 
 def place(me, arrived, terms):
@@ -193,13 +211,16 @@
         place_kernel,
         out_shape=jax.ShapeDtypeStruct((ROWS, BW), F32),
         in_specs=[SMEM] + [VMEM] * 4,
-        out_specs=VMEM,
+        out_specs=HBM,
         scratch_shapes=[
-            pltpu.VMEM((ROWS, CAP * 128 + 256), BF16),
-            pltpu.VMEM((CAP * 128 + 256, 2 * BW), BF16),
+            pltpu.VMEM((ROWS, BW), F32),
+            pltpu.VMEM((ROWS // 2, CAP * 128), BF16),
+            pltpu.VMEM((CAP * 128, 2 * BW + 128), BF16),
+            pltpu.VMEM((ROWS, 256), BF16),
+            pltpu.SemaphoreType.DMA((4,)),
         ],
         compiler_params=pltpu.CompilerParams(vmem_limit_bytes=40 * 2**20),
-        cost_estimate=pl.CostEstimate(flops=2 * DEV * CAP * ROWS * 2 * BW, bytes_accessed=4 * 2**20, transcendentals=0),
+        cost_estimate=pl.CostEstimate(flops=DEV * CAP * ROWS * 2 * BW, bytes_accessed=4 * 2**20, transcendentals=0),
         name="place_rows",
     )(me, arrived, *terms)
 
@@ -234,7 +255,7 @@
 STEP = 4
 
 
-def term_kernel(count_ref, mats_ref, targets_ref, own_ref, near_ref, far_ref, out_ref, acc, vecs):
+def term_kernel(count_ref, mats_ref, targets_ref, own_ref, far_ref, near_ref, out_ref, acc, vecs):
     step = pl.program_id(0)
 
     @pl.when(step == 0)
@@ -290,7 +311,7 @@
     cols = (correction_cols, swap_near(correction_cols), swap_far(correction_cols))
     message = pack(leaf_to_panel, potentials)
     own, for_near, for_far, message = fetch(me, cols, density, message)
-    rows = (own, swap_near(for_near), swap_far(for_far))
+    rows = (own, swap_far(for_far), swap_near(for_near))
     arrived = lax.all_to_all(
         message.reshape(DEV, LINES, 1, 128), AXES, split_axis=0, concat_axis=0, tiled=True
     ).reshape(DEV * LINES, 128)

time: 60 us -> 56.5 us (0.942)
  Pallas kernels: 17.6 us -> 15 us
  starting transfers between devices: 25.7 us -> 24.8 us
    pallas_call x1, Pallas kernels: 7.91 us -> 5.82 us  [pack(): pl.pallas_call(pack_kernel, out_shape=jax.ShapeDtypeStruct((DEV * LINES,...]
    ppermute x3, starting transfers between devices: 1.54 us -> 0.37 us  [swap_near(): return lax.ppermute(value, AXES, [(i, i ^ 1) for i in range(DEV)])]
    ppermute x3, starting transfers between devices: 14.1 us -> 14.8 us  [swap_far(): lax.ppermute(value, AXES, [(i, (i - 1 + 2 * (i % 2)) % DEV) for i in rang...]
  transfers between devices with their start and end apart: 7 -> 7, of which waited for: 2 -> 2; matrix products, arithmetic and copies ran while one was open for 0% -> 0% of each run, Pallas kernels for 20% -> 18%
where the time goes in v5:
time: 56.5 us; the launch traced here: 55.5 us
  starting transfers between devices  24.8 us (44%)
  Pallas kernels  15 us (27%)
  waiting for transfers between devices  11.1 us (20%)
  local copies, waits for them, and re-layouts  3.77 us (7%)
  between operations  0.77 us (1%)
    ppermute x3, starting transfers between devices, swap_far(): lax.ppermute(value, AXES, [(i, (i - 1 + 2 * (i % 2)) % DEV) for i in rang...  14.8 us
    all_to_all x1, starting transfers between devices, on_device(): lax.all_to_all(message.reshape(DEV, LINES, 1, 128), AXES, split_axis=0, c...  9.69 us
    ppermute x3, waiting for transfers between devices, swap_far(): lax.ppermute(value, AXES, [(i, (i - 1 + 2 * (i % 2)) % DEV) for i in rang...  9.08 us
    pallas_call x1, Pallas kernels, pack(): pl.pallas_call(pack_kernel, out_shape=jax.ShapeDtypeStruct((DEV * LINES,...  5.82 us
    pallas_call x1, Pallas kernels, place(): pl.pallas_call(place_kernel, out_shape=jax.ShapeDtypeStruct((ROWS, BW), F...  4.8 us
    pallas_call x1, Pallas kernels, make_terms(): pl.pallas_call(term_kernel, grid=(SLOTS // STEP,), out_shape=jax.ShapeDty...  3.98 us
    unnamed x8, local copies, waits for them, and re-layouts  3.69 us
    all_to_all x1, waiting for transfers between devices, on_device(): lax.all_to_all(message.reshape(DEV, LINES, 1, 128), AXES, split_axis=0, c...  2.06 us
  transfers between devices with their start and end apart: 7, of which 2 were waited for; matrix products, arithmetic and copies ran while one was open for 0% of the time, Pallas kernels for 18%

profile of v5, /device:TPU:1, one launch (start us, length us, event | category | flops | bytes accessed | tf_op | source)
XLA Modules:
  0.0 55.5 jit_solution(7549933751525599460)
XLA Ops:
  0.0 7.6 %collective-permute-start.1 = (s32[32]{0:T(128)}, s32[32]{0:T(128)S(1)}, u32[]{:S(2)}, u32[]{:S(2)}) collective-permute-start(s32[32]{0:T(128)} %param.12), channel_id=1, source_target_pairs={{0,127},{1,2},{2,1},{3,4},{4,3},{5,6},{6,5},{7,8},{8,7},{9,10},{10... | collective-permute-start | bytes 392 | tf_op jit(solution)/shard_map/ppermute | solution.py:306
  7.6 0.0 collective-permute-start
  7.6 5.8 %pack_rows.1.msg_ref = s32[3200,128]{1,0:T(8,128)} custom-call(s32[8,128]{1,0:T(8,128)} %bitcast.12, f32[1024,384]{1,0:T(8,128)} %pot_hbm.1), custom_call_target="tpu_custom_call" | custom-call | flops 3221225472 | bytes 4194304 | tf_op jit(solution)/shard_map/pack_rows/pallas_call | solution.py:133
  13.4 0.0 copy-start.3
  13.5 0.0 collective-permute-done.1
  13.5 0.0 collective-permute-done
  13.5 0.0 copy-done
  13.5 0.0 copy-done.1
  13.5 0.4 fetch_density.1
  13.9 1.3 %collective-permute-start.2 = (bf16[32,384]{1,0:T(8,128)(2,1)S(1)}, bf16[32,384]{1,0:T(8,128)(2,1)S(1)}, u32[]{:S(2)}, u32[]{:S(2)}) collective-permute-start(bf16[32,384]{1,0:T(8,128)(2,1)S(1)} %get-tuple-element.11), channel_id=1, source_target_pairs={{0,127},{1,2},{2,1},{3,4},{4,3},{5,6},{6,5},{7,8},{8,7},{9,10},{10... | collective-permute-start | bytes 73736 | tf_op jit(solution)/shard_map/ppermute | solution.py:306
  15.2 0.4 collective-permute-start.3
  16.2 0.1 reshape_tile.3.targets_ref
  16.3 9.7 %all-to-all-start = ((s32[128,25,1,128]{3,2,1,0:T(1,128)}), s32[128,25,1,128]{3,2,1,0:T(1,128)S(1)}, u32[]{:S(2)}, u32[]{:S(2)}) async-start(s32[128,25,1,128]{3,2,1,0:T(1,128)} %bitcast.11), calls=%async_computation | async-start | bytes 3276800 | tf_op jit(solution)/shard_map/all_to_all | solution.py:315
  26.0 0.0 collective-permute-done.2.far_ref
  26.0 0.0 collective-permute-done.3.near_ref
  26.0 0.0 copy-start.2
  26.0 3.7 %copy-done.2 = bf16[32,384,384]{2,1,0:T(8,128)(2,1)S(1)} copy-done((bf16[32,384,384]{2,1,0:T(8,128)(2,1)S(1)}, bf16[32,384,384]{2,1,0:T(8,128)(2,1)}, u32[]{:S(2)}) %copy-start.2) | copy-done | bytes 9437208
  29.7 4.0 %near_terms.1.own_ref = f32[40,384]{1,0:T(8,128)S(1)} custom-call(s32[1]{0:T(128)S(6)} %copy.11.count_ref, bf16[32,384,384]{2,1,0:T(8,128)(2,1)S(1)} %copy-done.2, s32[1,128]{1,0:T(1,128)S(1)} %reshape_tile.3.targets_ref, bf16[32,384]{1,0:T(8,128)(2,1)S(1)} %get-tuple-element.10.own_ref, bf16[32,384]{1,0:T(8,128)(2,1)S(1)} %collective-permute-done.2.far_ref, ...), custom_call_target="tpu_custom_call" | custom-call | flops 60000002048 | bytes 9437184 | tf_op jit(solution)/shard_map/near_terms/pallas_call | solution.py:288
  33.7 5.9 %collective-permute-start.5 = (f32[40,384]{1,0:T(8,128)S(1)}, f32[40,384]{1,0:T(8,128)S(1)}, u32[]{:S(2)}, u32[]{:S(2)}) collective-permute-start(f32[40,384]{1,0:T(8,128)S(1)} %near_terms.1.own_ref), channel_id=1, source_target_pairs={{0,127},{1,2},{2,1},{3,4},{4,3},{5,6},{6,5},{7,8},{8,7},{9,10},{10... | collective-permute-start | bytes 184328 | tf_op jit(solution)/shard_map/ppermute | solution.py:306
  39.6 0.0 collective-permute-start.4
  39.6 9.1 %collective-permute-done.5.far_ref = f32[40,384]{1,0:T(8,128)S(1)} collective-permute-done((f32[40,384]{1,0:T(8,128)S(1)}, f32[40,384]{1,0:T(8,128)S(1)}, u32[]{:S(2)}, u32[]{:S(2)}) %collective-permute-start.5) | collective-permute-done | bytes 61472 | tf_op jit(solution)/shard_map/ppermute | solution.py:306
  48.7 0.0 collective-permute-done.4.near_ref
  48.7 2.1 %all-to-all-done = s32[128,25,1,128]{3,2,1,0:T(1,128)S(1)} async-done(((s32[128,25,1,128]{3,2,1,0:T(1,128)}), s32[128,25,1,128]{3,2,1,0:T(1,128)S(1)}, u32[]{:S(2)}, u32[]{:S(2)}) %all-to-all-start) | async-done | bytes 1638432 | tf_op jit(solution)/shard_map/all_to_all | solution.py:315
  50.7 4.8 %place_rows.1 = f32[1024,384]{1,0:T(8,128)} custom-call(s32[1]{0:T(128)} %bitcast.me_ref, s32[3200,128]{1,0:T(8,128)S(1)} %bitcast.7, f32[40,384]{1,0:T(8,128)S(1)} %near_terms.1.own_ref, f32[40,384]{1,0:T(8,128)S(1)} %collective-permute-done.4.near_ref, f32[40,384]{1,0:T(8,128)S(1)} %collective-permute-done.5.far_ref), custom_call_target="tpu_custom_call" | custom-call | flops 1610612736 | bytes 4194304 | tf_op jit(solution)/shard_map/place_rows/pallas_call | solution.py:210
  (4 shorter events, 0.0 us)
Async XLA Ops:
  0.0 13.5 %collective-permute-start.1 = (s32[32]{0:T(128)}, s32[32]{0:T(128)S(1)}, u32[]{:S(2)}, u32[]{:S(2)}) collective-permute-start(s32[32]{0:T(128)} %param.12), channel_id=1, source_target_pairs={{0,127},{1,2},{2,1},{3,4},{4,3},{5,6},{6,5},{7,8},{8,7},{9,10},{10... | collective-permute-start | bytes 392 | tf_op jit(solution)/shard_map/ppermute | solution.py:306
  7.6 5.9 %collective-permute-start = (s32[32]{0:T(128)}, s32[32]{0:T(128)S(1)}, u32[]{:S(2)}, u32[]{:S(2)}) collective-permute-start(s32[32]{0:T(128)} %param.12), channel_id=1, source_target_pairs={{0,1},{1,0},{2,3},{3,2},{4,5},{5,4},{6,7},{7,6},{8,9},{9,8},{10,11... | collective-permute-start | bytes 392 | tf_op jit(solution)/shard_map/ppermute | solution.py:302
  7.6 5.9 %copy-start = (bf16[1024,384]{1,0:T(8,128)(2,1)S(1)}, bf16[1024,384]{1,0:T(8,128)(2,1)}, u32[]{:S(2)}) copy-start(bf16[1024,384]{1,0:T(8,128)(2,1)} %density_ref.1) | copy-start | bytes 2359300
  7.6 5.9 %copy-start.1 = (s32[32]{0:T(128)S(1)}, s32[32]{0:T(128)}, u32[]{:S(2)}) copy-start(s32[32]{0:T(128)} %param.12) | copy-start | bytes 388
  13.4 2.8 %copy-start.3 = (s32[32]{0:T(128)S(1)}, s32[32]{0:T(128)}, u32[]{:S(2)}) copy-start(s32[32]{0:T(128)} %param.11) | copy-start | bytes 388
  13.9 12.1 %collective-permute-start.2 = (bf16[32,384]{1,0:T(8,128)(2,1)S(1)}, bf16[32,384]{1,0:T(8,128)(2,1)S(1)}, u32[]{:S(2)}, u32[]{:S(2)}) collective-permute-start(bf16[32,384]{1,0:T(8,128)(2,1)S(1)} %get-tuple-element.11), channel_id=1, source_target_pairs={{0,127},{1,2},{2,1},{3,4},{4,3},{5,6},{6,5},{7,8},{8,7},{9,10},{10... | collective-permute-start | bytes 73736 | tf_op jit(solution)/shard_map/ppermute | solution.py:306
  15.2 10.8 %collective-permute-start.3 = (bf16[32,384]{1,0:T(8,128)(2,1)S(1)}, bf16[32,384]{1,0:T(8,128)(2,1)S(1)}, u32[]{:S(2)}, u32[]{:S(2)}) collective-permute-start(bf16[32,384]{1,0:T(8,128)(2,1)S(1)} %get-tuple-element.12), channel_id=1, source_target_pairs={{0,1},{1,0},{2,3},{3,2},{4,5},{5,4},{6,7},{7,6},{8,9},{9,8},{10,11... | collective-permute-start | bytes 73736 | tf_op jit(solution)/shard_map/ppermute | solution.py:302
  16.3 34.4 %all-to-all-start = ((s32[128,25,1,128]{3,2,1,0:T(1,128)}), s32[128,25,1,128]{3,2,1,0:T(1,128)S(1)}, u32[]{:S(2)}, u32[]{:S(2)}) async-start(s32[128,25,1,128]{3,2,1,0:T(1,128)} %bitcast.11), calls=%async_computation | async-start | bytes 3276800 | tf_op jit(solution)/shard_map/all_to_all | solution.py:315
  26.0 3.7 %copy-start.2 = (bf16[32,384,384]{2,1,0:T(8,128)(2,1)S(1)}, bf16[32,384,384]{2,1,0:T(8,128)(2,1)}, u32[]{:S(2)}) copy-start(bf16[32,384,384]{2,1,0:T(8,128)(2,1)} %mats_ref.1) | copy-start | bytes 28311556
  33.7 15.0 %collective-permute-start.5 = (f32[40,384]{1,0:T(8,128)S(1)}, f32[40,384]{1,0:T(8,128)S(1)}, u32[]{:S(2)}, u32[]{:S(2)}) collective-permute-start(f32[40,384]{1,0:T(8,128)S(1)} %near_terms.1.own_ref), channel_id=1, source_target_pairs={{0,127},{1,2},{2,1},{3,4},{4,3},{5,6},{6,5},{7,8},{8,7},{9,10},{10... | collective-permute-start | bytes 184328 | tf_op jit(solution)/shard_map/ppermute | solution.py:306
  39.6 9.1 %collective-permute-start.4 = (f32[40,384]{1,0:T(8,128)S(1)}, f32[40,384]{1,0:T(8,128)S(1)}, u32[]{:S(2)}, u32[]{:S(2)}) collective-permute-start(f32[40,384]{1,0:T(8,128)S(1)} %near_terms.1.own_ref), channel_id=1, source_target_pairs={{0,1},{1,0},{2,3},{3,2},{4,5},{5,4},{6,7},{7,6},{8,9},{9,8},{10,11... | collective-permute-start | bytes 184328 | tf_op jit(solution)/shard_map/ppermute | solution.py:302

commit v6 on v5

--- a/solution.py
+++ b/solution.py
@@ -292,7 +292,7 @@
         in_specs=[SMEM, pl.BlockSpec((STEP, BW, BW), lambda i: (i, 0, 0)), whole(1, 128)] + [whole(SLOTS, BW)] * 3,
         out_specs=whole(SLOTS + 8, BW),
         scratch_shapes=[pltpu.VMEM((BW, 128), F32), pltpu.VMEM((128, BW), BF16)],
-        compiler_params=pltpu.CompilerParams(vmem_limit_bytes=20 * 2**20),
+        compiler_params=pltpu.CompilerParams(vmem_limit_bytes=46 * 2**20),
         cost_estimate=pl.CostEstimate(flops=6 * 10**10, bytes_accessed=SLOTS * BW * BW * 2, transcendentals=0),
         name="near_terms",
     )(count, mats, targets, *rows)

time: 56.5 us -> 56.6 us (level)
  Pallas kernels: 15 us -> 18.9 us
  local copies, waits for them, and re-layouts: 3.77 us -> 0.1 us
    pallas_call x1, Pallas kernels: 3.98 us -> 7.88 us  [make_terms(): pl.pallas_call(term_kernel, grid=(SLOTS // STEP,), out_shape=jax.ShapeDty...]
    unnamed x8 -> x6, local copies, waits for them, and re-layouts: 3.69 us -> 0.01 us
  transfers between devices with their start and end apart: 7 -> 7, of which waited for: 2 -> 2; matrix products, arithmetic and copies ran while one was open for 0% -> 0% of each run, Pallas kernels for 18% -> 25%
where the time goes in v6:
time: 56.6 us; the launch traced here: 55.5 us
  starting transfers between devices  24.8 us (44%)
  Pallas kernels  18.9 us (33%)
  waiting for transfers between devices  10.9 us (19%)
  between operations  0.77 us (1%)
    ppermute x3, starting transfers between devices, swap_far(): lax.ppermute(value, AXES, [(i, (i - 1 + 2 * (i % 2)) % DEV) for i in rang...  14.8 us
    all_to_all x1, starting transfers between devices, on_device(): lax.all_to_all(message.reshape(DEV, LINES, 1, 128), AXES, split_axis=0, c...  9.69 us
    ppermute x3, waiting for transfers between devices, swap_far(): lax.ppermute(value, AXES, [(i, (i - 1 + 2 * (i % 2)) % DEV) for i in rang...  8.82 us
    pallas_call x1, Pallas kernels, make_terms(): pl.pallas_call(term_kernel, grid=(SLOTS // STEP,), out_shape=jax.ShapeDty...  7.88 us
    pallas_call x1, Pallas kernels, pack(): pl.pallas_call(pack_kernel, out_shape=jax.ShapeDtypeStruct((DEV * LINES,...  5.82 us
    pallas_call x1, Pallas kernels, place(): pl.pallas_call(place_kernel, out_shape=jax.ShapeDtypeStruct((ROWS, BW), F...  4.8 us
    all_to_all x1, waiting for transfers between devices, on_device(): lax.all_to_all(message.reshape(DEV, LINES, 1, 128), AXES, split_axis=0, c...  2.1 us
  transfers between devices with their start and end apart: 7, of which 2 were waited for; matrix products, arithmetic and copies ran while one was open for 0% of the time, Pallas kernels for 25%

profile of v6, /device:TPU:1, one launch (start us, length us, event | category | flops | bytes accessed | tf_op | source)
XLA Modules:
  0.0 55.5 jit_solution(14113330277482515516)
XLA Ops:
  0.0 7.6 %collective-permute-start.1 = (s32[32]{0:T(128)}, s32[32]{0:T(128)S(1)}, u32[]{:S(2)}, u32[]{:S(2)}) collective-permute-start(s32[32]{0:T(128)} %param.12), channel_id=1, source_target_pairs={{0,127},{1,2},{2,1},{3,4},{4,3},{5,6},{6,5},{7,8},{8,7},{9,10},{10... | collective-permute-start | bytes 392 | tf_op jit(solution)/shard_map/ppermute | solution.py:306
  7.6 0.0 collective-permute-start
  7.6 0.0 copy-start
  7.6 5.8 %pack_rows.1.msg_ref = s32[3200,128]{1,0:T(8,128)} custom-call(s32[8,128]{1,0:T(8,128)} %bitcast.12, f32[1024,384]{1,0:T(8,128)} %pot_hbm.1), custom_call_target="tpu_custom_call" | custom-call | flops 3221225472 | bytes 4194304 | tf_op jit(solution)/shard_map/pack_rows/pallas_call | solution.py:133
  13.4 0.0 copy-start.2
  13.5 0.0 collective-permute-done.1
  13.5 0.0 collective-permute-done
  13.5 0.0 copy-done
  13.5 0.0 copy-done.1
  13.5 0.4 fetch_density.1
  13.9 1.3 %collective-permute-start.2 = (bf16[32,384]{1,0:T(8,128)(2,1)S(1)}, bf16[32,384]{1,0:T(8,128)(2,1)S(1)}, u32[]{:S(2)}, u32[]{:S(2)}) collective-permute-start(bf16[32,384]{1,0:T(8,128)(2,1)S(1)} %get-tuple-element.11), channel_id=1, source_target_pairs={{0,127},{1,2},{2,1},{3,4},{4,3},{5,6},{6,5},{7,8},{8,7},{9,10},{10... | collective-permute-start | bytes 73736 | tf_op jit(solution)/shard_map/ppermute | solution.py:306
  15.2 0.4 collective-permute-start.3
  16.2 0.0 copy-done.2
  16.2 0.1 reshape_tile.3.targets_ref
  16.3 9.7 %all-to-all-start = ((s32[128,25,1,128]{3,2,1,0:T(1,128)}), s32[128,25,1,128]{3,2,1,0:T(1,128)S(1)}, u32[]{:S(2)}, u32[]{:S(2)}) async-start(s32[128,25,1,128]{3,2,1,0:T(1,128)} %bitcast.11), calls=%async_computation | async-start | bytes 3276800 | tf_op jit(solution)/shard_map/all_to_all | solution.py:315
  26.0 0.0 collective-permute-done.2.far_ref
  26.0 0.0 collective-permute-done.3.near_ref
  26.0 7.9 %near_terms.1.own_ref = f32[40,384]{1,0:T(8,128)S(1)} custom-call(s32[1]{0:T(128)S(6)} %copy.11.count_ref, bf16[32,384,384]{2,1,0:T(8,128)(2,1)} %mats_ref.1, s32[1,128]{1,0:T(1,128)S(1)} %reshape_tile.3.targets_ref, bf16[32,384]{1,0:T(8,128)(2,1)S(1)} %get-tuple-element.10.own_ref, bf16[32,384]{1,0:T(8,128)(2,1)S(1)} %collective-permute-done.2.far_ref, ...), custom_call_target="tpu_custom_call" | custom-call | flops 60000002048 | bytes 9437184 | tf_op jit(solution)/shard_map/near_terms/pallas_call | solution.py:288
  33.9 5.9 %collective-permute-start.5 = (f32[40,384]{1,0:T(8,128)S(1)}, f32[40,384]{1,0:T(8,128)S(1)}, u32[]{:S(2)}, u32[]{:S(2)}) collective-permute-start(f32[40,384]{1,0:T(8,128)S(1)} %near_terms.1.own_ref), channel_id=1, source_target_pairs={{0,127},{1,2},{2,1},{3,4},{4,3},{5,6},{6,5},{7,8},{8,7},{9,10},{10... | collective-permute-start | bytes 184328 | tf_op jit(solution)/shard_map/ppermute | solution.py:306
  39.8 0.0 collective-permute-start.4
  39.8 8.8 %collective-permute-done.5.far_ref = f32[40,384]{1,0:T(8,128)S(1)} collective-permute-done((f32[40,384]{1,0:T(8,128)S(1)}, f32[40,384]{1,0:T(8,128)S(1)}, u32[]{:S(2)}, u32[]{:S(2)}) %collective-permute-start.5) | collective-permute-done | bytes 61472 | tf_op jit(solution)/shard_map/ppermute | solution.py:306
  48.6 0.0 collective-permute-done.4.near_ref
  48.6 2.1 %all-to-all-done = s32[128,25,1,128]{3,2,1,0:T(1,128)S(1)} async-done(((s32[128,25,1,128]{3,2,1,0:T(1,128)}), s32[128,25,1,128]{3,2,1,0:T(1,128)S(1)}, u32[]{:S(2)}, u32[]{:S(2)}) %all-to-all-start) | async-done | bytes 1638432 | tf_op jit(solution)/shard_map/all_to_all | solution.py:315
  50.7 4.8 %place_rows.1 = f32[1024,384]{1,0:T(8,128)} custom-call(s32[1]{0:T(128)} %bitcast.me_ref, s32[3200,128]{1,0:T(8,128)S(1)} %bitcast.7, f32[40,384]{1,0:T(8,128)S(1)} %near_terms.1.own_ref, f32[40,384]{1,0:T(8,128)S(1)} %collective-permute-done.4.near_ref, f32[40,384]{1,0:T(8,128)S(1)} %collective-permute-done.5.far_ref), custom_call_target="tpu_custom_call" | custom-call | flops 1610612736 | bytes 4194304 | tf_op jit(solution)/shard_map/place_rows/pallas_call | solution.py:210
  (2 shorter events, 0.0 us)
Async XLA Ops:
  0.0 13.5 %collective-permute-start.1 = (s32[32]{0:T(128)}, s32[32]{0:T(128)S(1)}, u32[]{:S(2)}, u32[]{:S(2)}) collective-permute-start(s32[32]{0:T(128)} %param.12), channel_id=1, source_target_pairs={{0,127},{1,2},{2,1},{3,4},{4,3},{5,6},{6,5},{7,8},{8,7},{9,10},{10... | collective-permute-start | bytes 392 | tf_op jit(solution)/shard_map/ppermute | solution.py:306
  7.6 5.9 %collective-permute-start = (s32[32]{0:T(128)}, s32[32]{0:T(128)S(1)}, u32[]{:S(2)}, u32[]{:S(2)}) collective-permute-start(s32[32]{0:T(128)} %param.12), channel_id=1, source_target_pairs={{0,1},{1,0},{2,3},{3,2},{4,5},{5,4},{6,7},{7,6},{8,9},{9,8},{10,11... | collective-permute-start | bytes 392 | tf_op jit(solution)/shard_map/ppermute | solution.py:302
  7.6 5.9 %copy-start = (bf16[1024,384]{1,0:T(8,128)(2,1)S(1)}, bf16[1024,384]{1,0:T(8,128)(2,1)}, u32[]{:S(2)}) copy-start(bf16[1024,384]{1,0:T(8,128)(2,1)} %density_ref.1) | copy-start | bytes 2359300
  7.6 5.9 %copy-start.1 = (s32[32]{0:T(128)S(1)}, s32[32]{0:T(128)}, u32[]{:S(2)}) copy-start(s32[32]{0:T(128)} %param.12) | copy-start | bytes 388
  13.4 2.8 %copy-start.2 = (s32[32]{0:T(128)S(1)}, s32[32]{0:T(128)}, u32[]{:S(2)}) copy-start(s32[32]{0:T(128)} %param.11) | copy-start | bytes 388
  13.9 12.1 %collective-permute-start.2 = (bf16[32,384]{1,0:T(8,128)(2,1)S(1)}, bf16[32,384]{1,0:T(8,128)(2,1)S(1)}, u32[]{:S(2)}, u32[]{:S(2)}) collective-permute-start(bf16[32,384]{1,0:T(8,128)(2,1)S(1)} %get-tuple-element.11), channel_id=1, source_target_pairs={{0,127},{1,2},{2,1},{3,4},{4,3},{5,6},{6,5},{7,8},{8,7},{9,10},{10... | collective-permute-start | bytes 73736 | tf_op jit(solution)/shard_map/ppermute | solution.py:306
  15.2 10.8 %collective-permute-start.3 = (bf16[32,384]{1,0:T(8,128)(2,1)S(1)}, bf16[32,384]{1,0:T(8,128)(2,1)S(1)}, u32[]{:S(2)}, u32[]{:S(2)}) collective-permute-start(bf16[32,384]{1,0:T(8,128)(2,1)S(1)} %get-tuple-element.12), channel_id=1, source_target_pairs={{0,1},{1,0},{2,3},{3,2},{4,5},{5,4},{6,7},{7,6},{8,9},{9,8},{10,11... | collective-permute-start | bytes 73736 | tf_op jit(solution)/shard_map/ppermute | solution.py:302
  16.3 34.4 %all-to-all-start = ((s32[128,25,1,128]{3,2,1,0:T(1,128)}), s32[128,25,1,128]{3,2,1,0:T(1,128)S(1)}, u32[]{:S(2)}, u32[]{:S(2)}) async-start(s32[128,25,1,128]{3,2,1,0:T(1,128)} %bitcast.11), calls=%async_computation | async-start | bytes 3276800 | tf_op jit(solution)/shard_map/all_to_all | solution.py:315
  33.9 14.7 %collective-permute-start.5 = (f32[40,384]{1,0:T(8,128)S(1)}, f32[40,384]{1,0:T(8,128)S(1)}, u32[]{:S(2)}, u32[]{:S(2)}) collective-permute-start(f32[40,384]{1,0:T(8,128)S(1)} %near_terms.1.own_ref), channel_id=1, source_target_pairs={{0,127},{1,2},{2,1},{3,4},{4,3},{5,6},{6,5},{7,8},{8,7},{9,10},{10... | collective-permute-start | bytes 184328 | tf_op jit(solution)/shard_map/ppermute | solution.py:306
  39.8 8.8 %collective-permute-start.4 = (f32[40,384]{1,0:T(8,128)S(1)}, f32[40,384]{1,0:T(8,128)S(1)}, u32[]{:S(2)}, u32[]{:S(2)}) collective-permute-start(f32[40,384]{1,0:T(8,128)S(1)} %near_terms.1.own_ref), channel_id=1, source_target_pairs={{0,1},{1,0},{2,3},{3,2},{4,5},{5,4},{6,7},{7,6},{8,9},{9,8},{10,11... | collective-permute-start | bytes 184328 | tf_op jit(solution)/shard_map/ppermute | solution.py:302

commit v7 on v5

--- a/solution.py
+++ b/solution.py
@@ -255,13 +255,19 @@
 STEP = 4
 
 
-def term_kernel(count_ref, mats_ref, targets_ref, own_ref, far_ref, near_ref, out_ref, acc, vecs):
+def term_kernel(me_ref, count_ref, mats_ref, sources_ref, targets_ref, own_ref, far_ref, near_ref, block_ref, out_ref, acc, vecs):
     step = pl.program_id(0)
 
     @pl.when(step == 0)
     def _():
         acc[...] = jnp.zeros_like(acc)
         got = own_ref[...].astype(F32) + near_ref[...].astype(F32) + far_ref[...].astype(F32)
+        other = (me_ref[0] - 1 + 2 * (me_ref[0] & 1)) & (DEV - 1)
+        at = ((sources_ref[...] - other * ROWS) & (TOTAL - 1)).astype(F32)
+        at = jnp.transpose(jnp.broadcast_to(at, (128, 128)))[0:SLOTS].astype(I32)
+        spot = iota((SLOTS, 128), 1)
+        hot = jnp.concatenate([one_hot(at - b * 128 == spot) for b in range(8)], axis=1)
+        got = got + mm(hot, block_ref[...])
         vecs[...] = jnp.concatenate([got, jnp.zeros((128 - SLOTS, BW), F32)], axis=0).astype(BF16)
 
     lane = iota((BW, 128), 1)
@@ -281,7 +287,7 @@
             out_ref[SLOTS : SLOTS + 8, n * 128 : n * 128 + 128] = jnp.broadcast_to(rows, (8, 128))
 
 
-def make_terms(count, mats, targets, rows):
+def make_terms(me, count, mats, sources, targets, rows, block):
     def whole(rows, width):
         return pl.BlockSpec((rows, width), lambda i: (0, 0))
 
@@ -289,35 +295,52 @@
         term_kernel,
         grid=(SLOTS // STEP,),
         out_shape=jax.ShapeDtypeStruct((SLOTS + 8, BW), F32),
-        in_specs=[SMEM, pl.BlockSpec((STEP, BW, BW), lambda i: (i, 0, 0)), whole(1, 128)] + [whole(SLOTS, BW)] * 3,
+        in_specs=[SMEM, SMEM, pl.BlockSpec((STEP, BW, BW), lambda i: (i, 0, 0))]
+        + [whole(1, 128)] * 2
+        + [whole(SLOTS, BW)] * 3
+        + [whole(ROWS, BW)],
         out_specs=whole(SLOTS + 8, BW),
         scratch_shapes=[pltpu.VMEM((BW, 128), F32), pltpu.VMEM((128, BW), BF16)],
         compiler_params=pltpu.CompilerParams(vmem_limit_bytes=20 * 2**20),
         cost_estimate=pl.CostEstimate(flops=6 * 10**10, bytes_accessed=SLOTS * BW * BW * 2, transcendentals=0),
         name="near_terms",
-    )(count, mats, targets, *rows)
+    )(me, count, mats, sources, targets, *rows, block)
 
 
 def swap_near(value):
     return lax.ppermute(value, AXES, [(i, i ^ 1) for i in range(DEV)])
 
 
+FAR = [(i, (i - 1 + 2 * (i % 2)) % DEV) for i in range(DEV)]
+
+
 def swap_far(value):
-    return lax.ppermute(value, AXES, [(i, (i - 1 + 2 * (i % 2)) % DEV) for i in range(DEV)])
+    return lax.ppermute(value, AXES, FAR)
+
+
+def swap_inner(value):
+    size = lax.axis_size("panel")
+    return lax.ppermute(value, AXES, [(i, j) for i, j in FAR if i // size == j // size])
+
+
+def swap_cross(value):
+    size = lax.axis_size("panel")
+    return lax.ppermute(value, AXES, [(i, j) for i, j in FAR if i // size != j // size])
 
 
 def on_device(potentials, leaf_to_panel, density, corrections, correction_rows, correction_cols, block_count):
     me = lax.axis_index(AXES).astype(I32).reshape(1)
-    cols = (correction_cols, swap_near(correction_cols), swap_far(correction_cols))
+    block = swap_cross(density)
+    cols = (correction_cols, swap_near(correction_cols), swap_inner(correction_cols))
     message = pack(leaf_to_panel, potentials)
     own, for_near, for_far, message = fetch(me, cols, density, message)
-    rows = (own, swap_far(for_far), swap_near(for_near))
+    rows = (own, swap_inner(for_far), swap_near(for_near))
     arrived = lax.all_to_all(
         message.reshape(DEV, LINES, 1, 128), AXES, split_axis=0, concat_axis=0, tiled=True
     ).reshape(DEV * LINES, 128)
-    targets = jnp.tile(correction_rows, 128 // SLOTS).reshape(1, 128)
-    term = make_terms(block_count, corrections, targets, rows)
-    terms = (term, swap_near(term), swap_far(term))
+    sources, targets = (jnp.tile(x, 128 // SLOTS).reshape(1, 128) for x in (correction_cols, correction_rows))
+    term = make_terms(me, block_count, corrections, sources, targets, rows, block)
+    terms = (term, swap_far(term), swap_near(term))
     return place(me, arrived, terms)
 
 

time: 56.5 us -> 60.9 us (1.078)
  starting transfers between devices: 24.8 us -> 29 us
    ppermute x3, starting transfers between devices: 0.37 us -> 5.57 us  [swap_near(): return lax.ppermute(value, AXES, [(i, i ^ 1) for i in range(DEV)])]
    all_to_all x1, starting transfers between devices: 9.69 us -> 6.59 us  [on_device(): lax.all_to_all(message.reshape(DEV, LINES, 1, 128), AXES, split_axis=0, c...]
    ppermute x3 -> x4, starting transfers between devices: 14.8 us -> 16.9 us  [the longest x1 9.49 us: swap_cross(): lax.ppermute(value, AXES, [(i, j) for i, j in FAR if i // size != j // si...]
    ppermute x3 -> x4, waiting for transfers between devices: 9.08 us -> 8.74 us  [the longest x1 8.74 us: swap_far(): return lax.ppermute(value, AXES, FAR)]
  transfers between devices with their start and end apart: 7 -> 8, of which waited for: 2 -> 2; matrix products, arithmetic and copies ran while one was open for 0% -> 0% of each run, Pallas kernels for 18% -> 18%
where the time goes in v7:
time: 60.9 us; the launch traced here: 59.8 us
  starting transfers between devices  29 us (48%)
  Pallas kernels  15.3 us (25%)
  waiting for transfers between devices  10.9 us (18%)
  local copies, waits for them, and re-layouts  3.86 us (6%)
  between operations  0.82 us (1%)
    ppermute x1, starting transfers between devices, swap_cross(): lax.ppermute(value, AXES, [(i, j) for i, j in FAR if i // size != j // si...  9.49 us
    ppermute x1, waiting for transfers between devices, swap_far(): return lax.ppermute(value, AXES, FAR)  8.74 us
    all_to_all x1, starting transfers between devices, on_device(): lax.all_to_all(message.reshape(DEV, LINES, 1, 128), AXES, split_axis=0, c...  6.59 us
    ppermute x1, starting transfers between devices, swap_far(): return lax.ppermute(value, AXES, FAR)  6.03 us
    pallas_call x1, Pallas kernels, pack(): pl.pallas_call(pack_kernel, out_shape=jax.ShapeDtypeStruct((DEV * LINES,...  5.82 us
    ppermute x3, starting transfers between devices, swap_near(): return lax.ppermute(value, AXES, [(i, i ^ 1) for i in range(DEV)])  5.57 us
    pallas_call x1, Pallas kernels, place(): pl.pallas_call(place_kernel, out_shape=jax.ShapeDtypeStruct((ROWS, BW), F...  4.79 us
    pallas_call x1, Pallas kernels, make_terms(): pl.pallas_call(term_kernel, grid=(SLOTS // STEP,), out_shape=jax.ShapeDty...  4.25 us
  transfers between devices with their start and end apart: 8, of which 2 were waited for; matrix products, arithmetic and copies ran while one was open for 0% of the time, Pallas kernels for 18%

profile of v7, /device:TPU:1, one launch (start us, length us, event | category | flops | bytes accessed | tf_op | source)
XLA Modules:
  0.0 59.8 jit_solution(13876902213664398346)
XLA Ops:
  0.0 9.5 %collective-permute-start.4 = (bf16[1024,384]{1,0:T(8,128)(2,1)}, bf16[1024,384]{1,0:T(8,128)(2,1)S(1)}, u32[]{:S(2)}, u32[]{:S(2)}) collective-permute-start(bf16[1024,384]{1,0:T(8,128)(2,1)} %density_ref.1), channel_id=1, source_target_pairs={{0,127},{15,16},{16,15},{31,32},{32,31},{47,48},{48,47},{63,64},{6... | collective-permute-start | bytes 2359304 | tf_op jit(solution)/shard_map/ppermute | solution.py:328
  9.5 0.1 collective-permute-start
  9.6 0.7 %collective-permute-start.1 = (s32[32]{0:T(128)}, s32[32]{0:T(128)S(1)}, u32[]{:S(2)}, u32[]{:S(2)}) collective-permute-start(s32[32]{0:T(128)} %param.12), channel_id=1, source_target_pairs={{1,2},{2,1},{3,4},{4,3},{5,6},{6,5},{7,8},{8,7},{9,10},{10,9},{11,... | collective-permute-start | bytes 392 | tf_op jit(solution)/shard_map/ppermute | solution.py:323
  10.3 5.8 %pack_rows.1.msg_ref = s32[3200,128]{1,0:T(8,128)} custom-call(s32[8,128]{1,0:T(8,128)} %bitcast.12, f32[1024,384]{1,0:T(8,128)} %pot_hbm.1), custom_call_target="tpu_custom_call" | custom-call | flops 3221225472 | bytes 4194304 | tf_op jit(solution)/shard_map/pack_rows/pallas_call | solution.py:133
  16.1 0.0 copy-start.3
  16.1 0.0 collective-permute-done
  16.1 0.0 collective-permute-done.1
  16.2 0.4 fetch_density.1
  16.6 0.7 %collective-permute-start.2 = (bf16[32,384]{1,0:T(8,128)(2,1)S(1)}, bf16[32,384]{1,0:T(8,128)(2,1)S(1)}, u32[]{:S(2)}, u32[]{:S(2)}) collective-permute-start(bf16[32,384]{1,0:T(8,128)(2,1)S(1)} %get-tuple-element.11), channel_id=1, source_target_pairs={{1,2},{2,1},{3,4},{4,3},{5,6},{6,5},{7,8},{8,7},{9,10},{10,9},{11,... | collective-permute-start | bytes 73736 | tf_op jit(solution)/shard_map/ppermute | solution.py:323
  17.3 5.5 %collective-permute-start.3 = (bf16[32,384]{1,0:T(8,128)(2,1)S(1)}, bf16[32,384]{1,0:T(8,128)(2,1)S(1)}, u32[]{:S(2)}, u32[]{:S(2)}) collective-permute-start(bf16[32,384]{1,0:T(8,128)(2,1)S(1)} %get-tuple-element.12), channel_id=1, source_target_pairs={{0,1},{1,0},{2,3},{3,2},{4,5},{5,4},{6,7},{7,6},{8,9},{9,8},{10,11... | collective-permute-start | bytes 73736 | tf_op jit(solution)/shard_map/ppermute | solution.py:311
  23.4 0.1 reshape_tile.6.sources_ref
  23.5 0.1 reshape_tile.7.targets_ref
  23.6 6.6 %all-to-all-start = ((s32[128,25,1,128]{3,2,1,0:T(1,128)}), s32[128,25,1,128]{3,2,1,0:T(1,128)S(1)}, u32[]{:S(2)}, u32[]{:S(2)}) async-start(s32[128,25,1,128]{3,2,1,0:T(1,128)} %bitcast.11), calls=%async_computation | async-start | bytes 3276800 | tf_op jit(solution)/shard_map/all_to_all | solution.py:338
  30.2 0.0 collective-permute-done.2.far_ref
  30.2 0.0 collective-permute-done.3.near_ref
  30.2 0.0 collective-permute-done.4.block_ref
  30.2 0.0 copy-start.2
  30.2 3.7 %copy-done.2 = bf16[32,384,384]{2,1,0:T(8,128)(2,1)S(1)} copy-done((bf16[32,384,384]{2,1,0:T(8,128)(2,1)S(1)}, bf16[32,384,384]{2,1,0:T(8,128)(2,1)}, u32[]{:S(2)}) %copy-start.2) | copy-done | bytes 9437208
  33.9 4.3 %near_terms.1.own_ref = f32[40,384]{1,0:T(8,128)S(1)} custom-call(s32[1]{0:T(128)} %bitcast.me_ref, s32[1]{0:T(128)S(6)} %copy.11.count_ref, bf16[32,384,384]{2,1,0:T(8,128)(2,1)S(1)} %copy-done.2, s32[1,128]{1,0:T(1,128)S(1)} %reshape_tile.6.sources_ref, s32[1,128]{1,0:T(1,128)S(1)} %reshape_tile.7.targets_ref, ...), custom_call_target="tpu_custom_call" | custom-call | flops 60000002048 | bytes 9437184 | tf_op jit(solution)/shard_map/near_terms/pallas_call | solution.py:294
  38.1 6.0 %collective-permute-start.5 = (f32[40,384]{1,0:T(8,128)S(1)}, f32[40,384]{1,0:T(8,128)S(1)}, u32[]{:S(2)}, u32[]{:S(2)}) collective-permute-start(f32[40,384]{1,0:T(8,128)S(1)} %near_terms.1.own_ref), channel_id=1, source_target_pairs={{0,127},{1,2},{2,1},{3,4},{4,3},{5,6},{6,5},{7,8},{8,7},{9,10},{10... | collective-permute-start | bytes 184328 | tf_op jit(solution)/shard_map/ppermute | solution.py:318
  44.2 0.0 collective-permute-start.6
  44.2 8.7 %collective-permute-done.5.near_ref = f32[40,384]{1,0:T(8,128)S(1)} collective-permute-done((f32[40,384]{1,0:T(8,128)S(1)}, f32[40,384]{1,0:T(8,128)S(1)}, u32[]{:S(2)}, u32[]{:S(2)}) %collective-permute-start.5) | collective-permute-done | bytes 61472 | tf_op jit(solution)/shard_map/ppermute | solution.py:318
  52.9 2.1 %all-to-all-done = s32[128,25,1,128]{3,2,1,0:T(1,128)S(1)} async-done(((s32[128,25,1,128]{3,2,1,0:T(1,128)}), s32[128,25,1,128]{3,2,1,0:T(1,128)S(1)}, u32[]{:S(2)}, u32[]{:S(2)}) %all-to-all-start) | async-done | bytes 1638432 | tf_op jit(solution)/shard_map/all_to_all | solution.py:338
  55.0 4.8 %place_rows.1 = f32[1024,384]{1,0:T(8,128)} custom-call(s32[1]{0:T(128)} %bitcast.me_ref, s32[3200,128]{1,0:T(8,128)S(1)} %bitcast.7, f32[40,384]{1,0:T(8,128)S(1)} %near_terms.1.own_ref, f32[40,384]{1,0:T(8,128)S(1)} %collective-permute-done.5.near_ref, f32[40,384]{1,0:T(8,128)S(1)} %collective-permute-done.6.far_ref), custom_call_target="tpu_custom_call" | custom-call | flops 1610612736 | bytes 4194304 | tf_op jit(solution)/shard_map/place_rows/pallas_call | solution.py:210
  (8 shorter events, 0.0 us)
Async XLA Ops:
  0.0 30.2 %collective-permute-start.4 = (bf16[1024,384]{1,0:T(8,128)(2,1)}, bf16[1024,384]{1,0:T(8,128)(2,1)S(1)}, u32[]{:S(2)}, u32[]{:S(2)}) collective-permute-start(bf16[1024,384]{1,0:T(8,128)(2,1)} %density_ref.1), channel_id=1, source_target_pairs={{0,127},{15,16},{16,15},{31,32},{32,31},{47,48},{48,47},{63,64},{6... | collective-permute-start | bytes 2359304 | tf_op jit(solution)/shard_map/ppermute | solution.py:328
  9.5 6.6 %collective-permute-start = (s32[32]{0:T(128)}, s32[32]{0:T(128)S(1)}, u32[]{:S(2)}, u32[]{:S(2)}) collective-permute-start(s32[32]{0:T(128)} %param.12), channel_id=1, source_target_pairs={{0,1},{1,0},{2,3},{3,2},{4,5},{5,4},{6,7},{7,6},{8,9},{9,8},{10,11... | collective-permute-start | bytes 392 | tf_op jit(solution)/shard_map/ppermute | solution.py:311
  9.6 6.6 %collective-permute-start.1 = (s32[32]{0:T(128)}, s32[32]{0:T(128)S(1)}, u32[]{:S(2)}, u32[]{:S(2)}) collective-permute-start(s32[32]{0:T(128)} %param.12), channel_id=1, source_target_pairs={{1,2},{2,1},{3,4},{4,3},{5,6},{6,5},{7,8},{8,7},{9,10},{10,9},{11,... | collective-permute-start | bytes 392 | tf_op jit(solution)/shard_map/ppermute | solution.py:323
  10.3 5.9 %copy-start = (bf16[1024,384]{1,0:T(8,128)(2,1)S(1)}, bf16[1024,384]{1,0:T(8,128)(2,1)}, u32[]{:S(2)}) copy-start(bf16[1024,384]{1,0:T(8,128)(2,1)} %density_ref.1) | copy-start | bytes 2359300
  10.3 5.9 %copy-start.1 = (s32[32]{0:T(128)S(1)}, s32[32]{0:T(128)}, u32[]{:S(2)}) copy-start(s32[32]{0:T(128)} %param.12) | copy-start | bytes 388
  16.1 7.4 %copy-start.3 = (s32[32]{0:T(128)S(1)}, s32[32]{0:T(128)}, u32[]{:S(2)}) copy-start(s32[32]{0:T(128)} %param.11) | copy-start | bytes 388
  16.6 13.6 %collective-permute-start.2 = (bf16[32,384]{1,0:T(8,128)(2,1)S(1)}, bf16[32,384]{1,0:T(8,128)(2,1)S(1)}, u32[]{:S(2)}, u32[]{:S(2)}) collective-permute-start(bf16[32,384]{1,0:T(8,128)(2,1)S(1)} %get-tuple-element.11), channel_id=1, source_target_pairs={{1,2},{2,1},{3,4},{4,3},{5,6},{6,5},{7,8},{8,7},{9,10},{10,9},{11,... | collective-permute-start | bytes 73736 | tf_op jit(solution)/shard_map/ppermute | solution.py:323
  17.3 12.9 %collective-permute-start.3 = (bf16[32,384]{1,0:T(8,128)(2,1)S(1)}, bf16[32,384]{1,0:T(8,128)(2,1)S(1)}, u32[]{:S(2)}, u32[]{:S(2)}) collective-permute-start(bf16[32,384]{1,0:T(8,128)(2,1)S(1)} %get-tuple-element.12), channel_id=1, source_target_pairs={{0,1},{1,0},{2,3},{3,2},{4,5},{5,4},{6,7},{7,6},{8,9},{9,8},{10,11... | collective-permute-start | bytes 73736 | tf_op jit(solution)/shard_map/ppermute | solution.py:311
  23.6 31.4 %all-to-all-start = ((s32[128,25,1,128]{3,2,1,0:T(1,128)}), s32[128,25,1,128]{3,2,1,0:T(1,128)S(1)}, u32[]{:S(2)}, u32[]{:S(2)}) async-start(s32[128,25,1,128]{3,2,1,0:T(1,128)} %bitcast.11), calls=%async_computation | async-start | bytes 3276800 | tf_op jit(solution)/shard_map/all_to_all | solution.py:338
  30.2 3.7 %copy-start.2 = (bf16[32,384,384]{2,1,0:T(8,128)(2,1)S(1)}, bf16[32,384,384]{2,1,0:T(8,128)(2,1)}, u32[]{:S(2)}) copy-start(bf16[32,384,384]{2,1,0:T(8,128)(2,1)} %mats_ref.1) | copy-start | bytes 28311556
  38.1 14.8 %collective-permute-start.5 = (f32[40,384]{1,0:T(8,128)S(1)}, f32[40,384]{1,0:T(8,128)S(1)}, u32[]{:S(2)}, u32[]{:S(2)}) collective-permute-start(f32[40,384]{1,0:T(8,128)S(1)} %near_terms.1.own_ref), channel_id=1, source_target_pairs={{0,127},{1,2},{2,1},{3,4},{4,3},{5,6},{6,5},{7,8},{8,7},{9,10},{10... | collective-permute-start | bytes 184328 | tf_op jit(solution)/shard_map/ppermute | solution.py:318
  44.2 8.7 %collective-permute-start.6 = (f32[40,384]{1,0:T(8,128)S(1)}, f32[40,384]{1,0:T(8,128)S(1)}, u32[]{:S(2)}, u32[]{:S(2)}) collective-permute-start(f32[40,384]{1,0:T(8,128)S(1)} %near_terms.1.own_ref), channel_id=1, source_target_pairs={{0,1},{1,0},{2,3},{3,2},{4,5},{5,4},{6,7},{7,6},{8,9},{9,8},{10,11... | collective-permute-start | bytes 184328 | tf_op jit(solution)/shard_map/ppermute | solution.py:311

commit v8 on v5

--- a/solution.py
+++ b/solution.py
@@ -150,7 +150,7 @@
     )(leaf_to_panel.reshape(8, 128), potentials)
 
 
-def place_kernel(me_ref, msg_ref, own_ref, near_ref, far_ref, out_hbm, out, sel, dig, hot_near, sems):
+def place_kernel(msg_ref, out, sel, dig):
     heads = msg_ref[pl.ds(LINES - 1, DEV, stride=LINES), :]
     turned = jnp.transpose(heads.astype(F32)).astype(I32)
     target = turned[0:CAP] - 1
@@ -171,18 +171,6 @@
             for c, hi, lo in ((r, (w >> 16) & 255, w & 255), (r + HALF, (w >> 24) & 255, (w >> 8) & 255)):
                 dig[pl.ds(c * 128, 128), pl.ds(n * 256, 128)] = hi.astype(F32).astype(BF16)
                 dig[pl.ds(c * 128, 128), pl.ds(n * 256 + 128, 128)] = lo.astype(F32).astype(BF16)
-    lane = iota((1, 128), 1)
-    own, adjacent, other = (ref[SLOTS : SLOTS + 1, 0:128] for ref in (own_ref, near_ref, far_ref))
-    rows = jnp.where(lane < SLOTS, own, jnp.where(lane < 2 * SLOTS, adjacent, other)).astype(I32)
-    target = jnp.where((rows < 0) | (lane >= 3 * SLOTS), -1, (rows - me_ref[0] * ROWS) & (TOTAL - 1))
-    for g in range(8):
-        hot = one_hot(target - g * 128 == sub)
-        hot_near[pl.ds(g * 128, 128), 0:128] = hot
-        hot_near[pl.ds(g * 128, 128), 128:256] = hot
-    near = jnp.concatenate([own_ref[0:SLOTS], near_ref[0:SLOTS], far_ref[0:SLOTS], jnp.zeros((SLOTS, BW), F32)], axis=0)
-    first = near.astype(BF16)
-    near = jnp.concatenate([first, (near - first.astype(F32)).astype(BF16)], axis=0)
-    put = []
     for g in range(2):
         part = sel[pl.ds(g * 256, 256), :]
         codes = mm(part, dig[:, pl.ds(2 * BW, 128)])[:, 0:2].astype(I32)
@@ -197,32 +185,56 @@
             hi, lo = both[:, :128], both[:, 128:]
             values = (((hi & 255) << 8) | (lo & 255), (hi & 0xFF00) | (lo >> 8))
             for h in range(2):
-                added = mm(hot_near[spots[h], :], near[:, n * 128 : n * 128 + 128])
-                out[spots[h], cols] = (values[h] - 32768).astype(F32) * scales[h] + added
-        for h in range(2):
-            put.append(pltpu.make_async_copy(out.at[spots[h]], out_hbm.at[spots[h]], sems.at[g * 2 + h]))
-            put[-1].start()
-    for copy in put:
-        copy.wait()
-
-
-def place(me, arrived, terms):
+                out[spots[h], cols] = (values[h] - 32768).astype(F32) * scales[h]
+
+
+def place(arrived):
     return pl.pallas_call(
         place_kernel,
         out_shape=jax.ShapeDtypeStruct((ROWS, BW), F32),
-        in_specs=[SMEM] + [VMEM] * 4,
-        out_specs=HBM,
+        in_specs=[VMEM],
+        out_specs=VMEM,
         scratch_shapes=[
-            pltpu.VMEM((ROWS, BW), F32),
             pltpu.VMEM((ROWS // 2, CAP * 128), BF16),
             pltpu.VMEM((CAP * 128, 2 * BW + 128), BF16),
-            pltpu.VMEM((ROWS, 256), BF16),
-            pltpu.SemaphoreType.DMA((4,)),
         ],
         compiler_params=pltpu.CompilerParams(vmem_limit_bytes=40 * 2**20),
         cost_estimate=pl.CostEstimate(flops=DEV * CAP * ROWS * 2 * BW, bytes_accessed=4 * 2**20, transcendentals=0),
         name="place_rows",
-    )(me, arrived, *terms)
+    )(arrived)
+
+
+def add_kernel(me_ref, placed_ref, own_ref, near_ref, far_ref, out_hbm, out, sems):
+    lane = iota((1, 128), 1)
+    own, adjacent, other = (ref[SLOTS : SLOTS + 1, 0:128] for ref in (own_ref, near_ref, far_ref))
+    rows = jnp.where(lane < SLOTS, own, jnp.where(lane < 2 * SLOTS, adjacent, other)).astype(I32)
+    target = jnp.where((rows < 0) | (lane >= 3 * SLOTS), -1, (rows - me_ref[0] * ROWS) & (TOTAL - 1))
+    near = jnp.concatenate([own_ref[0:SLOTS], near_ref[0:SLOTS], far_ref[0:SLOTS], jnp.zeros((SLOTS, BW), F32)], axis=0)
+    first = near.astype(BF16)
+    near = jnp.concatenate([first, (near - first.astype(F32)).astype(BF16)], axis=0)
+    sub = iota((256, 128), 0)
+    put = []
+    for g in range(4):
+        hot = one_hot(target - g * 256 == sub)
+        spot = pl.ds(g * 256, 256)
+        out[spot, :] = placed_ref[spot, :] + mm(jnp.concatenate([hot, hot], axis=1), near)
+        put.append(pltpu.make_async_copy(out.at[spot], out_hbm.at[spot], sems.at[g]))
+        put[g].start()
+    for copy in put:
+        copy.wait()
+
+
+def add_terms(me, placed, terms):
+    return pl.pallas_call(
+        add_kernel,
+        out_shape=jax.ShapeDtypeStruct((ROWS, BW), F32),
+        in_specs=[SMEM] + [VMEM] * 4,
+        out_specs=HBM,
+        scratch_shapes=[pltpu.VMEM((ROWS, BW), F32), pltpu.SemaphoreType.DMA((4,))],
+        compiler_params=pltpu.CompilerParams(vmem_limit_bytes=12 * 2**20),
+        cost_estimate=pl.CostEstimate(flops=2 * ROWS * 256 * BW, bytes_accessed=4 * 2**20, transcendentals=0),
+        name="add_terms",
+    )(me, placed, *terms)
 
 
 def fetch_kernel(me_ref, own_cols, near_cols, far_cols, density_ref, msg_ref, own_ref, near_ref, far_ref, out_ref):
@@ -273,10 +285,11 @@
 
     @pl.when(step == SLOTS // STEP - 1)
     def _():
-        live = iota((SLOTS, BW), 0) < count_ref[0]
+        live = iota((SLOTS, BW), 0) < count_ref[...]
         out_ref[0:SLOTS, :] = jnp.where(live, jnp.transpose(acc[...])[0:SLOTS], 0.0)
         slot = iota((1, 128), 1) & (SLOTS - 1)
-        rows = jnp.where(slot < count_ref[0], targets_ref[...], -1).astype(F32)
+        rows = jnp.concatenate([targets_ref[...]] * (128 // SLOTS), axis=1)
+        rows = jnp.where(slot < count_ref[...], rows, -1).astype(F32)
         for n in range(TILES):
             out_ref[SLOTS : SLOTS + 8, n * 128 : n * 128 + 128] = jnp.broadcast_to(rows, (8, 128))
 
@@ -289,7 +302,7 @@
         term_kernel,
         grid=(SLOTS // STEP,),
         out_shape=jax.ShapeDtypeStruct((SLOTS + 8, BW), F32),
-        in_specs=[SMEM, pl.BlockSpec((STEP, BW, BW), lambda i: (i, 0, 0)), whole(1, 128)] + [whole(SLOTS, BW)] * 3,
+        in_specs=[whole(1, 1), pl.BlockSpec((STEP, BW, BW), lambda i: (i, 0, 0)), whole(1, SLOTS)] + [whole(SLOTS, BW)] * 3,
         out_specs=whole(SLOTS + 8, BW),
         scratch_shapes=[pltpu.VMEM((BW, 128), F32), pltpu.VMEM((128, BW), BF16)],
         compiler_params=pltpu.CompilerParams(vmem_limit_bytes=20 * 2**20),
@@ -308,17 +321,16 @@
 
 def on_device(potentials, leaf_to_panel, density, corrections, correction_rows, correction_cols, block_count):
     me = lax.axis_index(AXES).astype(I32).reshape(1)
-    cols = (correction_cols, swap_near(correction_cols), swap_far(correction_cols))
+    cols = (correction_cols, swap_far(correction_cols), swap_near(correction_cols))
     message = pack(leaf_to_panel, potentials)
-    own, for_near, for_far, message = fetch(me, cols, density, message)
+    own, for_far, for_near, message = fetch(me, cols, density, message)
     rows = (own, swap_far(for_far), swap_near(for_near))
     arrived = lax.all_to_all(
         message.reshape(DEV, LINES, 1, 128), AXES, split_axis=0, concat_axis=0, tiled=True
     ).reshape(DEV * LINES, 128)
-    targets = jnp.tile(correction_rows, 128 // SLOTS).reshape(1, 128)
-    term = make_terms(block_count, corrections, targets, rows)
-    terms = (term, swap_near(term), swap_far(term))
-    return place(me, arrived, terms)
+    term = make_terms(block_count.reshape(1, 1), corrections, correction_rows.reshape(1, SLOTS), rows)
+    terms = (term, swap_far(term), swap_near(term))
+    return add_terms(me, place(arrived), terms)
 
 
 def solution(mesh):

time: 56.5 us -> 55.6 us (0.984); the launches traced: 55.5 us -> 55.4 us
    ppermute x3, waiting for transfers between devices: 9.08 us -> 0.01 us  [swap_far(): lax.ppermute(value, AXES, [(i, (i - 1 + 2 * (i % 2)) % DEV) for i in rang...]
    all_to_all x1, waiting for transfers between devices: 2.06 us -> 11.1 us  [on_device(): lax.all_to_all(message.reshape(DEV, LINES, 1, 128), AXES, split_axis=0, c...]
    pallas_call x1, Pallas kernels: 4.8 us -> 3.34 us  [place(): pl.pallas_call(place_kernel, out_shape=jax.ShapeDtypeStruct((ROWS, BW), F...]
    pallas_call x0 -> x1, Pallas kernels: none -> 1.4 us  [add_terms(): pl.pallas_call(add_kernel, out_shape=jax.ShapeDtypeStruct((ROWS, BW), F32...]
  transfers between devices with their start and end apart: 7 -> 7, of which waited for: 2 -> 1; matrix products, arithmetic and copies ran while one was open for 0% -> 0% of each run, Pallas kernels for 18% -> 24%
where the time goes in v8:
time: 55.6 us; the launch traced here: 55.4 us
  starting transfers between devices  24.8 us (45%)
  Pallas kernels  15 us (27%)
  waiting for transfers between devices  11.1 us (20%)
  local copies, waits for them, and re-layouts  3.69 us (7%)
  between operations  0.79 us (1%)
    ppermute x3, starting transfers between devices, swap_far(): lax.ppermute(value, AXES, [(i, (i - 1 + 2 * (i % 2)) % DEV) for i in rang...  14.8 us
    all_to_all x1, waiting for transfers between devices, on_device(): lax.all_to_all(message.reshape(DEV, LINES, 1, 128), AXES, split_axis=0, c...  11.1 us
    all_to_all x1, starting transfers between devices, on_device(): lax.all_to_all(message.reshape(DEV, LINES, 1, 128), AXES, split_axis=0, c...  9.7 us
    pallas_call x1, Pallas kernels, pack(): pl.pallas_call(pack_kernel, out_shape=jax.ShapeDtypeStruct((DEV * LINES,...  5.82 us
    pallas_call x1, Pallas kernels, make_terms(): pl.pallas_call(term_kernel, grid=(SLOTS // STEP,), out_shape=jax.ShapeDty...  4.02 us
    unnamed x8, local copies, waits for them, and re-layouts  3.69 us
    pallas_call x1, Pallas kernels, place(): pl.pallas_call(place_kernel, out_shape=jax.ShapeDtypeStruct((ROWS, BW), F...  3.34 us
    pallas_call x1, Pallas kernels, add_terms(): pl.pallas_call(add_kernel, out_shape=jax.ShapeDtypeStruct((ROWS, BW), F32...  1.4 us
  transfers between devices with their start and end apart: 7, of which 1 were waited for; matrix products, arithmetic and copies ran while one was open for 0% of the time, Pallas kernels for 24%

profile of v8, /device:TPU:1, one launch (start us, length us, event | category | flops | bytes accessed | tf_op | source)
XLA Modules:
  0.0 55.4 jit_solution(14822230519898109685)
XLA Ops:
  0.0 7.6 %collective-permute-start = (s32[32]{0:T(128)}, s32[32]{0:T(128)S(1)}, u32[]{:S(2)}, u32[]{:S(2)}) collective-permute-start(s32[32]{0:T(128)} %param.12), channel_id=1, source_target_pairs={{0,127},{1,2},{2,1},{3,4},{4,3},{5,6},{6,5},{7,8},{8,7},{9,10},{10... | collective-permute-start | bytes 392 | tf_op jit(solution)/shard_map/ppermute | solution.py:319
  7.6 0.0 collective-permute-start.1
  7.6 5.8 %pack_rows.1.msg_ref = s32[3200,128]{1,0:T(8,128)} custom-call(s32[8,128]{1,0:T(8,128)} %bitcast.16, f32[1024,384]{1,0:T(8,128)} %pot_hbm.1), custom_call_target="tpu_custom_call" | custom-call | flops 3221225472 | bytes 4194304 | tf_op jit(solution)/shard_map/pack_rows/pallas_call | solution.py:133
  13.4 0.0 collective-permute-done
  13.5 0.0 collective-permute-done.1
  13.5 0.0 copy-done
  13.5 0.0 copy-done.1
  13.5 0.4 fetch_density.1
  13.9 1.3 %collective-permute-start.2 = (bf16[32,384]{1,0:T(8,128)(2,1)S(1)}, bf16[32,384]{1,0:T(8,128)(2,1)S(1)}, u32[]{:S(2)}, u32[]{:S(2)}) collective-permute-start(bf16[32,384]{1,0:T(8,128)(2,1)S(1)} %get-tuple-element.11), channel_id=1, source_target_pairs={{0,127},{1,2},{2,1},{3,4},{4,3},{5,6},{6,5},{7,8},{8,7},{9,10},{10... | collective-permute-start | bytes 73736 | tf_op jit(solution)/shard_map/ppermute | solution.py:319
  15.2 0.4 collective-permute-start.3
  16.2 0.0 copy-start.3
  16.2 9.7 %all-to-all-start = ((s32[128,25,1,128]{3,2,1,0:T(1,128)}), s32[128,25,1,128]{3,2,1,0:T(1,128)S(1)}, u32[]{:S(2)}, u32[]{:S(2)}) async-start(s32[128,25,1,128]{3,2,1,0:T(1,128)} %bitcast.15), calls=%async_computation | async-start | bytes 3276800 | tf_op jit(solution)/shard_map/all_to_all | solution.py:328
  25.9 0.0 collective-permute-done.2.far_ref
  25.9 0.0 collective-permute-done.3.near_ref
  25.9 0.0 copy-start.2
  26.0 3.7 %copy-done.2 = bf16[32,384,384]{2,1,0:T(8,128)(2,1)S(1)} copy-done((bf16[32,384,384]{2,1,0:T(8,128)(2,1)S(1)}, bf16[32,384,384]{2,1,0:T(8,128)(2,1)}, u32[]{:S(2)}) %copy-start.2) | copy-done | bytes 9437208
  29.6 4.0 %near_terms.1.own_ref = f32[40,384]{1,0:T(8,128)S(1)} custom-call(s32[1,1]{1,0:T(1,128)} %bitcast.9.count_ref, bf16[32,384,384]{2,1,0:T(8,128)(2,1)S(1)} %copy-done.2, s32[1,32]{1,0:T(1,128)S(1)} %bitcast.14, bf16[32,384]{1,0:T(8,128)(2,1)S(1)} %get-tuple-element.10.own_ref, bf16[32,384]{1,0:T(8,128)(2,1)S(1)} %collective-permute-done.2.far_ref, ...), custom_call_target="tpu_custom_call" | custom-call | flops 60000002048 | bytes 9437184 | tf_op jit(solution)/shard_map/near_terms/pallas_call | solution.py:301
  33.7 5.9 %collective-permute-start.4 = (f32[40,384]{1,0:T(8,128)S(1)}, f32[40,384]{1,0:T(8,128)S(1)}, u32[]{:S(2)}, u32[]{:S(2)}) collective-permute-start(f32[40,384]{1,0:T(8,128)S(1)} %near_terms.1.own_ref), channel_id=1, source_target_pairs={{0,127},{1,2},{2,1},{3,4},{4,3},{5,6},{6,5},{7,8},{8,7},{9,10},{10... | collective-permute-start | bytes 184328 | tf_op jit(solution)/shard_map/ppermute | solution.py:319
  39.5 0.0 collective-permute-start.5
  39.5 11.1 %all-to-all-done = s32[128,25,1,128]{3,2,1,0:T(1,128)S(1)} async-done(((s32[128,25,1,128]{3,2,1,0:T(1,128)}), s32[128,25,1,128]{3,2,1,0:T(1,128)S(1)}, u32[]{:S(2)}, u32[]{:S(2)}) %all-to-all-start) | async-done | bytes 1638432 | tf_op jit(solution)/shard_map/all_to_all | solution.py:328
  50.6 3.3 %place_rows.1.placed_ref = f32[1024,384]{1,0:T(8,128)S(1)} custom-call(s32[3200,128]{1,0:T(8,128)S(1)} %bitcast.10), custom_call_target="tpu_custom_call" | custom-call | flops 1610612736 | bytes 4194304 | tf_op jit(solution)/shard_map/place_rows/pallas_call | solution.py:192
  54.0 0.0 collective-permute-done.4.near_ref
  54.0 0.0 collective-permute-done.5.far_ref
  54.0 1.4 %add_terms.1 = f32[1024,384]{1,0:T(8,128)} custom-call(s32[1]{0:T(128)} %bitcast.me_ref, f32[1024,384]{1,0:T(8,128)S(1)} %place_rows.1.placed_ref, f32[40,384]{1,0:T(8,128)S(1)} %near_terms.1.own_ref, f32[40,384]{1,0:T(8,128)S(1)} %collective-permute-done.4.near_ref, f32[40,384]{1,0:T(8,128)S(1)} %collective-permute-done.5.far_ref), custom_call_target="tpu_custom_call" | custom-call | flops 201326592 | bytes 4194304 | tf_op jit(solution)/shard_map/add_terms/pallas_call | solution.py:228
  (3 shorter events, 0.0 us)
Async XLA Ops:
  0.0 13.4 %collective-permute-start = (s32[32]{0:T(128)}, s32[32]{0:T(128)S(1)}, u32[]{:S(2)}, u32[]{:S(2)}) collective-permute-start(s32[32]{0:T(128)} %param.12), channel_id=1, source_target_pairs={{0,127},{1,2},{2,1},{3,4},{4,3},{5,6},{6,5},{7,8},{8,7},{9,10},{10... | collective-permute-start | bytes 392 | tf_op jit(solution)/shard_map/ppermute | solution.py:319
  7.6 5.9 %collective-permute-start.1 = (s32[32]{0:T(128)}, s32[32]{0:T(128)S(1)}, u32[]{:S(2)}, u32[]{:S(2)}) collective-permute-start(s32[32]{0:T(128)} %param.12), channel_id=1, source_target_pairs={{0,1},{1,0},{2,3},{3,2},{4,5},{5,4},{6,7},{7,6},{8,9},{9,8},{10,11... | collective-permute-start | bytes 392 | tf_op jit(solution)/shard_map/ppermute | solution.py:315
  7.6 5.9 %copy-start = (bf16[1024,384]{1,0:T(8,128)(2,1)S(1)}, bf16[1024,384]{1,0:T(8,128)(2,1)}, u32[]{:S(2)}) copy-start(bf16[1024,384]{1,0:T(8,128)(2,1)} %density_ref.1) | copy-start | bytes 2359300
  7.6 5.9 %copy-start.1 = (s32[32]{0:T(128)S(1)}, s32[32]{0:T(128)}, u32[]{:S(2)}) copy-start(s32[32]{0:T(128)} %param.12) | copy-start | bytes 388
  13.9 12.0 %collective-permute-start.2 = (bf16[32,384]{1,0:T(8,128)(2,1)S(1)}, bf16[32,384]{1,0:T(8,128)(2,1)S(1)}, u32[]{:S(2)}, u32[]{:S(2)}) collective-permute-start(bf16[32,384]{1,0:T(8,128)(2,1)S(1)} %get-tuple-element.11), channel_id=1, source_target_pairs={{0,127},{1,2},{2,1},{3,4},{4,3},{5,6},{6,5},{7,8},{8,7},{9,10},{10... | collective-permute-start | bytes 73736 | tf_op jit(solution)/shard_map/ppermute | solution.py:319
  15.2 10.8 %collective-permute-start.3 = (bf16[32,384]{1,0:T(8,128)(2,1)S(1)}, bf16[32,384]{1,0:T(8,128)(2,1)S(1)}, u32[]{:S(2)}, u32[]{:S(2)}) collective-permute-start(bf16[32,384]{1,0:T(8,128)(2,1)S(1)} %get-tuple-element.12), channel_id=1, source_target_pairs={{0,1},{1,0},{2,3},{3,2},{4,5},{5,4},{6,7},{7,6},{8,9},{9,8},{10,11... | collective-permute-start | bytes 73736 | tf_op jit(solution)/shard_map/ppermute | solution.py:315
  16.2 9.7 %copy-start.3 = (s32[32]{0:T(128)S(1)}, s32[32]{0:T(128)}, u32[]{:S(2)}) copy-start(s32[32]{0:T(128)} %param.11) | copy-start | bytes 388
  16.2 34.4 %all-to-all-start = ((s32[128,25,1,128]{3,2,1,0:T(1,128)}), s32[128,25,1,128]{3,2,1,0:T(1,128)S(1)}, u32[]{:S(2)}, u32[]{:S(2)}) async-start(s32[128,25,1,128]{3,2,1,0:T(1,128)} %bitcast.15), calls=%async_computation | async-start | bytes 3276800 | tf_op jit(solution)/shard_map/all_to_all | solution.py:328
  25.9 3.7 %copy-start.2 = (bf16[32,384,384]{2,1,0:T(8,128)(2,1)S(1)}, bf16[32,384,384]{2,1,0:T(8,128)(2,1)}, u32[]{:S(2)}) copy-start(bf16[32,384,384]{2,1,0:T(8,128)(2,1)} %mats_ref.1) | copy-start | bytes 28311556
  33.7 20.3 %collective-permute-start.4 = (f32[40,384]{1,0:T(8,128)S(1)}, f32[40,384]{1,0:T(8,128)S(1)}, u32[]{:S(2)}, u32[]{:S(2)}) collective-permute-start(f32[40,384]{1,0:T(8,128)S(1)} %near_terms.1.own_ref), channel_id=1, source_target_pairs={{0,127},{1,2},{2,1},{3,4},{4,3},{5,6},{6,5},{7,8},{8,7},{9,10},{10... | collective-permute-start | bytes 184328 | tf_op jit(solution)/shard_map/ppermute | solution.py:319
  39.5 14.4 %collective-permute-start.5 = (f32[40,384]{1,0:T(8,128)S(1)}, f32[40,384]{1,0:T(8,128)S(1)}, u32[]{:S(2)}, u32[]{:S(2)}) collective-permute-start(f32[40,384]{1,0:T(8,128)S(1)} %near_terms.1.own_ref), channel_id=1, source_target_pairs={{0,1},{1,0},{2,3},{3,2},{4,5},{5,4},{6,7},{7,6},{8,9},{9,8},{10,11... | collective-permute-start | bytes 184328 | tf_op jit(solution)/shard_map/ppermute | solution.py:315

commit v9 on v8

--- a/solution.py
+++ b/solution.py
@@ -44,7 +44,7 @@
     return jnp.dot(a, b, preferred_element_type=F32)
 
 
-def pack_kernel(map_hbm, pot_hbm, out_hbm, place, pot, msg, sel, dig, head, sems):
+def pack_kernel(map_hbm, pot_hbm, out_hbm, place, pot, msg, sel, dig, head, half, sems):
     get_map = pltpu.make_async_copy(map_hbm, place, sems.at[0])
     get_map.start()
     get_pot = []
@@ -78,8 +78,16 @@
         ranked.append(one_hot(ranks[b].astype(I32) == low))
 
     for g in range(8):
-        if g % 2 == 0:
-            get_pot[g // 2].wait()
+        if g == 0:
+            get_pot[0].wait()
+            get_pot[1].wait()
+        if g == 4:
+            get_pot[2].wait()
+            get_pot[3].wait()
+            for k in range(4):
+                for n in range(TILES):
+                    cols = pl.ds(n * 256, 256)
+                    half[pl.ds(k * 256, 256), cols] = mm(sel[pl.ds(k * 256, 256), 0:512], dig[0:512, cols])
         rows = pl.ds(g * 128, 128)
         x = pot[rows, :]
         top = jnp.max(jnp.abs(x), axis=1, keepdims=True)
@@ -88,10 +96,9 @@
         power = jnp.exp2(expo).astype(BF16).astype(F32)
         mant = jnp.maximum(jnp.ceil((step / power - 1.0) * 64.0), 0.0)
         scale = power * (1.0 + mant * (1.0 / 64.0))
-        q = jnp.clip(jnp.round(x * (1.0 / scale)), -32767.0, 32767.0)
+        q = jnp.round(x * (1.0 / scale)) + 32768.0
         hi = jnp.floor(q * (1.0 / 256.0))
         lo = q - hi * 256.0
-        hi = hi + 128.0
         for n in range(TILES):
             dig[rows, pl.ds(n * 256, 128)] = hi[:, n * 128 : n * 128 + 128].astype(BF16)
             dig[rows, pl.ds(n * 256 + 128, 128)] = lo[:, n * 128 : n * 128 + 128].astype(BF16)
@@ -118,7 +125,9 @@
     put = []
     for g in range(4):
         for n in range(TILES):
-            both = mm(sel[pl.ds(g * 256, 256), :], dig[:, pl.ds(n * 256, 256)]).astype(I32)
+            cols = pl.ds(n * 256, 256)
+            both = half[pl.ds(g * 256, 256), cols] + mm(sel[pl.ds(g * 256, 256), 512:1024], dig[512:1024, cols])
+            both = both.astype(I32)
             w = (both[:, :128] << 16) | both[:, 128:]
             for r in range(HALF):
                 msg[pl.ds(g * 32 * LINES + n * HALF + r, 32, stride=LINES), :] = w[r * 32 : r * 32 + 32]
@@ -142,6 +151,7 @@
             pltpu.VMEM((DEV * HALF, ROWS), BF16),
             pltpu.VMEM((ROWS, 2 * BW), BF16),
             pltpu.VMEM((ROWS, 128), BF16),
+            pltpu.VMEM((ROWS, 2 * BW), F32),
             pltpu.SemaphoreType.DMA((9,)),
         ],
         compiler_params=pltpu.CompilerParams(vmem_limit_bytes=60 * 2**20),
@@ -171,14 +181,13 @@
             for c, hi, lo in ((r, (w >> 16) & 255, w & 255), (r + HALF, (w >> 24) & 255, (w >> 8) & 255)):
                 dig[pl.ds(c * 128, 128), pl.ds(n * 256, 128)] = hi.astype(F32).astype(BF16)
                 dig[pl.ds(c * 128, 128), pl.ds(n * 256 + 128, 128)] = lo.astype(F32).astype(BF16)
-    for g in range(2):
-        part = sel[pl.ds(g * 256, 256), :]
+    for part in (sel[...],):
         codes = mm(part, dig[:, pl.ds(2 * BW, 128)])[:, 0:2].astype(I32)
         scales = []
         for code in (codes & 255, codes >> 8):
             power = jnp.exp2(code[:, 0:1].astype(F32) - 128.0).astype(BF16).astype(F32)
             scales.append(power * (1.0 + code[:, 1:2].astype(F32) * (1.0 / 64.0)))
-        spots = [pl.ds(h * 512 + g * 256, 256) for h in range(2)]
+        spots = [pl.ds(h * 512, 512) for h in range(2)]
         for n in range(TILES):
             cols = pl.ds(n * 128, 128)
             both = mm(part, dig[:, pl.ds(n * 256, 256)]).astype(I32)

time: 55.6 us -> 55 us (0.989)
  Pallas kernels: 15 us -> 14.4 us
  transfers between devices with their start and end apart: 7 -> 7, of which waited for: 1 -> 1; matrix products, arithmetic and copies ran while one was open for 0% -> 0% of each run, Pallas kernels for 24% -> 23%
where the time goes in v9:
time: 55 us; the launch traced here: 54.8 us
  starting transfers between devices  24.8 us (45%)
  Pallas kernels  14.4 us (26%)
  waiting for transfers between devices  11.1 us (20%)
  local copies, waits for them, and re-layouts  3.69 us (7%)
  between operations  0.79 us (1%)
    ppermute x3, starting transfers between devices, swap_far(): lax.ppermute(value, AXES, [(i, (i - 1 + 2 * (i % 2)) % DEV) for i in rang...  14.8 us
    all_to_all x1, waiting for transfers between devices, on_device(): lax.all_to_all(message.reshape(DEV, LINES, 1, 128), AXES, split_axis=0, c...  11.1 us
    all_to_all x1, starting transfers between devices, on_device(): lax.all_to_all(message.reshape(DEV, LINES, 1, 128), AXES, split_axis=0, c...  9.68 us
    pallas_call x1, Pallas kernels, pack(): pl.pallas_call(pack_kernel, out_shape=jax.ShapeDtypeStruct((DEV * LINES,...  5.43 us
    pallas_call x1, Pallas kernels, make_terms(): pl.pallas_call(term_kernel, grid=(SLOTS // STEP,), out_shape=jax.ShapeDty...  4.02 us
    unnamed x8, local copies, waits for them, and re-layouts  3.69 us
    pallas_call x1, Pallas kernels, place(): pl.pallas_call(place_kernel, out_shape=jax.ShapeDtypeStruct((ROWS, BW), F...  3.13 us
    pallas_call x1, Pallas kernels, add_terms(): pl.pallas_call(add_kernel, out_shape=jax.ShapeDtypeStruct((ROWS, BW), F32...  1.4 us
  transfers between devices with their start and end apart: 7, of which 1 were waited for; matrix products, arithmetic and copies ran while one was open for 0% of the time, Pallas kernels for 23%

profile of v9, /device:TPU:1, one launch (start us, length us, event | category | flops | bytes accessed | tf_op | source)
XLA Modules:
  0.0 54.8 jit_solution(5259957953056655163)
XLA Ops:
  0.0 7.6 %collective-permute-start = (s32[32]{0:T(128)}, s32[32]{0:T(128)S(1)}, u32[]{:S(2)}, u32[]{:S(2)}) collective-permute-start(s32[32]{0:T(128)} %param.12), channel_id=1, source_target_pairs={{0,127},{1,2},{2,1},{3,4},{4,3},{5,6},{6,5},{7,8},{8,7},{9,10},{10... | collective-permute-start | bytes 392 | tf_op jit(solution)/shard_map/ppermute | solution.py:328
  7.6 0.0 collective-permute-start.1
  7.6 5.4 %pack_rows.1.msg_ref = s32[3200,128]{1,0:T(8,128)} custom-call(s32[8,128]{1,0:T(8,128)} %bitcast.16, f32[1024,384]{1,0:T(8,128)} %pot_hbm.1), custom_call_target="tpu_custom_call" | custom-call | flops 3221225472 | bytes 4194304 | tf_op jit(solution)/shard_map/pack_rows/pallas_call | solution.py:142
  13.0 0.0 collective-permute-done
  13.1 0.0 collective-permute-done.1
  13.1 0.0 copy-done
  13.1 0.4 fetch_density.1
  13.5 1.3 %collective-permute-start.2 = (bf16[32,384]{1,0:T(8,128)(2,1)S(1)}, bf16[32,384]{1,0:T(8,128)(2,1)S(1)}, u32[]{:S(2)}, u32[]{:S(2)}) collective-permute-start(bf16[32,384]{1,0:T(8,128)(2,1)S(1)} %get-tuple-element.11), channel_id=1, source_target_pairs={{0,127},{1,2},{2,1},{3,4},{4,3},{5,6},{6,5},{7,8},{8,7},{9,10},{10... | collective-permute-start | bytes 73736 | tf_op jit(solution)/shard_map/ppermute | solution.py:328
  14.8 0.4 collective-permute-start.3
  15.8 0.0 copy-start.3
  15.8 9.7 %all-to-all-start = ((s32[128,25,1,128]{3,2,1,0:T(1,128)}), s32[128,25,1,128]{3,2,1,0:T(1,128)S(1)}, u32[]{:S(2)}, u32[]{:S(2)}) async-start(s32[128,25,1,128]{3,2,1,0:T(1,128)} %bitcast.15), calls=%async_computation | async-start | bytes 3276800 | tf_op jit(solution)/shard_map/all_to_all | solution.py:337
  25.5 0.0 collective-permute-done.2.far_ref
  25.5 0.0 collective-permute-done.3.near_ref
  25.5 0.0 copy-done.3
  25.5 0.0 copy-start.2
  25.6 3.7 %copy-done.2 = bf16[32,384,384]{2,1,0:T(8,128)(2,1)S(1)} copy-done((bf16[32,384,384]{2,1,0:T(8,128)(2,1)S(1)}, bf16[32,384,384]{2,1,0:T(8,128)(2,1)}, u32[]{:S(2)}) %copy-start.2) | copy-done | bytes 9437208
  29.2 4.0 %near_terms.1.own_ref = f32[40,384]{1,0:T(8,128)S(1)} custom-call(s32[1,1]{1,0:T(1,128)} %bitcast.9.count_ref, bf16[32,384,384]{2,1,0:T(8,128)(2,1)S(1)} %copy-done.2, s32[1,32]{1,0:T(1,128)S(1)} %bitcast.14, bf16[32,384]{1,0:T(8,128)(2,1)S(1)} %get-tuple-element.10.own_ref, bf16[32,384]{1,0:T(8,128)(2,1)S(1)} %collective-permute-done.2.far_ref, ...), custom_call_target="tpu_custom_call" | custom-call | flops 60000002048 | bytes 9437184 | tf_op jit(solution)/shard_map/near_terms/pallas_call | solution.py:310
  33.3 5.9 %collective-permute-start.4 = (f32[40,384]{1,0:T(8,128)S(1)}, f32[40,384]{1,0:T(8,128)S(1)}, u32[]{:S(2)}, u32[]{:S(2)}) collective-permute-start(f32[40,384]{1,0:T(8,128)S(1)} %near_terms.1.own_ref), channel_id=1, source_target_pairs={{0,127},{1,2},{2,1},{3,4},{4,3},{5,6},{6,5},{7,8},{8,7},{9,10},{10... | collective-permute-start | bytes 184328 | tf_op jit(solution)/shard_map/ppermute | solution.py:328
  39.1 0.0 collective-permute-start.5
  39.1 11.1 %all-to-all-done = s32[128,25,1,128]{3,2,1,0:T(1,128)S(1)} async-done(((s32[128,25,1,128]{3,2,1,0:T(1,128)}), s32[128,25,1,128]{3,2,1,0:T(1,128)S(1)}, u32[]{:S(2)}, u32[]{:S(2)}) %all-to-all-start) | async-done | bytes 1638432 | tf_op jit(solution)/shard_map/all_to_all | solution.py:337
  50.2 3.1 %place_rows.1.placed_ref = f32[1024,384]{1,0:T(8,128)S(1)} custom-call(s32[3200,128]{1,0:T(8,128)S(1)} %bitcast.10), custom_call_target="tpu_custom_call" | custom-call | flops 1610612736 | bytes 4194304 | tf_op jit(solution)/shard_map/place_rows/pallas_call | solution.py:201
  53.4 0.0 collective-permute-done.4.near_ref
  53.4 0.0 collective-permute-done.5.far_ref
  53.4 1.4 %add_terms.1 = f32[1024,384]{1,0:T(8,128)} custom-call(s32[1]{0:T(128)} %bitcast.me_ref, f32[1024,384]{1,0:T(8,128)S(1)} %place_rows.1.placed_ref, f32[40,384]{1,0:T(8,128)S(1)} %near_terms.1.own_ref, f32[40,384]{1,0:T(8,128)S(1)} %collective-permute-done.4.near_ref, f32[40,384]{1,0:T(8,128)S(1)} %collective-permute-done.5.far_ref), custom_call_target="tpu_custom_call" | custom-call | flops 201326592 | bytes 4194304 | tf_op jit(solution)/shard_map/add_terms/pallas_call | solution.py:237
  (3 shorter events, 0.0 us)
Async XLA Ops:
  0.0 13.1 %collective-permute-start = (s32[32]{0:T(128)}, s32[32]{0:T(128)S(1)}, u32[]{:S(2)}, u32[]{:S(2)}) collective-permute-start(s32[32]{0:T(128)} %param.12), channel_id=1, source_target_pairs={{0,127},{1,2},{2,1},{3,4},{4,3},{5,6},{6,5},{7,8},{8,7},{9,10},{10... | collective-permute-start | bytes 392 | tf_op jit(solution)/shard_map/ppermute | solution.py:328
  7.6 5.5 %collective-permute-start.1 = (s32[32]{0:T(128)}, s32[32]{0:T(128)S(1)}, u32[]{:S(2)}, u32[]{:S(2)}) collective-permute-start(s32[32]{0:T(128)} %param.12), channel_id=1, source_target_pairs={{0,1},{1,0},{2,3},{3,2},{4,5},{5,4},{6,7},{7,6},{8,9},{9,8},{10,11... | collective-permute-start | bytes 392 | tf_op jit(solution)/shard_map/ppermute | solution.py:324
  7.6 5.5 %copy-start = (bf16[1024,384]{1,0:T(8,128)(2,1)S(1)}, bf16[1024,384]{1,0:T(8,128)(2,1)}, u32[]{:S(2)}) copy-start(bf16[1024,384]{1,0:T(8,128)(2,1)} %density_ref.1) | copy-start | bytes 2359300
  7.6 5.5 %copy-start.1 = (s32[32]{0:T(128)S(1)}, s32[32]{0:T(128)}, u32[]{:S(2)}) copy-start(s32[32]{0:T(128)} %param.12) | copy-start | bytes 388
  13.5 12.0 %collective-permute-start.2 = (bf16[32,384]{1,0:T(8,128)(2,1)S(1)}, bf16[32,384]{1,0:T(8,128)(2,1)S(1)}, u32[]{:S(2)}, u32[]{:S(2)}) collective-permute-start(bf16[32,384]{1,0:T(8,128)(2,1)S(1)} %get-tuple-element.11), channel_id=1, source_target_pairs={{0,127},{1,2},{2,1},{3,4},{4,3},{5,6},{6,5},{7,8},{8,7},{9,10},{10... | collective-permute-start | bytes 73736 | tf_op jit(solution)/shard_map/ppermute | solution.py:328
  14.8 10.8 %collective-permute-start.3 = (bf16[32,384]{1,0:T(8,128)(2,1)S(1)}, bf16[32,384]{1,0:T(8,128)(2,1)S(1)}, u32[]{:S(2)}, u32[]{:S(2)}) collective-permute-start(bf16[32,384]{1,0:T(8,128)(2,1)S(1)} %get-tuple-element.12), channel_id=1, source_target_pairs={{0,1},{1,0},{2,3},{3,2},{4,5},{5,4},{6,7},{7,6},{8,9},{9,8},{10,11... | collective-permute-start | bytes 73736 | tf_op jit(solution)/shard_map/ppermute | solution.py:324
  15.8 9.7 %copy-start.3 = (s32[32]{0:T(128)S(1)}, s32[32]{0:T(128)}, u32[]{:S(2)}) copy-start(s32[32]{0:T(128)} %param.11) | copy-start | bytes 388
  15.8 34.4 %all-to-all-start = ((s32[128,25,1,128]{3,2,1,0:T(1,128)}), s32[128,25,1,128]{3,2,1,0:T(1,128)S(1)}, u32[]{:S(2)}, u32[]{:S(2)}) async-start(s32[128,25,1,128]{3,2,1,0:T(1,128)} %bitcast.15), calls=%async_computation | async-start | bytes 3276800 | tf_op jit(solution)/shard_map/all_to_all | solution.py:337
  25.5 3.7 %copy-start.2 = (bf16[32,384,384]{2,1,0:T(8,128)(2,1)S(1)}, bf16[32,384,384]{2,1,0:T(8,128)(2,1)}, u32[]{:S(2)}) copy-start(bf16[32,384,384]{2,1,0:T(8,128)(2,1)} %mats_ref.1) | copy-start | bytes 28311556
  33.3 20.1 %collective-permute-start.4 = (f32[40,384]{1,0:T(8,128)S(1)}, f32[40,384]{1,0:T(8,128)S(1)}, u32[]{:S(2)}, u32[]{:S(2)}) collective-permute-start(f32[40,384]{1,0:T(8,128)S(1)} %near_terms.1.own_ref), channel_id=1, source_target_pairs={{0,127},{1,2},{2,1},{3,4},{4,3},{5,6},{6,5},{7,8},{8,7},{9,10},{10... | collective-permute-start | bytes 184328 | tf_op jit(solution)/shard_map/ppermute | solution.py:328
  39.1 14.2 %collective-permute-start.5 = (f32[40,384]{1,0:T(8,128)S(1)}, f32[40,384]{1,0:T(8,128)S(1)}, u32[]{:S(2)}, u32[]{:S(2)}) collective-permute-start(f32[40,384]{1,0:T(8,128)S(1)} %near_terms.1.own_ref), channel_id=1, source_target_pairs={{0,1},{1,0},{2,3},{3,2},{4,5},{5,4},{6,7},{7,6},{8,9},{9,8},{10,11... | collective-permute-start | bytes 184328 | tf_op jit(solution)/shard_map/ppermute | solution.py:324

commit v10 on v9

--- a/solution.py
+++ b/solution.py
@@ -44,15 +44,12 @@
     return jnp.dot(a, b, preferred_element_type=F32)
 
 
-def pack_kernel(map_hbm, pot_hbm, out_hbm, place, pot, msg, sel, dig, head, half, sems):
-    get_map = pltpu.make_async_copy(map_hbm, place, sems.at[0])
-    get_map.start()
+def pack_kernel(place, pot_hbm, out_hbm, pot, msg, sel, dig, head, half, sems):
     get_pot = []
     for g in range(4):
         rows = pl.ds(g * 256, 256)
         get_pot.append(pltpu.make_async_copy(pot_hbm.at[rows], pot.at[rows], sems.at[1 + g]))
         get_pot[g].start()
-    get_map.wait()
 
     dest, label = place[...] >> 10, (place[...] & (ROWS - 1)) + 1
     sub = iota((128, 128), 0)
@@ -142,10 +139,9 @@
     return pl.pallas_call(
         pack_kernel,
         out_shape=jax.ShapeDtypeStruct((DEV * LINES, 128), I32),
-        in_specs=[HBM, HBM],
+        in_specs=[VMEM, HBM],
         out_specs=HBM,
         scratch_shapes=[
-            pltpu.VMEM((8, 128), I32),
             pltpu.VMEM((ROWS, BW), F32),
             pltpu.VMEM((DEV * LINES, 128), I32),
             pltpu.VMEM((DEV * HALF, ROWS), BF16),
@@ -154,7 +150,7 @@
             pltpu.VMEM((ROWS, 2 * BW), F32),
             pltpu.SemaphoreType.DMA((9,)),
         ],
-        compiler_params=pltpu.CompilerParams(vmem_limit_bytes=60 * 2**20),
+        compiler_params=pltpu.CompilerParams(vmem_limit_bytes=105 * 2**19),
         cost_estimate=pl.CostEstimate(flops=2 * DEV * CAP * ROWS * 2 * BW, bytes_accessed=4 * 2**20, transcendentals=0),
         name="pack_rows",
     )(leaf_to_panel.reshape(8, 128), potentials)

time: 55 us -> 55.3 us (level)
  local copies, waits for them, and re-layouts: 3.69 us -> 4.38 us
    unnamed x8 -> x10, local copies, waits for them, and re-layouts: 3.69 us -> 4.38 us
  transfers between devices with their start and end apart: 7 -> 7, of which waited for: 1 -> 1; matrix products, arithmetic and copies ran while one was open for 0% -> 0% of each run, Pallas kernels for 23% -> 22%
where the time goes in v10:
time: 55.3 us; the launch traced here: 55 us
  starting transfers between devices  24.8 us (45%)
  Pallas kernels  13.9 us (25%)
  waiting for transfers between devices  11.1 us (20%)
  local copies, waits for them, and re-layouts  4.38 us (8%)
  between operations  0.79 us (1%)
    ppermute x3, starting transfers between devices, swap_far(): lax.ppermute(value, AXES, [(i, (i - 1 + 2 * (i % 2)) % DEV) for i in rang...  14.8 us
    all_to_all x1, waiting for transfers between devices, on_device(): lax.all_to_all(message.reshape(DEV, LINES, 1, 128), AXES, split_axis=0, c...  11.1 us
    all_to_all x1, starting transfers between devices, on_device(): lax.all_to_all(message.reshape(DEV, LINES, 1, 128), AXES, split_axis=0, c...  9.7 us
    pallas_call x1, Pallas kernels, pack(): pl.pallas_call(pack_kernel, out_shape=jax.ShapeDtypeStruct((DEV * LINES,...  4.98 us
    unnamed x10, local copies, waits for them, and re-layouts  4.38 us
    pallas_call x1, Pallas kernels, make_terms(): pl.pallas_call(term_kernel, grid=(SLOTS // STEP,), out_shape=jax.ShapeDty...  4.02 us
    pallas_call x1, Pallas kernels, place(): pl.pallas_call(place_kernel, out_shape=jax.ShapeDtypeStruct((ROWS, BW), F...  3.13 us
    pallas_call x1, Pallas kernels, add_terms(): pl.pallas_call(add_kernel, out_shape=jax.ShapeDtypeStruct((ROWS, BW), F32...  1.4 us
  transfers between devices with their start and end apart: 7, of which 1 were waited for; matrix products, arithmetic and copies ran while one was open for 0% of the time, Pallas kernels for 22%

profile of v10, /device:TPU:1, one launch (start us, length us, event | category | flops | bytes accessed | tf_op | source)
XLA Modules:
  0.0 55.0 jit_solution(13702426923651053201)
XLA Ops:
  0.0 7.6 %collective-permute-start = (s32[32]{0:T(128)}, s32[32]{0:T(128)S(1)}, u32[]{:S(2)}, u32[]{:S(2)}) collective-permute-start(s32[32]{0:T(128)} %param.12), channel_id=1, source_target_pairs={{0,127},{1,2},{2,1},{3,4},{4,3},{5,6},{6,5},{7,8},{8,7},{9,10},{10... | collective-permute-start | bytes 392 | tf_op jit(solution)/shard_map/ppermute | solution.py:324
  7.6 0.0 collective-permute-start.1
  7.6 0.7 %copy-done.3 = s32[1024]{0:T(1024)S(1)} copy-done((s32[1024]{0:T(1024)S(1)}, s32[1024]{0:T(1024)}, u32[]{:S(2)}) %copy-start.3) | copy-done | bytes 4120
  8.3 5.0 %pack_rows.1.msg_ref = s32[3200,128]{1,0:T(8,128)} custom-call(s32[8,128]{1,0:T(8,128)S(1)} %bitcast.14, f32[1024,384]{1,0:T(8,128)} %pot_hbm.1), custom_call_target="tpu_custom_call" | custom-call | flops 3221225472 | bytes 4194304 | tf_op jit(solution)/shard_map/pack_rows/pallas_call | solution.py:139
  13.3 0.0 collective-permute-done
  13.3 0.0 collective-permute-done.1
  13.3 0.0 copy-done
  13.3 0.4 fetch_density.1
  13.7 1.3 %collective-permute-start.2 = (bf16[32,384]{1,0:T(8,128)(2,1)S(1)}, bf16[32,384]{1,0:T(8,128)(2,1)S(1)}, u32[]{:S(2)}, u32[]{:S(2)}) collective-permute-start(bf16[32,384]{1,0:T(8,128)(2,1)S(1)} %get-tuple-element.11), channel_id=1, source_target_pairs={{0,127},{1,2},{2,1},{3,4},{4,3},{5,6},{6,5},{7,8},{8,7},{9,10},{10... | collective-permute-start | bytes 73736 | tf_op jit(solution)/shard_map/ppermute | solution.py:324
  15.0 0.4 collective-permute-start.3
  16.0 0.0 copy-start.4
  16.1 9.7 %all-to-all-start = ((s32[128,25,1,128]{3,2,1,0:T(1,128)}), s32[128,25,1,128]{3,2,1,0:T(1,128)S(1)}, u32[]{:S(2)}, u32[]{:S(2)}) async-start(s32[128,25,1,128]{3,2,1,0:T(1,128)} %bitcast.16), calls=%async_computation | async-start | bytes 3276800 | tf_op jit(solution)/shard_map/all_to_all | solution.py:333
  25.8 0.0 collective-permute-done.2.far_ref
  25.8 0.0 collective-permute-done.3.near_ref
  25.8 0.0 copy-start.2
  25.8 3.7 %copy-done.2 = bf16[32,384,384]{2,1,0:T(8,128)(2,1)S(1)} copy-done((bf16[32,384,384]{2,1,0:T(8,128)(2,1)S(1)}, bf16[32,384,384]{2,1,0:T(8,128)(2,1)}, u32[]{:S(2)}) %copy-start.2) | copy-done | bytes 9437208
  29.5 4.0 %near_terms.1.own_ref = f32[40,384]{1,0:T(8,128)S(1)} custom-call(s32[1,1]{1,0:T(1,128)} %bitcast.9.count_ref, bf16[32,384,384]{2,1,0:T(8,128)(2,1)S(1)} %copy-done.2, s32[1,32]{1,0:T(1,128)S(1)} %bitcast.15, bf16[32,384]{1,0:T(8,128)(2,1)S(1)} %get-tuple-element.10.own_ref, bf16[32,384]{1,0:T(8,128)(2,1)S(1)} %collective-permute-done.2.far_ref, ...), custom_call_target="tpu_custom_call" | custom-call | flops 60000002048 | bytes 9437184 | tf_op jit(solution)/shard_map/near_terms/pallas_call | solution.py:306
  33.5 5.9 %collective-permute-start.4 = (f32[40,384]{1,0:T(8,128)S(1)}, f32[40,384]{1,0:T(8,128)S(1)}, u32[]{:S(2)}, u32[]{:S(2)}) collective-permute-start(f32[40,384]{1,0:T(8,128)S(1)} %near_terms.1.own_ref), channel_id=1, source_target_pairs={{0,127},{1,2},{2,1},{3,4},{4,3},{5,6},{6,5},{7,8},{8,7},{9,10},{10... | collective-permute-start | bytes 184328 | tf_op jit(solution)/shard_map/ppermute | solution.py:324
  39.4 0.0 collective-permute-start.5
  39.4 11.1 %all-to-all-done = s32[128,25,1,128]{3,2,1,0:T(1,128)S(1)} async-done(((s32[128,25,1,128]{3,2,1,0:T(1,128)}), s32[128,25,1,128]{3,2,1,0:T(1,128)S(1)}, u32[]{:S(2)}, u32[]{:S(2)}) %all-to-all-start) | async-done | bytes 1638432 | tf_op jit(solution)/shard_map/all_to_all | solution.py:333
  50.5 3.1 %place_rows.1.placed_ref = f32[1024,384]{1,0:T(8,128)S(1)} custom-call(s32[3200,128]{1,0:T(8,128)S(1)} %bitcast.10), custom_call_target="tpu_custom_call" | custom-call | flops 1610612736 | bytes 4194304 | tf_op jit(solution)/shard_map/place_rows/pallas_call | solution.py:197
  53.6 0.0 collective-permute-done.4.near_ref
  53.6 0.0 collective-permute-done.5.far_ref
  53.6 1.4 %add_terms.1 = f32[1024,384]{1,0:T(8,128)} custom-call(s32[1]{0:T(128)} %bitcast.me_ref, f32[1024,384]{1,0:T(8,128)S(1)} %place_rows.1.placed_ref, f32[40,384]{1,0:T(8,128)S(1)} %near_terms.1.own_ref, f32[40,384]{1,0:T(8,128)S(1)} %collective-permute-done.4.near_ref, f32[40,384]{1,0:T(8,128)S(1)} %collective-permute-done.5.far_ref), custom_call_target="tpu_custom_call" | custom-call | flops 201326592 | bytes 4194304 | tf_op jit(solution)/shard_map/add_terms/pallas_call | solution.py:233
  (5 shorter events, 0.0 us)
Async XLA Ops:
  0.0 13.3 %collective-permute-start = (s32[32]{0:T(128)}, s32[32]{0:T(128)S(1)}, u32[]{:S(2)}, u32[]{:S(2)}) collective-permute-start(s32[32]{0:T(128)} %param.12), channel_id=1, source_target_pairs={{0,127},{1,2},{2,1},{3,4},{4,3},{5,6},{6,5},{7,8},{8,7},{9,10},{10... | collective-permute-start | bytes 392 | tf_op jit(solution)/shard_map/ppermute | solution.py:324
  7.6 5.7 %collective-permute-start.1 = (s32[32]{0:T(128)}, s32[32]{0:T(128)S(1)}, u32[]{:S(2)}, u32[]{:S(2)}) collective-permute-start(s32[32]{0:T(128)} %param.12), channel_id=1, source_target_pairs={{0,1},{1,0},{2,3},{3,2},{4,5},{5,4},{6,7},{7,6},{8,9},{9,8},{10,11... | collective-permute-start | bytes 392 | tf_op jit(solution)/shard_map/ppermute | solution.py:320
  7.6 0.7 %copy-start.3 = (s32[1024]{0:T(1024)S(1)}, s32[1024]{0:T(1024)}, u32[]{:S(2)}) copy-start(s32[1024]{0:T(1024)} %param.8) | copy-start | bytes 12292
  8.3 5.0 %copy-start = (bf16[1024,384]{1,0:T(8,128)(2,1)S(1)}, bf16[1024,384]{1,0:T(8,128)(2,1)}, u32[]{:S(2)}) copy-start(bf16[1024,384]{1,0:T(8,128)(2,1)} %density_ref.1) | copy-start | bytes 2359300
  8.3 5.0 %copy-start.1 = (s32[32]{0:T(128)S(1)}, s32[32]{0:T(128)}, u32[]{:S(2)}) copy-start(s32[32]{0:T(128)} %param.12) | copy-start | bytes 388
  13.7 12.0 %collective-permute-start.2 = (bf16[32,384]{1,0:T(8,128)(2,1)S(1)}, bf16[32,384]{1,0:T(8,128)(2,1)S(1)}, u32[]{:S(2)}, u32[]{:S(2)}) collective-permute-start(bf16[32,384]{1,0:T(8,128)(2,1)S(1)} %get-tuple-element.11), channel_id=1, source_target_pairs={{0,127},{1,2},{2,1},{3,4},{4,3},{5,6},{6,5},{7,8},{8,7},{9,10},{10... | collective-permute-start | bytes 73736 | tf_op jit(solution)/shard_map/ppermute | solution.py:324
  15.0 10.8 %collective-permute-start.3 = (bf16[32,384]{1,0:T(8,128)(2,1)S(1)}, bf16[32,384]{1,0:T(8,128)(2,1)S(1)}, u32[]{:S(2)}, u32[]{:S(2)}) collective-permute-start(bf16[32,384]{1,0:T(8,128)(2,1)S(1)} %get-tuple-element.12), channel_id=1, source_target_pairs={{0,1},{1,0},{2,3},{3,2},{4,5},{5,4},{6,7},{7,6},{8,9},{9,8},{10,11... | collective-permute-start | bytes 73736 | tf_op jit(solution)/shard_map/ppermute | solution.py:320
  16.0 9.7 %copy-start.4 = (s32[32]{0:T(128)S(1)}, s32[32]{0:T(128)}, u32[]{:S(2)}) copy-start(s32[32]{0:T(128)} %param.11) | copy-start | bytes 388
  16.1 34.4 %all-to-all-start = ((s32[128,25,1,128]{3,2,1,0:T(1,128)}), s32[128,25,1,128]{3,2,1,0:T(1,128)S(1)}, u32[]{:S(2)}, u32[]{:S(2)}) async-start(s32[128,25,1,128]{3,2,1,0:T(1,128)} %bitcast.16), calls=%async_computation | async-start | bytes 3276800 | tf_op jit(solution)/shard_map/all_to_all | solution.py:333
  25.8 3.7 %copy-start.2 = (bf16[32,384,384]{2,1,0:T(8,128)(2,1)S(1)}, bf16[32,384,384]{2,1,0:T(8,128)(2,1)}, u32[]{:S(2)}) copy-start(bf16[32,384,384]{2,1,0:T(8,128)(2,1)} %mats_ref.1) | copy-start | bytes 28311556
  33.5 20.1 %collective-permute-start.4 = (f32[40,384]{1,0:T(8,128)S(1)}, f32[40,384]{1,0:T(8,128)S(1)}, u32[]{:S(2)}, u32[]{:S(2)}) collective-permute-start(f32[40,384]{1,0:T(8,128)S(1)} %near_terms.1.own_ref), channel_id=1, source_target_pairs={{0,127},{1,2},{2,1},{3,4},{4,3},{5,6},{6,5},{7,8},{8,7},{9,10},{10... | collective-permute-start | bytes 184328 | tf_op jit(solution)/shard_map/ppermute | solution.py:324
  39.4 14.2 %collective-permute-start.5 = (f32[40,384]{1,0:T(8,128)S(1)}, f32[40,384]{1,0:T(8,128)S(1)}, u32[]{:S(2)}, u32[]{:S(2)}) collective-permute-start(f32[40,384]{1,0:T(8,128)S(1)} %near_terms.1.own_ref), channel_id=1, source_target_pairs={{0,1},{1,0},{2,3},{3,2},{4,5},{5,4},{6,7},{7,6},{8,9},{9,8},{10,11... | collective-permute-start | bytes 184328 | tf_op jit(solution)/shard_map/ppermute | solution.py:320
